TPU v7x, 256 devices: a whole 4x4x8 slice. The times are simulated.
256 devices in a mesh: group: 2 (over core), dp: 16 (over x, y), head: 8 (over z).
Axes of the slice: x: 4, y: 4, z: 8, core: 2. Of those that a mesh axis runs over, the one named last changes fastest.
Arguments:
- queries: bfloat16 [2, 512, 64, 576], P('group', 'dp', 'head'), may hold values from -400 to 400
- latent_cache: bfloat16 [2, 512, 192, 576], P('group', 'dp'), may hold values from -9 to 9
- lengths: int32 [2, 512], P('group', 'dp'), may hold values from 2 to 192, as said below
- w_value: bfloat16 [64, 512, 128], P('head'), may hold values from -0.25 to 0.25
- w_out: bfloat16 [8192, 7168], P('head', 'dp'), may hold values from -0.0625 to 0.0625
- residual: bfloat16 [2, 512, 7168], P('group', ('dp', 'head')), may hold values from -6 to 6
- norm_gain: float32 [7168], replicated, may hold values from 0.5 to 1.5
- routes: int32 [2, 512, 8], P('group', ('dp', 'head')), may hold values from 0 to 15, all different within a row; in each aligned block of 4 rows (0 to 3, 4 to 7, ..., all dimensions but the last counted through in order) at most 3 rows name the same one
- gate_weights: float32 [2, 512, 8], P('group', ('dp', 'head')), may hold values from 0.2 to 1
- w_gate: bfloat16 [16, 7168, 2048], P('dp', None, ('group', 'head')), may hold values from -0.0625 to 0.0625
- w_up: bfloat16 [16, 7168, 2048], P('dp', None, ('group', 'head')), may hold values from -0.0625 to 0.0625
- w_down: bfloat16 [16, 7168, 2048], P('dp', None, ('group', 'head')), may hold values from -0.125 to 0.125
Outputs:
- layer_out: bfloat16 [2, 512, 7168], P('group', ('dp', 'head'))
Inputs may be any that keep to these rules, and one draw needn't show every extreme that they name: `lengths`: some request has exactly 192 cached tokens. `routes`: the 8 experts of a token differ; among the 4 rows of one device (aligned blocks along the requests of both micro-batches in order) no expert is named by more than 3 rows, and that bound is reached.
All inputs are finite; a program needn't handle non-finite values.
Results may differ from a plain program's by a relative error of at most 0.029.
Values may be sent and summed in bfloat16 or wider, within the bound.
No kernel may reach another device: no remote copies, remote signals or barrier semaphores. Data moves between devices by JAX's collectives and lax.ppermute only.
A program may use at most 128 MiB of HBM per device.

v0:
```python
import functools

import jax
import jax.numpy as jnp
from jax import lax
from jax.experimental import pallas as pl
from jax.experimental.pallas import tpu as pltpu
from jax.sharding import PartitionSpec as P

EXPERTS = 16
CAP = 3


softmax_scale = 0.07216878364870323
norm_eps = 1e-06
bf16 = jnp.bfloat16
f32 = jnp.float32


VMEM = pl.BlockSpec(memory_space=pltpu.VMEM)
SMEM = pl.BlockSpec(memory_space=pltpu.SMEM)
LANES = 128


def norm_pack_kernel(hidden_ref, gain_ref, pack_ref, extra_ref, out_ref):
    parts, count, cols = hidden_ref.shape
    square = jnp.zeros((count, 1), f32)
    for p in range(parts):
        part = hidden_ref[p].astype(f32)
        square += jnp.sum(part * part, axis=1, keepdims=True)
    scale = lax.rsqrt(square / (parts * cols) + norm_eps)
    pack = pack_ref[...]
    for p in range(parts):
        normed = (hidden_ref[p].astype(f32) * scale * gain_ref[p : p + 1]).astype(bf16)
        rows = jnp.dot(pack, normed, preferred_element_type=f32).astype(bf16)
        out_ref[:, p * cols : (p + 1) * cols] = rows
    extra = jnp.dot(pack, extra_ref[...], preferred_element_type=f32).astype(bf16)
    out_ref[:, parts * cols :] = extra


def norm_pack(hidden, gain, pack, extra):
    parts, _, cols = hidden.shape
    return pl.pallas_call(
        norm_pack_kernel,
        out_shape=jax.ShapeDtypeStruct((pack.shape[0], parts * cols + LANES), bf16),
        in_specs=[VMEM] * 4,
        out_specs=VMEM,
        compiler_params=pltpu.CompilerParams(vmem_limit_bytes=32 << 20),
    )(hidden, gain, pack, extra)


def gate_up_kernel(count, *refs):
    blocks, (gate_ref, up_ref, out_ref) = refs[:count], refs[count:]
    width = gate_ref.shape[0]
    step = 1024
    gate = up = 0.0
    for k in range(0, width, step):
        rows = jnp.concatenate([b[:, k : k + step] for b in blocks], axis=0)
        gate += jnp.dot(rows, gate_ref[k : k + step], preferred_element_type=f32)
        up += jnp.dot(rows, up_ref[k : k + step], preferred_element_type=f32)
    out_ref[:, :LANES] = (gate / (1.0 + jnp.exp(-gate)) * up).astype(bf16)
    out_ref[:, LANES:] = jnp.concatenate([b[:, width:] for b in blocks], axis=0)


def gate_up(blocks, w_gate, w_up):
    rows = sum(b.shape[0] for b in blocks)
    return pl.pallas_call(
        functools.partial(gate_up_kernel, len(blocks)),
        out_shape=jax.ShapeDtypeStruct((rows, 2 * LANES), bf16),
        in_specs=[VMEM] * (len(blocks) + 2),
        out_specs=VMEM,
        compiler_params=pltpu.CompilerParams(vmem_limit_bytes=32 << 20),
    )(*blocks, w_gate, w_up)


def down_kernel(count, *refs):
    g_ref, refs = refs[0], refs[1:]
    actives, downs, (keep_ref, give_ref) = refs[:count], refs[count : 2 * count], refs[2 * count :]
    g = g_ref[0]
    step = 256
    for at, out_ref in ((g, keep_ref), (1 - g, give_ref)):
        weights = [
            jnp.concatenate([downs[k][at], downs[k + 1][at]], axis=1) for k in range(0, count, 2)
        ]
        for r in range(0, keep_ref.shape[0], step):
            total = 0.0
            for k in range(0, count, 2):
                left = jnp.concatenate(
                    [actives[k][r : r + step], actives[k + 1][r : r + step]], axis=1
                )
                total += lax.dot_general(
                    left, weights[k // 2], (((1,), (1,)), ((), ())), preferred_element_type=f32
                )
            out_ref[r : r + step] = total.astype(out_ref.dtype)


def down_sums(g, actives, downs):
    shape = (actives[0].shape[0], downs[0].shape[1])
    return pl.pallas_call(
        functools.partial(down_kernel, len(actives)),
        out_shape=(jax.ShapeDtypeStruct(shape, f32), jax.ShapeDtypeStruct(shape, bf16)),
        in_specs=[SMEM] + [VMEM] * (2 * len(actives)),
        out_specs=(VMEM, VMEM),
        compiler_params=pltpu.CompilerParams(vmem_limit_bytes=32 << 20),
    )(g.reshape(1), *actives, *downs)


def combine_kernel(keep_ref, got_ref, facts_ref, out_ref):
    facts = facts_ref[...].astype(f32)
    cols = keep_ref.shape[1]
    total = (keep_ref[...] + got_ref[...].astype(f32)) * (facts[:, :1] + facts[:, 1:2])
    out_ref[:, :cols] = total.astype(bf16)
    rest = out_ref.shape[1] - cols
    out_ref[:, cols:] = jnp.broadcast_to(facts[:, 2:3], (facts.shape[0], rest)).astype(bf16)


def combine(keep, got, facts):
    rows, cols = keep.shape
    return pl.pallas_call(
        combine_kernel,
        out_shape=jax.ShapeDtypeStruct((rows, cols + -cols % LANES), bf16),
        in_specs=[VMEM] * 3,
        out_specs=VMEM,
        compiler_params=pltpu.CompilerParams(vmem_limit_bytes=32 << 20),
    )(keep, got, facts)


def ring(block, beside):
    count, cores = lax.axis_size("head"), lax.axis_size("group")
    right = [(i, (i + 1) % count) for i in range(count)]
    left = [(i, (i - 1) % count) for i in range(count)]
    both = [
        (c * count + i, c * count + (i + 1 - 2 * c) % count)
        for c in range(cores)
        for i in range(count)
    ]
    steps, results = [(block,)], []
    for step in range(count // 2):
        held = steps[-1]
        if step < count // 2 - 1:
            got = (lax.ppermute(held[0], "head", right), lax.ppermute(held[-1], "head", left))
        else:
            one = jnp.where(lax.axis_index("group") == 0, held[0], held[-1])
            got = (lax.ppermute(one, ("group", "head"), both),)
        if beside is not None:
            result = beside(held)
            got, result = lax.optimization_barrier((got, result))
            results.append(result)
        steps.append(got)
    if beside is not None:
        results.append(beside(steps[-1]))
    return steps, results


def local(
    queries,
    latent_cache,
    lengths,
    w_value,
    w_out,
    residual,
    norm_gain,
    routes,
    gate_weights,
    w_gate,
    w_up,
    w_down,
):
    reqs = queries.shape[1]
    heads = queries.shape[2]
    latent_width = w_value.shape[1]
    value_width = w_value.shape[2]
    span = latent_cache.shape[2]
    rows = residual.shape[1]
    width = residual.shape[2]
    n_group = lax.axis_size("group")
    n_dp = lax.axis_size("dp")
    n_head = lax.axis_size("head")
    n_col = n_group * n_head
    cols = width // n_dp
    piece = width // n_col
    g = lax.axis_index("group")
    dp = lax.axis_index("dp")
    z = lax.axis_index("head")

    slabs = w_down[0].reshape(n_group, n_head, piece, w_down.shape[2])
    slabs = [
        lax.dynamic_index_in_dim(slabs, lax.rem(z + k, n_head), 1, False) for k in range(n_head)
    ]
    shifts = [slabs[0]] + [None] * (n_head - 1)

    def shift(some):
        for k in some:
            shifts[k] = lax.ppermute(
                slabs[k], "head", [(i, (i + k) % n_head) for i in range(n_head)]
            )

    expert_ids = jnp.arange(EXPERTS, dtype=jnp.int32)
    chosen = routes[0][:, :, None] == expert_ids[None, None, :]
    table = jnp.max(jnp.where(chosen, gate_weights[0][:, :, None], -1.0), axis=1)
    table_high = table.astype(bf16)
    table_low = (table - table_high.astype(f32)).astype(bf16)

    cached = latent_cache[0]
    scores = (
        jnp.einsum("rhc,rlc->rhl", queries[0], cached, preferred_element_type=f32) * softmax_scale
    )
    visible = lax.broadcasted_iota(jnp.int32, (reqs, 1, span), 2) < lengths[0][:, None, None]
    scores = jnp.where(visible, scores, -jnp.inf)
    row_max = jnp.max(scores, axis=2, keepdims=True)
    weights = jnp.exp(scores - row_max)
    shares = (weights / jnp.sum(weights, axis=2, keepdims=True)).astype(bf16)
    latent = jnp.einsum(
        "rhl,rlc->rhc", shares, cached[:, :, :latent_width], preferred_element_type=f32
    ).astype(bf16)
    head_rows = jnp.einsum("rhc,hcv->hrv", latent, w_value, preferred_element_type=f32).astype(bf16)

    res = residual[0].reshape(rows, n_dp, cols).transpose(1, 0, 2).reshape(n_dp, -1, value_width)
    res_rows = res.shape[1]
    facts = jnp.stack([table_high.T, table_low.T], axis=1)
    facts = jnp.pad(facts, ((0, 0), (0, -res_rows % 16 - 2), (0, value_width - rows)))
    send = jnp.concatenate(
        [
            jnp.broadcast_to(
                head_rows.reshape(1, heads * reqs, value_width),
                (n_dp, heads * reqs, value_width),
            ),
            res,
            facts,
        ],
        axis=1,
    )
    got = lax.all_to_all(send, "dp", split_axis=0, concat_axis=0, tiled=True)
    shift((3, 5, 1, 7))
    early = lax.optimization_barrier((got, shifts[3], shifts[5], shifts[1], shifts[7]))
    got, shifts[3], shifts[5], shifts[1], shifts[7] = early
    res_piece = got[:, heads * reqs : heads * reqs + res_rows].reshape(n_dp * rows, cols)
    fact = got[:, heads * reqs + res_rows :, :rows]
    mine = fact[:, 0].reshape(1, n_dp * rows) > 0
    values = got[:, : heads * reqs].reshape(n_dp, heads, n_head, rows, value_width)
    partial = jnp.einsum(
        "dhziv,hvc->zdic",
        values,
        w_out.reshape(heads, value_width, cols),
        preferred_element_type=f32,
    ).astype(bf16)
    partial = lax.all_to_all(
        partial.reshape(n_head, n_dp * rows, cols), "head", split_axis=0, concat_axis=0, tiled=True
    )
    held = lax.optimization_barrier((partial, slabs[4], slabs[2], slabs[6]))
    partial, slabs[4], slabs[2], slabs[6] = held
    attended = jnp.sum(partial.astype(f32), axis=0).astype(bf16)
    hidden_piece = (res_piece.astype(f32) + attended.astype(f32)).astype(bf16)

    hidden = lax.all_to_all(
        jnp.broadcast_to(hidden_piece[None], (n_dp,) + hidden_piece.shape),
        "dp",
        split_axis=0,
        concat_axis=0,
        tiled=True,
    )
    shift((4, 2, 6))
    late = lax.optimization_barrier((hidden, shifts[4], shifts[2], shifts[6]))
    hidden, shifts[4], shifts[2], shifts[6] = late
    home = lax.dynamic_slice(hidden, (0, dp * rows, 0), (n_dp, rows, cols))

    def index(shape, axis):
        return lax.broadcasted_iota(jnp.int32, shape, axis)

    def before(count):
        a, b = index((count, count), 0), index((count, count), 1)
        return ((a // rows == b // rows) & (a < b)).astype(bf16)

    count = n_dp * rows
    slot = jnp.dot(mine.astype(bf16), before(count), preferred_element_type=f32)
    at, of = index((n_dp * CAP, count), 0), index((n_dp * CAP, count), 1)
    pack = (at // CAP == of // rows) & mine & (slot == (at % CAP).astype(f32))
    extra = jnp.concatenate(
        [
            fact[:, :2].transpose(0, 2, 1).reshape(count, 2),
            (index((count, 1), 0) % rows).astype(bf16),
            jnp.zeros((count, LANES - 3), bf16),
        ],
        axis=1,
    )
    packed = norm_pack(hidden, norm_gain.reshape(n_dp, cols), pack.astype(bf16), extra)

    def swap(block):
        return lax.ppermute(block, "group", [(0, 1), (1, 0)])

    fill = n_dp * CAP
    def work(blocks):
        return gate_up(blocks + tuple(swap(b) for b in blocks), w_gate[0], w_up[0])

    _, done = ring(packed, work)
    active = jnp.concatenate(done, axis=0)

    r = index((1, n_col * fill), 1)
    first, final = 2 * fill, (n_col - 2) * fill
    at = jnp.where(r < first, 0, (r - first) // (4 * fill) + 1)
    within = jnp.where(r < first, r, (r - first) % (4 * fill))
    other = jnp.where((r < first) | (r >= final), within // fill, within // (2 * fill))
    leftward = jnp.where((r < first) | (r >= final), 0, within // fill % 2)
    from_z = jnp.where(leftward == 1, z + at, z - at + n_head) % n_head
    from_g = jnp.where(other == 1, 1 - g, g)
    home_dp, place = r % fill // CAP, r % CAP
    to = home_dp * (n_col * CAP) + (from_g * n_head + from_z) * CAP + place
    order = (index((n_col * fill, n_col * fill), 0) == to).astype(bf16)
    active = jnp.dot(order, active, preferred_element_type=f32).astype(bf16)
    row_facts = active[:, LANES:]
    active = active[:, :LANES]

    steps, _ = ring(active, None)
    actives = [s[0] for s in steps] + [s[1] for s in steps[-2:0:-1]]
    keep, give = down_sums(g, actives, shifts)
    out = combine(keep, swap(give), row_facts).reshape(n_dp, n_col * CAP, -1)
    back = lax.all_to_all(out, "dp", split_axis=0, concat_axis=0, tiled=True)

    back = back.reshape(EXPERTS * n_col * CAP, -1)
    token = index((back.shape[0], 1), 0) // CAP % n_col * rows
    token = token.astype(f32) + back[:, piece : piece + 1].astype(f32)
    hit = token == index((back.shape[0], n_col * rows), 1).astype(f32)
    mixed = lax.dot_general(
        hit.astype(bf16),
        back[:, :piece],
        (((0,), (0,)), ((), ())),
        preferred_element_type=f32,
    )
    mixed = lax.all_to_all(
        mixed.astype(bf16).reshape(n_col, rows, piece),
        ("group", "head"),
        split_axis=0,
        concat_axis=0,
        tiled=True,
    )
    layer_out = (home.astype(f32) + mixed.astype(f32)).astype(bf16)
    layer_out = layer_out.transpose(1, 0, 2).reshape(rows, width)
    return layer_out[None]


def solution(mesh):
    in_specs = (
        P("group", "dp", "head", None),
        P("group", "dp", None, None),
        P("group", "dp"),
        P("head", None, None),
        P("head", "dp"),
        P("group", ("dp", "head"), None),
        P(),
        P("group", ("dp", "head"), None),
        P("group", ("dp", "head"), None),
        P("dp", None, ("group", "head")),
        P("dp", None, ("group", "head")),
        P("dp", None, ("group", "head")),
    )
    out_specs = P("group", ("dp", "head"), None)
    return jax.shard_map(local, mesh=mesh, in_specs=in_specs, out_specs=out_specs, check_vma=False)
```

profile of v0, /device:TPU:1, one launch (start us, length us, event | category | flops | bytes accessed | tf_op | source)
XLA Modules:
  0.0 279.1 jit_solution(2331421255409741953)
XLA Ops:
  1.7 0.9 reshape_squeeze.7
  2.9 6.1 %fusion.87 = (f32[32,8]{1,0:T(8,128)S(1)}, f32[32,8,192]{2,1,0:T(8,128)S(1)}) fusion(bf16[1,32,8,576]{3,2,1,0:T(8,128)(2,1)} %param.12, pred[32,192]{1,0:T(8,128)(4,1)S(1)} %iota_compare_fusion.6, bf16[1,32,192,576]{3,2,1,0:T(8,128)(2,1)} %param.13), kind=kOutput, calls=%fused_computation.169 | convolution fusion | flops 56819904 | bytes 7576576 | tf_op jit(solution)/shard_map/sub | solution.py:211
  8.9 3.7 %fusion.8 = bf16[32,8,512]{2,1,0:T(8,128)(2,1)S(1)} fusion(bf16[32,192,576]{2,1,0:T(8,128)(2,1)} %bitcast.105, f32[32,8,192]{2,1,0:T(8,128)S(1)} %get-tuple-element.68, f32[32,8]{1,0:T(8,128)S(1)} %get-tuple-element.67), kind=kOutput, calls=%fused_computation.11 | convolution fusion | flops 50561024 | bytes 6751232 | tf_op jit(solution)/shard_map/rhl,rlc->rhc/dot_general | solution.py:213
  13.2 1.1 fusion.14
  14.4 7.6 %all-to-all-start = ((bf16[16,272,128]{2,1,0:T(8,128)(2,1)}), bf16[16,272,128]{2,1,0:T(8,128)(2,1)S(1)}, u32[]{:S(2)}, u32[]{:S(2)}) async-start(bf16[16,272,128]{2,1,0:T(8,128)(2,1)} %fusion.14), calls=%async_computation | async-start | bytes 2228224 | tf_op jit(solution)/shard_map/all_to_all | solution.py:233
  22.0 2.6 dynamic-slice_bitcast_fusion
  24.6 4.3 %collective-permute-start = (bf16[2,448,128]{2,1,0:T(8,128)(2,1)S(1)}, bf16[2,448,128]{2,1,0:T(8,128)(2,1)S(1)}, u32[]{:S(2)}, u32[]{:S(2)}) collective-permute-start(bf16[2,448,128]{2,1,0:T(8,128)(2,1)S(1)} %get-tuple-element.64), channel_id=1, source_target_pairs={{0,3},{1,4},{2,5},{3,6},{4,7},{5,0},{6,1},{7,2},{8,11},{9,12},{10,... | collective-permute-start | bytes 688136 | tf_op jit(solution)/shard_map/ppermute | solution.py:194
  29.0 2.1 collective-permute-start.1
  31.9 1.9 collective-permute-start.3
  33.8 1.2 copy.113
  35.0 6.2 %collective-permute-done.refs_12_ = bf16[2,448,128]{2,1,0:T(8,128)(2,1)S(1)} collective-permute-done((bf16[2,448,128]{2,1,0:T(8,128)(2,1)S(1)}, bf16[2,448,128]{2,1,0:T(8,128)(2,1)S(1)}, u32[]{:S(2)}, u32[]{:S(2)}) %collective-permute-start) | collective-permute-done | bytes 229408 | tf_op jit(solution)/shard_map/ppermute | solution.py:194
  42.6 8.1 %collective-permute-done.2.refs_10_ = bf16[2,448,128]{2,1,0:T(8,128)(2,1)S(1)} collective-permute-done((bf16[2,448,128]{2,1,0:T(8,128)(2,1)S(1)}, bf16[2,448,128]{2,1,0:T(8,128)(2,1)S(1)}, u32[]{:S(2)}, u32[]{:S(2)}) %collective-permute-start.2) | collective-permute-done | bytes 229408 | tf_op jit(solution)/shard_map/ppermute | solution.py:194
  54.2 0.9 copy.88
  55.2 5.8 %all-to-all-start.1 = ((bf16[8,64,448]{2,1,0:T(8,128)(2,1)}), bf16[8,64,448]{2,1,0:T(8,128)(2,1)S(1)}, u32[]{:S(2)}, u32[]{:S(2)}) async-start(bf16[8,64,448]{2,1,0:T(8,128)(2,1)} %copy.88), calls=%async_computation.1 | async-start | bytes 1048576 | tf_op jit(solution)/shard_map/all_to_all | solution.py:247
  61.3 16.2 %all-to-all-done.1 = bf16[8,64,448]{2,1,0:T(8,128)(2,1)S(1)} async-done(((bf16[8,64,448]{2,1,0:T(8,128)(2,1)}), bf16[8,64,448]{2,1,0:T(8,128)(2,1)S(1)}, u32[]{:S(2)}, u32[]{:S(2)}) %all-to-all-start.1) | async-done | bytes 458784 | tf_op jit(solution)/shard_map/all_to_all | solution.py:247
  77.6 1.1 broadcast_in_dim.63
  78.7 6.0 %all-to-all-start.2 = ((bf16[16,64,448]{2,1,0:T(8,128)(2,1)}), bf16[16,64,448]{2,1,0:T(8,128)(2,1)}, u32[]{:S(2)}, u32[]{:S(2)}) async-start(bf16[16,64,448]{2,1,0:T(8,128)(2,1)} %broadcast_in_dim.63), calls=%async_computation.2 | async-start | bytes 2097152 | tf_op jit(solution)/shard_map/all_to_all | solution.py:255
  86.7 3.1 %collective-permute-start.5 = (bf16[2,448,128]{2,1,0:T(8,128)(2,1)}, bf16[2,448,128]{2,1,0:T(8,128)(2,1)S(1)}, u32[]{:S(2)}, u32[]{:S(2)}) collective-permute-start(bf16[2,448,128]{2,1,0:T(8,128)(2,1)} %get-tuple-element.34), channel_id=1, source_target_pairs={{0,2},{1,3},{2,4},{3,5},{4,6},{5,7},{6,0},{7,1},{8,10},{9,11},{10,... | collective-permute-start | bytes 688136 | tf_op jit(solution)/shard_map/ppermute | solution.py:194
  90.8 9.6 %collective-permute-done.4.refs_13_ = bf16[2,448,128]{2,1,0:T(8,128)(2,1)S(1)} collective-permute-done((bf16[2,448,128]{2,1,0:T(8,128)(2,1)}, bf16[2,448,128]{2,1,0:T(8,128)(2,1)S(1)}, u32[]{:S(2)}, u32[]{:S(2)}) %collective-permute-start.4) | collective-permute-done | bytes 229408 | tf_op jit(solution)/shard_map/ppermute | solution.py:194
  100.4 8.8 %collective-permute-done.5.refs_11_ = bf16[2,448,128]{2,1,0:T(8,128)(2,1)S(1)} collective-permute-done((bf16[2,448,128]{2,1,0:T(8,128)(2,1)}, bf16[2,448,128]{2,1,0:T(8,128)(2,1)S(1)}, u32[]{:S(2)}, u32[]{:S(2)}) %collective-permute-start.5) | collective-permute-done | bytes 229408 | tf_op jit(solution)/shard_map/ppermute | solution.py:194
  109.2 2.0 shard_map.118.refs_0_
  111.3 2.2 collective-permute-start.9
  113.5 2.7 collective-permute-start.8
  116.2 1.5 copy-done.2
  117.7 0.9 shard_map.119
  118.6 13.3 %collective-permute-done.7.refs_0_ = bf16[48,7296]{1,0:T(8,128)(2,1)S(1)} collective-permute-done((bf16[48,7296]{1,0:T(8,128)(2,1)S(1)}, bf16[48,7296]{1,0:T(8,128)(2,1)S(1)}, u32[]{:S(2)}, u32[]{:S(2)}) %collective-permute-start.7) | collective-permute-done | bytes 700448 | tf_op jit(solution)/shard_map/ppermute | solution.py:141
  132.8 2.7 collective-permute-start.11
  135.6 1.6 shard_map.120
  137.3 13.7 %collective-permute-done.10.refs_0_ = bf16[48,7296]{1,0:T(8,128)(2,1)} collective-permute-done((bf16[48,7296]{1,0:T(8,128)(2,1)S(1)}, bf16[48,7296]{1,0:T(8,128)(2,1)}, u32[]{:S(2)}, u32[]{:S(2)}) %collective-permute-start.10) | collective-permute-done | bytes 700448 | tf_op jit(solution)/shard_map/ppermute | solution.py:141
  150.9 1.4 collective-permute-start.16
  152.3 2.7 collective-permute-start.15
  155.4 1.5 copy-done.3
  156.9 3.3 %shard_map.121 = bf16[192,256]{1,0:T(8,128)(2,1)S(1)} custom-call(bf16[48,7296]{1,0:T(8,128)(2,1)} %collective-permute-done.10.refs_0_, bf16[48,7296]{1,0:T(8,128)(2,1)} %collective-permute-done.11.refs_1_, bf16[48,7296]{1,0:T(8,128)(2,1)} %collective-permute-done.16.refs_2_, bf16[48,7296]{1,0:T(8,128)(2,1)} %collective-permute-done.17.refs_3_, ...), custom_call_target="tpu_custom_call" | custom-call | tf_op jit(solution)/shard_map/pallas_call | solution.py:67
  160.2 10.3 %collective-permute-done.14.refs_0_ = bf16[48,7296]{1,0:T(8,128)(2,1)} collective-permute-done((bf16[48,7296]{1,0:T(8,128)(2,1)}, bf16[48,7296]{1,0:T(8,128)(2,1)}, u32[]{:S(2)}, u32[]{:S(2)}) %collective-permute-start.14) | collective-permute-done | bytes 700448 | tf_op jit(solution)/shard_map/ppermute | solution.py:141
  170.6 1.4 collective-permute-start.19
  171.9 9.7 %collective-permute-start.20 = (bf16[48,7296]{1,0:T(8,128)(2,1)}, bf16[48,7296]{1,0:T(8,128)(2,1)S(1)}, u32[]{:S(2)}, u32[]{:S(2)}) collective-permute-start(bf16[48,7296]{1,0:T(8,128)(2,1)} %collective-permute-done.15.refs_1_), channel_id=1, source_target_pairs={{0,128},{128,0},{1,129},{129,1},{2,130},{130,2},{3,131},{131,3},{4... | collective-permute-start | bytes 2101256 | tf_op jit(solution)/shard_map/ppermute | solution.py:289
  181.6 1.2 broadcast_select_fusion
  182.8 2.7 collective-permute-start.18
  185.6 2.9 %shard_map.122 = bf16[192,256]{1,0:T(8,128)(2,1)S(1)} custom-call(bf16[48,7296]{1,0:T(8,128)(2,1)} %collective-permute-done.14.refs_0_, bf16[48,7296]{1,0:T(8,128)(2,1)} %collective-permute-done.15.refs_1_, bf16[48,7296]{1,0:T(8,128)(2,1)S(1)} %collective-permute-done.19.refs_2_, bf16[48,7296]{1,0:T(8,128)(2,1)S(1)} %collective-permute-done.20.refs_3_, ...), custom_call_target="tpu_custom_call" | custom-call | tf_op jit(solution)/shard_map/pallas_call | solution.py:67
  188.5 5.1 %collective-permute-done.18.refs_0_ = bf16[48,7296]{1,0:T(8,128)(2,1)} collective-permute-done((bf16[48,7296]{1,0:T(8,128)(2,1)S(1)}, bf16[48,7296]{1,0:T(8,128)(2,1)}, u32[]{:S(2)}, u32[]{:S(2)}) %collective-permute-start.18) | collective-permute-done | bytes 700448 | tf_op jit(solution)/shard_map/ppermute | solution.py:144
  193.6 2.2 collective-permute-start.21
  195.9 2.0 collective-permute-done.21.refs_1_
  197.9 1.5 copy-done.4
  199.4 2.2 shard_map.123
  202.9 2.7 collective-permute-start.25
  205.6 4.6 %collective-permute-done.22.refs_2_ = bf16[768,128]{1,0:T(8,128)(2,1)S(1)} collective-permute-done((bf16[768,128]{1,0:T(8,128)(2,1)S(1)}, bf16[768,128]{1,0:T(8,128)(2,1)S(1)}, u32[]{:S(2)}, u32[]{:S(2)}) %collective-permute-start.22) | collective-permute-done | bytes 196640 | tf_op jit(solution)/shard_map/ppermute | solution.py:141
  210.2 2.7 collective-permute-start.26
  212.9 3.7 %collective-permute-done.23.refs_3_ = bf16[768,128]{1,0:T(8,128)(2,1)S(1)} collective-permute-done((bf16[768,128]{1,0:T(8,128)(2,1)S(1)}, bf16[768,128]{1,0:T(8,128)(2,1)S(1)}, u32[]{:S(2)}, u32[]{:S(2)}) %collective-permute-start.23) | collective-permute-done | bytes 196640 | tf_op jit(solution)/shard_map/ppermute | solution.py:141
  216.6 2.7 collective-permute-start.27
  219.3 3.0 %collective-permute-done.24.refs_4_ = bf16[768,128]{1,0:T(8,128)(2,1)S(1)} collective-permute-done((bf16[768,128]{1,0:T(8,128)(2,1)S(1)}, bf16[768,128]{1,0:T(8,128)(2,1)S(1)}, u32[]{:S(2)}, u32[]{:S(2)}) %collective-permute-start.24) | collective-permute-done | bytes 196640 | tf_op jit(solution)/shard_map/ppermute | solution.py:141
  222.4 2.8 collective-permute-start.28
  225.1 2.6 collective-permute-done.28.refs_5_
  227.8 2.8 shard_map.124
  230.6 1.1 copy.95
  231.7 4.9 %collective-permute-start.29 = (bf16[768,448]{0,1:T(8,128)(2,1)}, bf16[768,448]{0,1:T(8,128)(2,1)}, u32[]{:S(2)}, u32[]{:S(2)}) collective-permute-start(bf16[768,448]{0,1:T(8,128)(2,1)} %copy.95), channel_id=1, source_target_pairs={{0,128},{128,0},{1,129},{129,1},{2,130},{130,2},{3,131},{131,3},{4... | collective-permute-start | bytes 2064392 | tf_op jit(solution)/shard_map/ppermute | solution.py:289
  236.5 2.1 collective-permute-done.29
  238.7 1.4 copy.96.got_ref
  240.0 0.9 copy-done.6
  241.0 1.2 shard_map.125
  242.2 6.6 %all-to-all-start.3 = ((bf16[16,48,512]{2,1,0:T(8,128)(2,1)}), bf16[16,48,512]{2,1,0:T(8,128)(2,1)S(1)}, u32[]{:S(2)}, u32[]{:S(2)}) async-start(bf16[16,48,512]{2,1,0:T(8,128)(2,1)} %bitcast.31), calls=%async_computation.3 | async-start | bytes 1572864 | tf_op jit(solution)/shard_map/all_to_all | solution.py:317
  248.8 12.7 %all-to-all-done.3 = bf16[16,48,512]{2,1,0:T(8,128)(2,1)S(1)} async-done(((bf16[16,48,512]{2,1,0:T(8,128)(2,1)}), bf16[16,48,512]{2,1,0:T(8,128)(2,1)S(1)}, u32[]{:S(2)}, u32[]{:S(2)}) %all-to-all-start.3) | async-done | bytes 786464 | tf_op jit(solution)/shard_map/all_to_all | solution.py:317
  263.0 7.1 %all-to-all-start.4 = ((bf16[16,4,448]{2,1,0:T(4,128)(2,1)}), bf16[16,4,448]{2,1,0:T(4,128)(2,1)S(1)}, u32[]{:S(2)}, u32[]{:S(2)}) async-start(bf16[16,4,448]{2,1,0:T(4,128)(2,1)} %reshape.401), calls=%async_computation.4 | async-start | bytes 131072 | tf_op jit(solution)/shard_map/all_to_all | solution.py:329
  270.0 7.2 %all-to-all-done.4 = bf16[16,4,448]{2,1,0:T(4,128)(2,1)S(1)} async-done(((bf16[16,4,448]{2,1,0:T(4,128)(2,1)}), bf16[16,4,448]{2,1,0:T(4,128)(2,1)S(1)}, u32[]{:S(2)}, u32[]{:S(2)}) %all-to-all-start.4) | async-done | bytes 57376 | tf_op jit(solution)/shard_map/all_to_all | solution.py:329
  277.2 1.0 fusion.32
  (121 shorter events, 16.6 us)
Async XLA Ops:
  0.0 12.7 %copy-start = (bf16[8,512,128]{2,1,0:T(8,128)(2,1)S(1)}, bf16[8,512,128]{2,1,0:T(8,128)(2,1)}, u32[]{:S(2)}) copy-start(bf16[8,512,128]{2,1,0:T(8,128)(2,1)} %param.15) | copy-start | bytes 3145732
  14.4 38.6 %all-to-all-start = ((bf16[16,272,128]{2,1,0:T(8,128)(2,1)}), bf16[16,272,128]{2,1,0:T(8,128)(2,1)S(1)}, u32[]{:S(2)}, u32[]{:S(2)}) async-start(bf16[16,272,128]{2,1,0:T(8,128)(2,1)} %fusion.14), calls=%async_computation | async-start | bytes 2228224 | tf_op jit(solution)/shard_map/all_to_all | solution.py:233
  21.9 11.9 %copy-start.20 = (bf16[1024,448]{0,1:T(8,128)(2,1)S(1)}, bf16[1024,448]{0,1:T(8,128)(2,1)}, u32[]{:S(2)}) copy-start(bf16[1024,448]{0,1:T(8,128)(2,1)} %param.16) | copy-start | bytes 2752516
  24.6 16.6 %collective-permute-start = (bf16[2,448,128]{2,1,0:T(8,128)(2,1)S(1)}, bf16[2,448,128]{2,1,0:T(8,128)(2,1)S(1)}, u32[]{:S(2)}, u32[]{:S(2)}) collective-permute-start(bf16[2,448,128]{2,1,0:T(8,128)(2,1)S(1)} %get-tuple-element.64), channel_id=1, source_target_pairs={{0,3},{1,4},{2,5},{3,6},{4,7},{5,0},{6,1},{7,2},{8,11},{9,12},{10,... | collective-permute-start | bytes 688136 | tf_op jit(solution)/shard_map/ppermute | solution.py:194
  29.0 12.9 %collective-permute-start.1 = (bf16[2,448,128]{2,1,0:T(8,128)(2,1)S(1)}, bf16[2,448,128]{2,1,0:T(8,128)(2,1)S(1)}, u32[]{:S(2)}, u32[]{:S(2)}) collective-permute-start(bf16[2,448,128]{2,1,0:T(8,128)(2,1)S(1)} %get-tuple-element.63), channel_id=1, source_target_pairs={{0,5},{1,6},{2,7},{3,0},{4,1},{5,2},{6,3},{7,4},{8,13},{9,14},{10,... | collective-permute-start | bytes 688136 | tf_op jit(solution)/shard_map/ppermute | solution.py:194
  31.1 19.5 %collective-permute-start.2 = (bf16[2,448,128]{2,1,0:T(8,128)(2,1)S(1)}, bf16[2,448,128]{2,1,0:T(8,128)(2,1)S(1)}, u32[]{:S(2)}, u32[]{:S(2)}) collective-permute-start(bf16[2,448,128]{2,1,0:T(8,128)(2,1)S(1)} %get-tuple-element.62), channel_id=1, source_target_pairs={{0,1},{1,2},{2,3},{3,4},{4,5},{5,6},{6,7},{7,0},{8,9},{9,10},{10,1... | collective-permute-start | bytes 688136 | tf_op jit(solution)/shard_map/ppermute | solution.py:194
  31.9 20.4 %collective-permute-start.3 = (bf16[2,448,128]{2,1,0:T(8,128)(2,1)S(1)}, bf16[2,448,128]{2,1,0:T(8,128)(2,1)S(1)}, u32[]{:S(2)}, u32[]{:S(2)}) collective-permute-start(bf16[2,448,128]{2,1,0:T(8,128)(2,1)S(1)} %get-tuple-element.61), channel_id=1, source_target_pairs={{0,7},{1,0},{2,1},{3,2},{4,3},{5,4},{6,5},{7,6},{8,15},{9,8},{10,9... | collective-permute-start | bytes 688136 | tf_op jit(solution)/shard_map/ppermute | solution.py:194
  35.0 18.4 %copy-start.21 = (bf16[56,8,8,128]{3,2,1,0:T(8,128)(2,1)S(1)}, bf16[56,8,8,128]{3,2,1,0:T(8,128)(2,1)}, u32[]{:S(2)}) copy-start(bf16[56,8,8,128]{3,2,1,0:T(8,128)(2,1)} %copy.113) | copy-start | bytes 2752516
  41.2 0.7 copy-start.7
  41.9 0.7 copy-start.9
  50.7 0.7 copy-start.11
  52.2 0.7 copy-start.13
  52.9 8.2 %copy-start.19 = (bf16[16,272,128]{2,1,0:T(8,128)(2,1)}, bf16[16,272,128]{2,1,0:T(8,128)(2,1)S(1)}, u32[]{:S(2)}) copy-start(bf16[16,272,128]{2,1,0:T(8,128)(2,1)S(1)} %all-to-all-done) | copy-start | bytes 3342340
  53.4 7.5 %copy-start.22 = (f32[7168]{0:T(1024)S(1)}, f32[7168]{0:T(1024)}, u32[]{:S(2)}) copy-start(f32[7168]{0:T(1024)} %param.18) | copy-start | bytes 86020
  55.2 22.3 %all-to-all-start.1 = ((bf16[8,64,448]{2,1,0:T(8,128)(2,1)}), bf16[8,64,448]{2,1,0:T(8,128)(2,1)S(1)}, u32[]{:S(2)}, u32[]{:S(2)}) async-start(bf16[8,64,448]{2,1,0:T(8,128)(2,1)} %copy.88), calls=%async_computation.1 | async-start | bytes 1048576 | tf_op jit(solution)/shard_map/all_to_all | solution.py:247
  78.7 37.5 %copy-start.1 = (bf16[1,7168,128]{2,1,0:T(8,128)(2,1)S(1)}, bf16[1,7168,128]{2,1,0:T(8,128)(2,1)}, u32[]{:S(2)}) copy-start(bf16[1,7168,128]{2,1,0:T(8,128)(2,1)} %param.21) | copy-start | bytes 5505028
  78.7 30.5 %all-to-all-start.2 = ((bf16[16,64,448]{2,1,0:T(8,128)(2,1)}), bf16[16,64,448]{2,1,0:T(8,128)(2,1)}, u32[]{:S(2)}, u32[]{:S(2)}) async-start(bf16[16,64,448]{2,1,0:T(8,128)(2,1)} %broadcast_in_dim.63), calls=%async_computation.2 | async-start | bytes 2097152 | tf_op jit(solution)/shard_map/all_to_all | solution.py:255
  86.6 13.8 %collective-permute-start.4 = (bf16[2,448,128]{2,1,0:T(8,128)(2,1)}, bf16[2,448,128]{2,1,0:T(8,128)(2,1)S(1)}, u32[]{:S(2)}, u32[]{:S(2)}) collective-permute-start(bf16[2,448,128]{2,1,0:T(8,128)(2,1)} %get-tuple-element.33), channel_id=1, source_target_pairs={{0,4},{1,5},{2,6},{3,7},{4,0},{5,1},{6,2},{7,3},{8,12},{9,13},{10,... | collective-permute-start | bytes 688136 | tf_op jit(solution)/shard_map/ppermute | solution.py:194
  86.7 22.5 %collective-permute-start.5 = (bf16[2,448,128]{2,1,0:T(8,128)(2,1)}, bf16[2,448,128]{2,1,0:T(8,128)(2,1)S(1)}, u32[]{:S(2)}, u32[]{:S(2)}) collective-permute-start(bf16[2,448,128]{2,1,0:T(8,128)(2,1)} %get-tuple-element.34), channel_id=1, source_target_pairs={{0,2},{1,3},{2,4},{3,5},{4,6},{5,7},{6,0},{7,1},{8,10},{9,11},{10,... | collective-permute-start | bytes 688136 | tf_op jit(solution)/shard_map/ppermute | solution.py:194
  89.8 19.4 %collective-permute-start.6 = (bf16[2,448,128]{2,1,0:T(8,128)(2,1)}, bf16[2,448,128]{2,1,0:T(8,128)(2,1)}, u32[]{:S(2)}, u32[]{:S(2)}) collective-permute-start(bf16[2,448,128]{2,1,0:T(8,128)(2,1)} %get-tuple-element.35), channel_id=1, source_target_pairs={{0,6},{1,7},{2,0},{3,1},{4,2},{5,3},{6,4},{7,5},{8,14},{9,15},{10,... | collective-permute-start | bytes 688136 | tf_op jit(solution)/shard_map/ppermute | solution.py:194
  100.4 18.2 %copy-start.15 = (bf16[2,448,128]{2,1,0:T(8,128)(2,1)}, bf16[2,448,128]{2,1,0:T(8,128)(2,1)S(1)}, u32[]{:S(2)}) copy-start(bf16[2,448,128]{2,1,0:T(8,128)(2,1)S(1)} %collective-permute-done.4.refs_13_) | copy-start | bytes 688132
  109.2 9.4 %copy-start.17 = (bf16[2,448,128]{2,1,0:T(8,128)(2,1)}, bf16[2,448,128]{2,1,0:T(8,128)(2,1)S(1)}, u32[]{:S(2)}) copy-start(bf16[2,448,128]{2,1,0:T(8,128)(2,1)S(1)} %collective-permute-done.5.refs_11_) | copy-start | bytes 688132
  111.3 4.9 %collective-permute-start.9 = (bf16[48,7296]{1,0:T(8,128)(2,1)S(1)}, bf16[48,7296]{1,0:T(8,128)(2,1)S(1)}, u32[]{:S(2)}, u32[]{:S(2)}) collective-permute-start(bf16[48,7296]{1,0:T(8,128)(2,1)S(1)} %shard_map.118.refs_0_), channel_id=1, source_target_pairs={{0,128},{128,0},{1,129},{129,1},{2,130},{130,2},{3,131},{131,3},{4... | collective-permute-start | bytes 2101256 | tf_op jit(solution)/shard_map/ppermute | solution.py:289
  113.5 18.5 %collective-permute-start.7 = (bf16[48,7296]{1,0:T(8,128)(2,1)S(1)}, bf16[48,7296]{1,0:T(8,128)(2,1)S(1)}, u32[]{:S(2)}, u32[]{:S(2)}) collective-permute-start(bf16[48,7296]{1,0:T(8,128)(2,1)S(1)} %shard_map.118.refs_0_), channel_id=1, source_target_pairs={{0,1},{1,2},{2,3},{3,4},{4,5},{5,6},{6,7},{7,0},{8,9},{9,10},{10,1... | collective-permute-start | bytes 2101256 | tf_op jit(solution)/shard_map/ppermute | solution.py:141
  113.5 18.5 %collective-permute-start.8 = (bf16[48,7296]{1,0:T(8,128)(2,1)S(1)}, bf16[48,7296]{1,0:T(8,128)(2,1)S(1)}, u32[]{:S(2)}, u32[]{:S(2)}) collective-permute-start(bf16[48,7296]{1,0:T(8,128)(2,1)S(1)} %shard_map.118.refs_0_), channel_id=1, source_target_pairs={{0,7},{1,0},{2,1},{3,2},{4,3},{5,4},{6,5},{7,6},{8,15},{9,8},{10,9... | collective-permute-start | bytes 2101256 | tf_op jit(solution)/shard_map/ppermute | solution.py:141
  116.2 1.5 copy-start.2
  132.0 3.6 %collective-permute-start.12 = (bf16[48,7296]{1,0:T(8,128)(2,1)S(1)}, bf16[48,7296]{1,0:T(8,128)(2,1)S(1)}, u32[]{:S(2)}, u32[]{:S(2)}) collective-permute-start(bf16[48,7296]{1,0:T(8,128)(2,1)S(1)} %collective-permute-done.7.refs_0_), channel_id=1, source_target_pairs={{0,128},{128,0},{1,129},{129,1},{2,130},{130,2},{3,131},{131,3},{4... | collective-permute-start | bytes 2101256 | tf_op jit(solution)/shard_map/ppermute | solution.py:289
  132.8 2.8 collective-permute-start.13
  132.8 18.1 %collective-permute-start.10 = (bf16[48,7296]{1,0:T(8,128)(2,1)S(1)}, bf16[48,7296]{1,0:T(8,128)(2,1)}, u32[]{:S(2)}, u32[]{:S(2)}) collective-permute-start(bf16[48,7296]{1,0:T(8,128)(2,1)S(1)} %collective-permute-done.7.refs_0_), channel_id=1, source_target_pairs={{0,1},{1,2},{2,3},{3,4},{4,5},{5,6},{6,7},{7,0},{8,9},{9,10},{10,1... | collective-permute-start | bytes 2101256 | tf_op jit(solution)/shard_map/ppermute | solution.py:141
  132.8 18.1 %collective-permute-start.11 = (bf16[48,7296]{1,0:T(8,128)(2,1)S(1)}, bf16[48,7296]{1,0:T(8,128)(2,1)}, u32[]{:S(2)}, u32[]{:S(2)}) collective-permute-start(bf16[48,7296]{1,0:T(8,128)(2,1)S(1)} %collective-permute-done.8.refs_1_), channel_id=1, source_target_pairs={{0,7},{1,0},{2,1},{3,2},{4,3},{5,4},{6,5},{7,6},{8,15},{9,8},{10,9... | collective-permute-start | bytes 2101256 | tf_op jit(solution)/shard_map/ppermute | solution.py:141
  150.9 4.0 %collective-permute-start.16 = (bf16[48,7296]{1,0:T(8,128)(2,1)}, bf16[48,7296]{1,0:T(8,128)(2,1)}, u32[]{:S(2)}, u32[]{:S(2)}) collective-permute-start(bf16[48,7296]{1,0:T(8,128)(2,1)} %collective-permute-done.10.refs_0_), channel_id=1, source_target_pairs={{0,128},{128,0},{1,129},{129,1},{2,130},{130,2},{3,131},{131,3},{4... | collective-permute-start | bytes 2101256 | tf_op jit(solution)/shard_map/ppermute | solution.py:289
  152.3 3.1 %collective-permute-start.17 = (bf16[48,7296]{1,0:T(8,128)(2,1)}, bf16[48,7296]{1,0:T(8,128)(2,1)}, u32[]{:S(2)}, u32[]{:S(2)}) collective-permute-start(bf16[48,7296]{1,0:T(8,128)(2,1)} %collective-permute-done.11.refs_1_), channel_id=1, source_target_pairs={{0,128},{128,0},{1,129},{129,1},{2,130},{130,2},{3,131},{131,3},{4... | collective-permute-start | bytes 2101256 | tf_op jit(solution)/shard_map/ppermute | solution.py:289
  152.3 18.3 %collective-permute-start.14 = (bf16[48,7296]{1,0:T(8,128)(2,1)}, bf16[48,7296]{1,0:T(8,128)(2,1)}, u32[]{:S(2)}, u32[]{:S(2)}) collective-permute-start(bf16[48,7296]{1,0:T(8,128)(2,1)} %collective-permute-done.10.refs_0_), channel_id=1, source_target_pairs={{0,1},{1,2},{2,3},{3,4},{4,5},{5,6},{6,7},{7,0},{8,9},{9,10},{10,1... | collective-permute-start | bytes 2101256 | tf_op jit(solution)/shard_map/ppermute | solution.py:141
  152.3 18.3 %collective-permute-start.15 = (bf16[48,7296]{1,0:T(8,128)(2,1)}, bf16[48,7296]{1,0:T(8,128)(2,1)}, u32[]{:S(2)}, u32[]{:S(2)}) collective-permute-start(bf16[48,7296]{1,0:T(8,128)(2,1)} %collective-permute-done.11.refs_1_), channel_id=1, source_target_pairs={{0,7},{1,0},{2,1},{3,2},{4,3},{5,4},{6,5},{7,6},{8,15},{9,8},{10,9... | collective-permute-start | bytes 2101256 | tf_op jit(solution)/shard_map/ppermute | solution.py:141
  155.4 1.5 copy-start.3
  170.6 15.0 %collective-permute-start.19 = (bf16[48,7296]{1,0:T(8,128)(2,1)}, bf16[48,7296]{1,0:T(8,128)(2,1)S(1)}, u32[]{:S(2)}, u32[]{:S(2)}) collective-permute-start(bf16[48,7296]{1,0:T(8,128)(2,1)} %collective-permute-done.14.refs_0_), channel_id=1, source_target_pairs={{0,128},{128,0},{1,129},{129,1},{2,130},{130,2},{3,131},{131,3},{4... | collective-permute-start | bytes 2101256 | tf_op jit(solution)/shard_map/ppermute | solution.py:289
  171.9 13.6 %collective-permute-start.20 = (bf16[48,7296]{1,0:T(8,128)(2,1)}, bf16[48,7296]{1,0:T(8,128)(2,1)S(1)}, u32[]{:S(2)}, u32[]{:S(2)}) collective-permute-start(bf16[48,7296]{1,0:T(8,128)(2,1)} %collective-permute-done.15.refs_1_), channel_id=1, source_target_pairs={{0,128},{128,0},{1,129},{129,1},{2,130},{130,2},{3,131},{131,3},{4... | collective-permute-start | bytes 2101256 | tf_op jit(solution)/shard_map/ppermute | solution.py:289
  182.8 10.8 %collective-permute-start.18 = (bf16[48,7296]{1,0:T(8,128)(2,1)S(1)}, bf16[48,7296]{1,0:T(8,128)(2,1)}, u32[]{:S(2)}, u32[]{:S(2)}) collective-permute-start(bf16[48,7296]{1,0:T(8,128)(2,1)S(1)} %broadcast_select_fusion), channel_id=1, source_target_pairs={{0,1},{1,2},{2,3},{3,4},{4,5},{5,6},{6,7},{7,0},{128,135},{129,128... | collective-permute-start | bytes 2101256 | tf_op jit(solution)/shard_map/ppermute | solution.py:144
  193.6 4.3 %collective-permute-start.21 = (bf16[48,7296]{1,0:T(8,128)(2,1)}, bf16[48,7296]{1,0:T(8,128)(2,1)}, u32[]{:S(2)}, u32[]{:S(2)}) collective-permute-start(bf16[48,7296]{1,0:T(8,128)(2,1)} %collective-permute-done.18.refs_0_), channel_id=1, source_target_pairs={{0,128},{128,0},{1,129},{129,1},{2,130},{130,2},{3,131},{131,3},{4... | collective-permute-start | bytes 2101256 | tf_op jit(solution)/shard_map/ppermute | solution.py:289
  197.9 1.5 copy-start.4
  201.6 26.2 %copy-start.5 = (bf16[2,448,128]{2,1,0:T(8,128)(2,1)S(1)}, bf16[2,448,128]{2,1,0:T(8,128)(2,1)}, u32[]{:S(2)}) copy-start(bf16[2,448,128]{2,1,0:T(8,128)(2,1)} %get-tuple-element.57.refs_9_) | copy-start | bytes 688132
  201.6 26.2 %copy-start.8 = (bf16[2,448,128]{2,1,0:T(8,128)(2,1)S(1)}, bf16[2,448,128]{2,1,0:T(8,128)(2,1)}, u32[]{:S(2)}) copy-start(bf16[2,448,128]{2,1,0:T(8,128)(2,1)} %copy-done.7) | copy-start | bytes 688132
  201.6 26.2 %copy-start.10 = (bf16[2,448,128]{2,1,0:T(8,128)(2,1)S(1)}, bf16[2,448,128]{2,1,0:T(8,128)(2,1)}, u32[]{:S(2)}) copy-start(bf16[2,448,128]{2,1,0:T(8,128)(2,1)} %copy-done.9) | copy-start | bytes 688132
  201.6 26.1 %copy-start.12 = (bf16[2,448,128]{2,1,0:T(8,128)(2,1)S(1)}, bf16[2,448,128]{2,1,0:T(8,128)(2,1)}, u32[]{:S(2)}) copy-start(bf16[2,448,128]{2,1,0:T(8,128)(2,1)} %copy-done.11) | copy-start | bytes 688132
  201.6 26.1 %copy-start.14 = (bf16[2,448,128]{2,1,0:T(8,128)(2,1)S(1)}, bf16[2,448,128]{2,1,0:T(8,128)(2,1)}, u32[]{:S(2)}) copy-start(bf16[2,448,128]{2,1,0:T(8,128)(2,1)} %copy-done.13) | copy-start | bytes 688132
  201.6 26.1 %copy-start.16 = (bf16[2,448,128]{2,1,0:T(8,128)(2,1)S(1)}, bf16[2,448,128]{2,1,0:T(8,128)(2,1)}, u32[]{:S(2)}) copy-start(bf16[2,448,128]{2,1,0:T(8,128)(2,1)} %copy-done.15) | copy-start | bytes 688132
  201.6 26.1 %copy-start.18 = (bf16[2,448,128]{2,1,0:T(8,128)(2,1)S(1)}, bf16[2,448,128]{2,1,0:T(8,128)(2,1)}, u32[]{:S(2)}) copy-start(bf16[2,448,128]{2,1,0:T(8,128)(2,1)} %copy-done.17) | copy-start | bytes 688132
  202.9 7.3 %collective-permute-start.22 = (bf16[768,128]{1,0:T(8,128)(2,1)S(1)}, bf16[768,128]{1,0:T(8,128)(2,1)S(1)}, u32[]{:S(2)}, u32[]{:S(2)}) collective-permute-start(bf16[768,128]{1,0:T(8,128)(2,1)S(1)} %get-tuple-element.66.refs_1_), channel_id=1, source_target_pairs={{0,1},{1,2},{2,3},{3,4},{4,5},{5,6},{6,7},{7,0},{8,9},{9,10},{10,1... | collective-permute-start | bytes 589832 | tf_op jit(solution)/shard_map/ppermute | solution.py:141
  202.9 7.3 %collective-permute-start.25 = (bf16[768,128]{1,0:T(8,128)(2,1)S(1)}, bf16[768,128]{1,0:T(8,128)(2,1)S(1)}, u32[]{:S(2)}, u32[]{:S(2)}) collective-permute-start(bf16[768,128]{1,0:T(8,128)(2,1)S(1)} %get-tuple-element.66.refs_1_), channel_id=1, source_target_pairs={{0,7},{1,0},{2,1},{3,2},{4,3},{5,4},{6,5},{7,6},{8,15},{9,8},{10,9... | collective-permute-start | bytes 589832 | tf_op jit(solution)/shard_map/ppermute | solution.py:141
  210.2 6.4 %collective-permute-start.23 = (bf16[768,128]{1,0:T(8,128)(2,1)S(1)}, bf16[768,128]{1,0:T(8,128)(2,1)S(1)}, u32[]{:S(2)}, u32[]{:S(2)}) collective-permute-start(bf16[768,128]{1,0:T(8,128)(2,1)S(1)} %collective-permute-done.22.refs_2_), channel_id=1, source_target_pairs={{0,1},{1,2},{2,3},{3,4},{4,5},{5,6},{6,7},{7,0},{8,9},{9,10},{10,1... | collective-permute-start | bytes 589832 | tf_op jit(solution)/shard_map/ppermute | solution.py:141
  210.2 6.4 %collective-permute-start.26 = (bf16[768,128]{1,0:T(8,128)(2,1)S(1)}, bf16[768,128]{1,0:T(8,128)(2,1)S(1)}, u32[]{:S(2)}, u32[]{:S(2)}) collective-permute-start(bf16[768,128]{1,0:T(8,128)(2,1)S(1)} %collective-permute-done.25.refs_8_), channel_id=1, source_target_pairs={{0,7},{1,0},{2,1},{3,2},{4,3},{5,4},{6,5},{7,6},{8,15},{9,8},{10,9... | collective-permute-start | bytes 589832 | tf_op jit(solution)/shard_map/ppermute | solution.py:141
  216.6 5.7 %collective-permute-start.24 = (bf16[768,128]{1,0:T(8,128)(2,1)S(1)}, bf16[768,128]{1,0:T(8,128)(2,1)S(1)}, u32[]{:S(2)}, u32[]{:S(2)}) collective-permute-start(bf16[768,128]{1,0:T(8,128)(2,1)S(1)} %collective-permute-done.23.refs_3_), channel_id=1, source_target_pairs={{0,1},{1,2},{2,3},{3,4},{4,5},{5,6},{6,7},{7,0},{8,9},{9,10},{10,1... | collective-permute-start | bytes 589832 | tf_op jit(solution)/shard_map/ppermute | solution.py:141
  216.6 5.7 %collective-permute-start.27 = (bf16[768,128]{1,0:T(8,128)(2,1)S(1)}, bf16[768,128]{1,0:T(8,128)(2,1)S(1)}, u32[]{:S(2)}, u32[]{:S(2)}) collective-permute-start(bf16[768,128]{1,0:T(8,128)(2,1)S(1)} %collective-permute-done.26.refs_7_), channel_id=1, source_target_pairs={{0,7},{1,0},{2,1},{3,2},{4,3},{5,4},{6,5},{7,6},{8,15},{9,8},{10,9... | collective-permute-start | bytes 589832 | tf_op jit(solution)/shard_map/ppermute | solution.py:141
  222.4 5.4 %collective-permute-start.28 = (bf16[768,128]{1,0:T(8,128)(2,1)S(1)}, bf16[768,128]{1,0:T(8,128)(2,1)S(1)}, u32[]{:S(2)}, u32[]{:S(2)}) collective-permute-start(bf16[768,128]{1,0:T(8,128)(2,1)S(1)} %broadcast_select_fusion.1), channel_id=1, source_target_pairs={{0,1},{1,2},{2,3},{3,4},{4,5},{5,6},{6,7},{7,0},{128,135},{129,128... | collective-permute-start | bytes 589832 | tf_op jit(solution)/shard_map/ppermute | solution.py:144
  231.7 7.0 %collective-permute-start.29 = (bf16[768,448]{0,1:T(8,128)(2,1)}, bf16[768,448]{0,1:T(8,128)(2,1)}, u32[]{:S(2)}, u32[]{:S(2)}) collective-permute-start(bf16[768,448]{0,1:T(8,128)(2,1)} %copy.95), channel_id=1, source_target_pairs={{0,128},{128,0},{1,129},{129,1},{2,130},{130,2},{3,131},{131,3},{4... | collective-permute-start | bytes 2064392 | tf_op jit(solution)/shard_map/ppermute | solution.py:289
  240.0 0.9 copy-start.6
  242.2 19.4 %all-to-all-start.3 = ((bf16[16,48,512]{2,1,0:T(8,128)(2,1)}), bf16[16,48,512]{2,1,0:T(8,128)(2,1)S(1)}, u32[]{:S(2)}, u32[]{:S(2)}) async-start(bf16[16,48,512]{2,1,0:T(8,128)(2,1)} %bitcast.31), calls=%async_computation.3 | async-start | bytes 1572864 | tf_op jit(solution)/shard_map/all_to_all | solution.py:317
  263.0 14.2 %all-to-all-start.4 = ((bf16[16,4,448]{2,1,0:T(4,128)(2,1)}), bf16[16,4,448]{2,1,0:T(4,128)(2,1)S(1)}, u32[]{:S(2)}, u32[]{:S(2)}) async-start(bf16[16,4,448]{2,1,0:T(4,128)(2,1)} %reshape.401), calls=%async_computation.4 | async-start | bytes 131072 | tf_op jit(solution)/shard_map/all_to_all | solution.py:329
where the time goes:
time: 284 us; the launch traced here: 279 us
  waiting for transfers between devices  131 us (46%)
  starting transfers between devices  90 us (32%)
  local copies, waits for them, and re-layouts  22.1 us (8%)
  Pallas kernels  17 us (6%)
  matrix products  12.1 us (4%)
  other arithmetic  6.48 us (2%)
    ppermute x6, waiting for transfers between devices, ring(): lax.ppermute(held[0], 'head', right)  48.7 us
    ppermute x7, waiting for transfers between devices, shift(): lax.ppermute(slabs[k], 'head', [(i, (i + k) % n_head) for i in range(n_he...  33.6 us
    ppermute x9, starting transfers between devices, swap(): return lax.ppermute(block, 'group', [(0, 1), (1, 0)])  22.5 us
    all_to_all x1, waiting for transfers between devices, local(): lax.all_to_all(partial.reshape(n_head, n_dp * rows, cols), 'head', split_...  16.2 us
    ppermute x6, starting transfers between devices, ring(): lax.ppermute(held[-1], 'head', left)  16.1 us
    ppermute x7, starting transfers between devices, shift(): lax.ppermute(slabs[k], 'head', [(i, (i + k) % n_head) for i in range(n_he...  12.9 us
    all_to_all x1, waiting for transfers between devices, local(): back = lax.all_to_all(out, 'dp', split_axis=0, concat_axis=0, tiled=True)  12.7 us
    pallas_call x5, Pallas kernels, gate_up(): pl.pallas_call(functools.partial(gate_up_kernel, len(blocks)), out_shape=...  11 us
  transfers between devices with their start and end apart: 35, of which 20 were waited for; matrix products, arithmetic and copies ran while one was open for 3% of the time, Pallas kernels for 3%

commit v1 on v0

--- a/solution.py
+++ b/solution.py
@@ -50,79 +50,68 @@
 
 
 def gate_up_kernel(count, *refs):
-    blocks, (gate_ref, up_ref, out_ref) = refs[:count], refs[count:]
+    blocks, (gate_ref, gate2_ref, up_ref, up2_ref, out_ref) = refs[:count], refs[count:]
     width = gate_ref.shape[0]
     step = 1024
     gate = up = 0.0
     for k in range(0, width, step):
         rows = jnp.concatenate([b[:, k : k + step] for b in blocks], axis=0)
-        gate += jnp.dot(rows, gate_ref[k : k + step], preferred_element_type=f32)
-        up += jnp.dot(rows, up_ref[k : k + step], preferred_element_type=f32)
-    out_ref[:, :LANES] = (gate / (1.0 + jnp.exp(-gate)) * up).astype(bf16)
-    out_ref[:, LANES:] = jnp.concatenate([b[:, width:] for b in blocks], axis=0)
-
-
-def gate_up(blocks, w_gate, w_up):
+        weights = jnp.concatenate([gate_ref[k : k + step], gate2_ref[k : k + step]], axis=1)
+        gate += jnp.dot(rows, weights, preferred_element_type=f32)
+        weights = jnp.concatenate([up_ref[k : k + step], up2_ref[k : k + step]], axis=1)
+        up += jnp.dot(rows, weights, preferred_element_type=f32)
+    out_ref[:, : 2 * LANES] = (gate / (1.0 + jnp.exp(-gate)) * up).astype(bf16)
+    out_ref[:, 2 * LANES :] = jnp.concatenate([b[:, width:] for b in blocks], axis=0)
+
+
+def gate_up(blocks, gates, ups):
     rows = sum(b.shape[0] for b in blocks)
+    width = gates[0].shape[0]
     return pl.pallas_call(
         functools.partial(gate_up_kernel, len(blocks)),
-        out_shape=jax.ShapeDtypeStruct((rows, 2 * LANES), bf16),
-        in_specs=[VMEM] * (len(blocks) + 2),
+        out_shape=jax.ShapeDtypeStruct((rows, 3 * LANES), bf16),
+        in_specs=[VMEM] * (len(blocks) + 4),
         out_specs=VMEM,
         compiler_params=pltpu.CompilerParams(vmem_limit_bytes=32 << 20),
-    )(*blocks, w_gate, w_up)
+        cost_estimate=pl.CostEstimate(
+            flops=8 * rows * width * LANES, bytes_accessed=8 * width * LANES, transcendentals=0
+        ),
+    )(*blocks, *gates, *ups)
 
 
 def down_kernel(count, *refs):
-    g_ref, refs = refs[0], refs[1:]
-    actives, downs, (keep_ref, give_ref) = refs[:count], refs[count : 2 * count], refs[2 * count :]
-    g = g_ref[0]
-    step = 256
-    for at, out_ref in ((g, keep_ref), (1 - g, give_ref)):
-        weights = [
-            jnp.concatenate([downs[k][at], downs[k + 1][at]], axis=1) for k in range(0, count, 2)
-        ]
-        for r in range(0, keep_ref.shape[0], step):
-            total = 0.0
-            for k in range(0, count, 2):
-                left = jnp.concatenate(
-                    [actives[k][r : r + step], actives[k + 1][r : r + step]], axis=1
-                )
-                total += lax.dot_general(
-                    left, weights[k // 2], (((1,), (1,)), ((), ())), preferred_element_type=f32
-                )
-            out_ref[r : r + step] = total.astype(out_ref.dtype)
-
-
-def down_sums(g, actives, downs):
-    shape = (actives[0].shape[0], downs[0].shape[1])
+    actives, downs, downs2 = refs[:count], refs[count : 2 * count], refs[2 * count : 3 * count]
+    facts_ref, out_ref = refs[3 * count :]
+    cols = downs[0].shape[0]
+    step = 128
+    weights = [
+        jnp.concatenate([one[...], two[...]], axis=1) for one, two in zip(downs, downs2)
+    ]
+    for r in range(0, out_ref.shape[0], step):
+        total = 0.0
+        for k in range(count):
+            total += lax.dot_general(
+                actives[k][r : r + step],
+                weights[k],
+                (((1,), (1,)), ((), ())),
+                preferred_element_type=f32,
+            )
+        facts = facts_ref[r : r + step].astype(f32)
+        total *= facts[:, :1] + facts[:, 1:2]
+        out_ref[r : r + step, :cols] = total.astype(bf16)
+        rest = out_ref.shape[1] - cols
+        out_ref[r : r + step, cols:] = jnp.broadcast_to(facts[:, 2:3], (step, rest)).astype(bf16)
+
+
+def down_sums(actives, downs, downs2, facts):
+    rows, cols = actives[0].shape[0], downs[0].shape[0]
     return pl.pallas_call(
         functools.partial(down_kernel, len(actives)),
-        out_shape=(jax.ShapeDtypeStruct(shape, f32), jax.ShapeDtypeStruct(shape, bf16)),
-        in_specs=[SMEM] + [VMEM] * (2 * len(actives)),
-        out_specs=(VMEM, VMEM),
-        compiler_params=pltpu.CompilerParams(vmem_limit_bytes=32 << 20),
-    )(g.reshape(1), *actives, *downs)
-
-
-def combine_kernel(keep_ref, got_ref, facts_ref, out_ref):
-    facts = facts_ref[...].astype(f32)
-    cols = keep_ref.shape[1]
-    total = (keep_ref[...] + got_ref[...].astype(f32)) * (facts[:, :1] + facts[:, 1:2])
-    out_ref[:, :cols] = total.astype(bf16)
-    rest = out_ref.shape[1] - cols
-    out_ref[:, cols:] = jnp.broadcast_to(facts[:, 2:3], (facts.shape[0], rest)).astype(bf16)
-
-
-def combine(keep, got, facts):
-    rows, cols = keep.shape
-    return pl.pallas_call(
-        combine_kernel,
-        out_shape=jax.ShapeDtypeStruct((rows, cols + -cols % LANES), bf16),
-        in_specs=[VMEM] * 3,
+        out_shape=jax.ShapeDtypeStruct((rows, cols + LANES), bf16),
+        in_specs=[VMEM] * (3 * len(actives) + 1),
         out_specs=VMEM,
         compiler_params=pltpu.CompilerParams(vmem_limit_bytes=32 << 20),
-    )(keep, got, facts)
+    )(*actives, *downs, *downs2, facts)
 
 
 def ring(block, beside):
@@ -176,24 +165,24 @@
     n_group = lax.axis_size("group")
     n_dp = lax.axis_size("dp")
     n_head = lax.axis_size("head")
-    n_col = n_group * n_head
     cols = width // n_dp
-    piece = width // n_col
-    g = lax.axis_index("group")
+    piece = width // n_head
     dp = lax.axis_index("dp")
     z = lax.axis_index("head")
 
-    slabs = w_down[0].reshape(n_group, n_head, piece, w_down.shape[2])
-    slabs = [
-        lax.dynamic_index_in_dim(slabs, lax.rem(z + k, n_head), 1, False) for k in range(n_head)
-    ]
-    shifts = [slabs[0]] + [None] * (n_head - 1)
-
-    def shift(some):
-        for k in some:
-            shifts[k] = lax.ppermute(
-                slabs[k], "head", [(i, (i + k) % n_head) for i in range(n_head)]
-            )
+    def swap(block):
+        return lax.ppermute(block, "group", [(0, 1), (1, 0)])
+
+    gates = (w_gate[0], swap(w_gate[0]))
+    ups = (w_up[0], swap(w_up[0]))
+
+    slabs = w_down[0].reshape(n_head, piece, w_down.shape[2])
+    downs = []
+    for k in range(n_head):
+        slab = lax.dynamic_index_in_dim(slabs, lax.rem(z + k, n_head), 0, False)
+        if k > 0:
+            slab = lax.ppermute(slab, "head", [(i, (i + k) % n_head) for i in range(n_head)])
+        downs.append(slab)
 
     expert_ids = jnp.arange(EXPERTS, dtype=jnp.int32)
     chosen = routes[0][:, :, None] == expert_ids[None, None, :]
@@ -231,9 +220,7 @@
         axis=1,
     )
     got = lax.all_to_all(send, "dp", split_axis=0, concat_axis=0, tiled=True)
-    shift((3, 5, 1, 7))
-    early = lax.optimization_barrier((got, shifts[3], shifts[5], shifts[1], shifts[7]))
-    got, shifts[3], shifts[5], shifts[1], shifts[7] = early
+    got, downs = lax.optimization_barrier((got, downs))
     res_piece = got[:, heads * reqs : heads * reqs + res_rows].reshape(n_dp * rows, cols)
     fact = got[:, heads * reqs + res_rows :, :rows]
     mine = fact[:, 0].reshape(1, n_dp * rows) > 0
@@ -247,8 +234,6 @@
     partial = lax.all_to_all(
         partial.reshape(n_head, n_dp * rows, cols), "head", split_axis=0, concat_axis=0, tiled=True
     )
-    held = lax.optimization_barrier((partial, slabs[4], slabs[2], slabs[6]))
-    partial, slabs[4], slabs[2], slabs[6] = held
     attended = jnp.sum(partial.astype(f32), axis=0).astype(bf16)
     hidden_piece = (res_piece.astype(f32) + attended.astype(f32)).astype(bf16)
 
@@ -259,9 +244,8 @@
         concat_axis=0,
         tiled=True,
     )
-    shift((4, 2, 6))
-    late = lax.optimization_barrier((hidden, shifts[4], shifts[2], shifts[6]))
-    hidden, shifts[4], shifts[2], shifts[6] = late
+    downs2 = [swap(d) for d in downs]
+    hidden, gates, ups, downs2 = lax.optimization_barrier((hidden, gates, ups, downs2))
     home = lax.dynamic_slice(hidden, (0, dp * rows, 0), (n_dp, rows, cols))
 
     def index(shape, axis):
@@ -285,41 +269,28 @@
     )
     packed = norm_pack(hidden, norm_gain.reshape(n_dp, cols), pack.astype(bf16), extra)
 
-    def swap(block):
-        return lax.ppermute(block, "group", [(0, 1), (1, 0)])
-
     fill = n_dp * CAP
-    def work(blocks):
-        return gate_up(blocks + tuple(swap(b) for b in blocks), w_gate[0], w_up[0])
-
-    _, done = ring(packed, work)
+    _, done = ring(packed, lambda blocks: gate_up(blocks, gates, ups))
     active = jnp.concatenate(done, axis=0)
 
-    r = index((1, n_col * fill), 1)
-    first, final = 2 * fill, (n_col - 2) * fill
-    at = jnp.where(r < first, 0, (r - first) // (4 * fill) + 1)
-    within = jnp.where(r < first, r, (r - first) % (4 * fill))
-    other = jnp.where((r < first) | (r >= final), within // fill, within // (2 * fill))
-    leftward = jnp.where((r < first) | (r >= final), 0, within // fill % 2)
-    from_z = jnp.where(leftward == 1, z + at, z - at + n_head) % n_head
-    from_g = jnp.where(other == 1, 1 - g, g)
-    home_dp, place = r % fill // CAP, r % CAP
-    to = home_dp * (n_col * CAP) + (from_g * n_head + from_z) * CAP + place
-    order = (index((n_col * fill, n_col * fill), 0) == to).astype(bf16)
+    r = index((1, n_head * fill), 1)
+    at = jnp.where(r < fill, 0, (r - fill) // (2 * fill) + 1)
+    leftward = (r >= fill) & ((r - fill) // fill % 2 == 1)
+    from_z = jnp.where(leftward, z + at, z - at + n_head) % n_head
+    to = r % fill // CAP * (n_head * CAP) + from_z * CAP + r % CAP
+    order = (index((n_head * fill, n_head * fill), 0) == to).astype(bf16)
     active = jnp.dot(order, active, preferred_element_type=f32).astype(bf16)
-    row_facts = active[:, LANES:]
-    active = active[:, :LANES]
-
-    steps, _ = ring(active, None)
+
+    steps, _ = ring(active[:, : 2 * LANES], None)
     actives = [s[0] for s in steps] + [s[1] for s in steps[-2:0:-1]]
-    keep, give = down_sums(g, actives, shifts)
-    out = combine(keep, swap(give), row_facts).reshape(n_dp, n_col * CAP, -1)
+    out = down_sums(actives, downs, downs2, active[:, 2 * LANES :])
+    out = out.reshape(n_dp, n_head * CAP, -1)
     back = lax.all_to_all(out, "dp", split_axis=0, concat_axis=0, tiled=True)
 
-    back = back.reshape(EXPERTS * n_col * CAP, -1)
-    token = index((back.shape[0], 1), 0) // CAP % n_col * rows
-    token = token.astype(f32) + back[:, piece : piece + 1].astype(f32)
-    hit = token == index((back.shape[0], n_col * rows), 1).astype(f32)
+    back = back.reshape(EXPERTS * n_head * CAP, -1)
+    token = (index((back.shape[0], 1), 0) // CAP % n_head * rows).astype(f32)
+    token = token + back[:, piece : piece + 1].astype(f32)
+    hit = token == index((back.shape[0], n_head * rows), 1).astype(f32)
     mixed = lax.dot_general(
         hit.astype(bf16),
         back[:, :piece],
@@ -327,14 +298,15 @@
         preferred_element_type=f32,
     )
     mixed = lax.all_to_all(
-        mixed.astype(bf16).reshape(n_col, rows, piece),
-        ("group", "head"),
+        mixed.astype(bf16).reshape(n_head, rows, piece),
+        "head",
         split_axis=0,
         concat_axis=0,
         tiled=True,
     )
+    home = home.transpose(1, 0, 2).reshape(rows, width)
+    mixed = mixed.transpose(1, 0, 2).reshape(rows, width)
     layer_out = (home.astype(f32) + mixed.astype(f32)).astype(bf16)
-    layer_out = layer_out.transpose(1, 0, 2).reshape(rows, width)
     return layer_out[None]
 
 

time: 284 us -> 279 us (0.982)
  the two profiles are of different devices: /device:TPU:1 before, /device:TPU:8 now
where the time goes in v1:
time: 279 us; the launch traced here: 274 us
  waiting for transfers between devices  134 us (48%)
  starting transfers between devices  76.5 us (27%)
  Pallas kernels  29 us (10%)
  matrix products  11.7 us (4%)
  other arithmetic  11.5 us (4%)
  local copies, waits for them, and re-layouts  10.6 us (4%)
    ppermute x7, waiting for transfers between devices, local(): lax.ppermute(slab, 'head', [(i, (i + k) % n_head) for i in range(n_head)])  37.1 us
    ppermute x6, waiting for transfers between devices, ring(): lax.ppermute(held[-1], 'head', left)  27.4 us
    pallas_call x5, Pallas kernels, gate_up(): pl.pallas_call(functools.partial(gate_up_kernel, len(blocks)), out_shape=...  20.7 us
    ppermute x6, starting transfers between devices, ring(): lax.ppermute(held[-1], 'head', left)  20.2 us
    ppermute x2, waiting for transfers between devices, ring(): got = (lax.ppermute(one, ('group', 'head'), both),)  13.5 us
    all_to_all x1, waiting for transfers between devices, local(): lax.all_to_all(partial.reshape(n_head, n_dp * rows, cols), 'head', split_...  13.3 us
    ppermute x7, starting transfers between devices, local(): lax.ppermute(slab, 'head', [(i, (i + k) % n_head) for i in range(n_head)])  12.9 us
    ppermute x6, waiting for transfers between devices, ring(): lax.ppermute(held[0], 'head', right)  12.7 us
  transfers between devices with their start and end apart: 36, of which 22 were waited for; matrix products, arithmetic and copies ran while one was open for 6% of the time, Pallas kernels for 6%

profile of v1, /device:TPU:8, one launch (start us, length us, event | category | flops | bytes accessed | tf_op | source)
XLA Modules:
  0.0 274.1 jit_solution(10564765617438366585)
XLA Ops:
  0.0 0.9 select_reduce_fusion
  1.7 0.9 reshape_squeeze.7
  2.9 6.1 %fusion.75 = (f32[32,8]{1,0:T(8,128)S(1)}, f32[32,8,192]{2,1,0:T(8,128)S(1)}) fusion(bf16[1,32,8,576]{3,2,1,0:T(8,128)(2,1)} %param.12, pred[32,192]{1,0:T(8,128)(4,1)S(1)} %iota_compare_fusion.4, bf16[1,32,192,576]{3,2,1,0:T(8,128)(2,1)} %param.13), kind=kOutput, calls=%fused_computation.154 | convolution fusion | flops 56819904 | bytes 7576576 | tf_op jit(solution)/shard_map/sub | solution.py:200
  8.9 3.7 %fusion.6 = bf16[32,8,512]{2,1,0:T(8,128)(2,1)S(1)} fusion(bf16[32,192,576]{2,1,0:T(8,128)(2,1)} %bitcast.87, f32[32,8,192]{2,1,0:T(8,128)S(1)} %get-tuple-element.80, f32[32,8]{1,0:T(8,128)S(1)} %get-tuple-element.79), kind=kOutput, calls=%fused_computation.9 | convolution fusion | flops 50561024 | bytes 6751232 | tf_op jit(solution)/shard_map/rhl,rlc->rhc/dot_general | solution.py:202
  13.2 1.1 fusion.11
  14.4 7.4 %all-to-all-start = ((bf16[16,272,128]{2,1,0:T(8,128)(2,1)}), bf16[16,272,128]{2,1,0:T(8,128)(2,1)}, u32[]{:S(2)}, u32[]{:S(2)}) async-start(bf16[16,272,128]{2,1,0:T(8,128)(2,1)} %fusion.11), calls=%async_computation | async-start | bytes 2228224 | tf_op jit(solution)/shard_map/all_to_all | solution.py:222
  21.9 5.9 %collective-permute-start.6 = (bf16[896,128]{1,0:T(8,128)(2,1)S(1)}, bf16[896,128]{1,0:T(8,128)(2,1)S(1)}, u32[]{:S(2)}, u32[]{:S(2)}) collective-permute-start(bf16[896,128]{1,0:T(8,128)(2,1)S(1)} %get-tuple-element.71), channel_id=1, source_target_pairs={{0,7},{1,0},{2,1},{3,2},{4,3},{5,4},{6,5},{7,6},{8,15},{9,8},{10,9... | collective-permute-start | bytes 688136 | tf_op jit(solution)/shard_map/ppermute | solution.py:184
  27.9 1.5 collective-permute-start.5
  29.8 5.0 %collective-permute-start.3 = (bf16[896,128]{1,0:T(8,128)(2,1)S(1)}, bf16[896,128]{1,0:T(8,128)(2,1)}, u32[]{:S(2)}, u32[]{:S(2)}) collective-permute-start(bf16[896,128]{1,0:T(8,128)(2,1)S(1)} %get-tuple-element.74), channel_id=1, source_target_pairs={{0,4},{1,5},{2,6},{3,7},{4,0},{5,1},{6,2},{7,3},{8,12},{9,13},{10,... | collective-permute-start | bytes 688136 | tf_op jit(solution)/shard_map/ppermute | solution.py:184
  34.8 3.6 %collective-permute-done.6.refs_15_ = bf16[896,128]{1,0:T(8,128)(2,1)S(1)} collective-permute-done((bf16[896,128]{1,0:T(8,128)(2,1)S(1)}, bf16[896,128]{1,0:T(8,128)(2,1)S(1)}, u32[]{:S(2)}, u32[]{:S(2)}) %collective-permute-start.6) | collective-permute-done | bytes 229408 | tf_op jit(solution)/shard_map/ppermute | solution.py:184
  38.4 14.7 %collective-permute-done.5.refs_14_ = bf16[896,128]{1,0:T(8,128)(2,1)} collective-permute-done((bf16[896,128]{1,0:T(8,128)(2,1)S(1)}, bf16[896,128]{1,0:T(8,128)(2,1)}, u32[]{:S(2)}, u32[]{:S(2)}) %collective-permute-start.5) | collective-permute-done | bytes 229408 | tf_op jit(solution)/shard_map/ppermute | solution.py:184
  53.1 1.2 copy.62
  54.3 12.3 %collective-permute-done.4.refs_13_ = bf16[896,128]{1,0:T(8,128)(2,1)S(1)} collective-permute-done((bf16[896,128]{1,0:T(8,128)(2,1)S(1)}, bf16[896,128]{1,0:T(8,128)(2,1)S(1)}, u32[]{:S(2)}, u32[]{:S(2)}) %collective-permute-start.4) | collective-permute-done | bytes 229408 | tf_op jit(solution)/shard_map/ppermute | solution.py:184
  67.8 4.2 %collective-permute-done.1.refs_10_ = bf16[896,128]{1,0:T(8,128)(2,1)} collective-permute-done((bf16[896,128]{1,0:T(8,128)(2,1)S(1)}, bf16[896,128]{1,0:T(8,128)(2,1)}, u32[]{:S(2)}, u32[]{:S(2)}) %collective-permute-start.1) | collective-permute-done | bytes 229408 | tf_op jit(solution)/shard_map/ppermute | solution.py:184
  72.0 2.3 collective-permute-done.refs_9_
  74.3 1.6 copy.48
  76.1 0.8 fusion.4
  76.9 0.9 copy.51
  77.8 4.1 %all-to-all-start.1 = ((bf16[8,64,448]{2,1,0:T(8,128)(2,1)}), bf16[8,64,448]{2,1,0:T(8,128)(2,1)}, u32[]{:S(2)}, u32[]{:S(2)}) async-start(bf16[8,64,448]{2,1,0:T(8,128)(2,1)} %copy.51), calls=%async_computation.1 | async-start | bytes 1048576 | tf_op jit(solution)/shard_map/all_to_all | solution.py:234
  82.7 1.5 slice_convert_fusion
  84.2 1.0 reshape.388
  85.3 0.7 collective-permute-start.10
  86.2 13.3 %all-to-all-done.1 = bf16[8,64,448]{2,1,0:T(8,128)(2,1)} async-done(((bf16[8,64,448]{2,1,0:T(8,128)(2,1)}), bf16[8,64,448]{2,1,0:T(8,128)(2,1)}, u32[]{:S(2)}, u32[]{:S(2)}) %all-to-all-start.1) | async-done | bytes 458784 | tf_op jit(solution)/shard_map/all_to_all | solution.py:234
  99.4 1.8 reduce_sum.22
  101.2 0.9 add_convert_fusion
  102.1 1.1 broadcast_in_dim.55
  103.2 7.2 %all-to-all-start.2 = ((bf16[16,64,448]{2,1,0:T(8,128)(2,1)}), bf16[16,64,448]{2,1,0:T(8,128)(2,1)}, u32[]{:S(2)}, u32[]{:S(2)}) async-start(bf16[16,64,448]{2,1,0:T(8,128)(2,1)} %broadcast_in_dim.55), calls=%async_computation.2 | async-start | bytes 2097152 | tf_op jit(solution)/shard_map/all_to_all | solution.py:240
  110.4 0.8 slice_bitcast_fusion
  111.8 0.8 compare_reduce_fusion
  114.2 0.8 collective-permute-done.14.refs_21_
  115.4 11.8 %all-to-all-done.2.hidden_ref = bf16[16,64,448]{2,1,0:T(8,128)(2,1)} async-done(((bf16[16,64,448]{2,1,0:T(8,128)(2,1)}), bf16[16,64,448]{2,1,0:T(8,128)(2,1)}, u32[]{:S(2)}, u32[]{:S(2)}) %all-to-all-start.2) | async-done | bytes 917536 | tf_op jit(solution)/shard_map/all_to_all | solution.py:240
  127.1 2.0 shard_map.118.refs_0_
  129.2 2.0 collective-permute-start.17
  131.2 4.0 %shard_map.119 = bf16[48,384]{1,0:T(8,128)(2,1)S(1)} custom-call(bf16[48,7296]{1,0:T(8,128)(2,1)S(1)} %shard_map.118.refs_0_, bf16[7168,128]{1,0:T(8,128)(2,1)S(1)} %bitcast.82, bf16[7168,128]{1,0:T(8,128)(2,1)} %collective-permute-done.7.refs_2_.refs_3_, bf16[7168,128]{1,0:T(8,128)(2,1)} %bitcast.26.refs_3_.refs_4_, ...), custom_call_target="tpu_custom_call" | custom-call | flops 352321536 | bytes 7340032 | tf_op jit(solution)/shard_map/pallas_call | solution.py:70
  135.2 8.7 %collective-permute-done.18.refs_1_ = bf16[48,7296]{1,0:T(8,128)(2,1)S(1)} collective-permute-done((bf16[48,7296]{1,0:T(8,128)(2,1)S(1)}, bf16[48,7296]{1,0:T(8,128)(2,1)S(1)}, u32[]{:S(2)}, u32[]{:S(2)}) %collective-permute-start.18) | collective-permute-done | bytes 700448 | tf_op jit(solution)/shard_map/ppermute | solution.py:130
  143.9 1.3 collective-permute-done.17.refs_0_
  145.2 1.8 collective-permute-start.19
  147.0 1.5 collective-permute-start.20
  148.4 3.9 %shard_map.120 = bf16[96,384]{1,0:T(8,128)(2,1)S(1)} custom-call(bf16[48,7296]{1,0:T(8,128)(2,1)S(1)} %collective-permute-done.17.refs_0_, bf16[48,7296]{1,0:T(8,128)(2,1)S(1)} %collective-permute-done.18.refs_1_, bf16[7168,128]{1,0:T(8,128)(2,1)S(1)} %bitcast.83, bf16[7168,128]{1,0:T(8,128)(2,1)} %collective-permute-done.7.refs_2_.refs_3_, ...), custom_call_target="tpu_custom_call" | custom-call | flops 704643072 | bytes 7340032 | tf_op jit(solution)/shard_map/pallas_call | solution.py:70
  152.4 8.5 %collective-permute-done.19.refs_0_ = bf16[48,7296]{1,0:T(8,128)(2,1)} collective-permute-done((bf16[48,7296]{1,0:T(8,128)(2,1)S(1)}, bf16[48,7296]{1,0:T(8,128)(2,1)}, u32[]{:S(2)}, u32[]{:S(2)}) %collective-permute-start.19) | collective-permute-done | bytes 700448 | tf_op jit(solution)/shard_map/ppermute | solution.py:130
  160.9 1.7 collective-permute-start.21
  162.6 10.6 %collective-permute-start.22 = (bf16[48,7296]{1,0:T(8,128)(2,1)}, bf16[48,7296]{1,0:T(8,128)(2,1)}, u32[]{:S(2)}, u32[]{:S(2)}) collective-permute-start(bf16[48,7296]{1,0:T(8,128)(2,1)} %collective-permute-done.20.refs_1_), channel_id=1, source_target_pairs={{0,7},{1,0},{2,1},{3,2},{4,3},{5,4},{6,5},{7,6},{8,15},{9,8},{10,9... | collective-permute-start | bytes 2101256 | tf_op jit(solution)/shard_map/ppermute | solution.py:130
  173.2 4.3 %shard_map.121 = bf16[96,384]{1,0:T(8,128)(2,1)S(1)} custom-call(bf16[48,7296]{1,0:T(8,128)(2,1)} %collective-permute-done.19.refs_0_, bf16[48,7296]{1,0:T(8,128)(2,1)} %collective-permute-done.20.refs_1_, bf16[7168,128]{1,0:T(8,128)(2,1)S(1)} %bitcast.84, bf16[7168,128]{1,0:T(8,128)(2,1)} %collective-permute-done.7.refs_2_.refs_3_, ...), custom_call_target="tpu_custom_call" | custom-call | flops 704643072 | bytes 7340032 | tf_op jit(solution)/shard_map/pallas_call | solution.py:70
  177.5 8.0 %collective-permute-done.22.refs_1_ = bf16[48,7296]{1,0:T(8,128)(2,1)} collective-permute-done((bf16[48,7296]{1,0:T(8,128)(2,1)}, bf16[48,7296]{1,0:T(8,128)(2,1)}, u32[]{:S(2)}, u32[]{:S(2)}) %collective-permute-start.22) | collective-permute-done | bytes 700448 | tf_op jit(solution)/shard_map/ppermute | solution.py:130
  185.5 1.2 broadcast_select_fusion
  186.7 1.2 collective-permute-start.23
  188.0 4.4 %shard_map.122 = bf16[96,384]{1,0:T(8,128)(2,1)S(1)} custom-call(bf16[48,7296]{1,0:T(8,128)(2,1)} %collective-permute-done.21.refs_0_, bf16[48,7296]{1,0:T(8,128)(2,1)} %collective-permute-done.22.refs_1_, bf16[7168,128]{1,0:T(8,128)(2,1)S(1)} %bitcast.85, bf16[7168,128]{1,0:T(8,128)(2,1)} %collective-permute-done.7.refs_2_.refs_3_, ...), custom_call_target="tpu_custom_call" | custom-call | flops 704643072 | bytes 7340032 | tf_op jit(solution)/shard_map/pallas_call | solution.py:70
  192.3 6.7 %collective-permute-done.23.refs_0_ = bf16[48,7296]{1,0:T(8,128)(2,1)S(1)} collective-permute-done((bf16[48,7296]{1,0:T(8,128)(2,1)S(1)}, bf16[48,7296]{1,0:T(8,128)(2,1)S(1)}, u32[]{:S(2)}, u32[]{:S(2)}) %collective-permute-start.23) | collective-permute-done | bytes 700448 | tf_op jit(solution)/shard_map/ppermute | solution.py:133
  199.0 4.0 %shard_map.123 = bf16[48,384]{1,0:T(8,128)(2,1)S(1)} custom-call(bf16[48,7296]{1,0:T(8,128)(2,1)S(1)} %collective-permute-done.23.refs_0_, bf16[7168,128]{1,0:T(8,128)(2,1)S(1)} %bitcast.86, bf16[7168,128]{1,0:T(8,128)(2,1)} %collective-permute-done.7.refs_2_.refs_3_, bf16[7168,128]{1,0:T(8,128)(2,1)} %bitcast.26.refs_3_.refs_4_, ...), custom_call_target="tpu_custom_call" | custom-call | flops 352321536 | bytes 7340032 | tf_op jit(solution)/shard_map/pallas_call | solution.py:70
  203.5 1.3 collective-permute-start.27
  204.8 0.8 collective-permute-start.24
  205.6 3.6 %collective-permute-done.27.refs_7_ = bf16[384,256]{1,0:T(8,128)(2,1)S(1)} collective-permute-done((bf16[384,256]{1,0:T(8,128)(2,1)S(1)}, bf16[384,256]{1,0:T(8,128)(2,1)S(1)}, u32[]{:S(2)}, u32[]{:S(2)}) %collective-permute-start.27) | collective-permute-done | bytes 196640 | tf_op jit(solution)/shard_map/ppermute | solution.py:130
  209.2 3.0 %collective-permute-start.28 = (bf16[384,256]{1,0:T(8,128)(2,1)S(1)}, bf16[384,256]{1,0:T(8,128)(2,1)S(1)}, u32[]{:S(2)}, u32[]{:S(2)}) collective-permute-start(bf16[384,256]{1,0:T(8,128)(2,1)S(1)} %collective-permute-done.27.refs_7_), channel_id=1, source_target_pairs={{0,7},{1,0},{2,1},{3,2},{4,3},{5,4},{6,5},{7,6},{8,15},{9,8},{10,9... | collective-permute-start | bytes 589832 | tf_op jit(solution)/shard_map/ppermute | solution.py:130
  212.2 3.2 %collective-permute-done.28.refs_6_ = bf16[384,256]{1,0:T(8,128)(2,1)S(1)} collective-permute-done((bf16[384,256]{1,0:T(8,128)(2,1)S(1)}, bf16[384,256]{1,0:T(8,128)(2,1)S(1)}, u32[]{:S(2)}, u32[]{:S(2)}) %collective-permute-start.28) | collective-permute-done | bytes 196640 | tf_op jit(solution)/shard_map/ppermute | solution.py:130
  215.4 3.7 %collective-permute-start.29 = (bf16[384,256]{1,0:T(8,128)(2,1)S(1)}, bf16[384,256]{1,0:T(8,128)(2,1)S(1)}, u32[]{:S(2)}, u32[]{:S(2)}) collective-permute-start(bf16[384,256]{1,0:T(8,128)(2,1)S(1)} %collective-permute-done.28.refs_6_), channel_id=1, source_target_pairs={{0,7},{1,0},{2,1},{3,2},{4,3},{5,4},{6,5},{7,6},{8,15},{9,8},{10,9... | collective-permute-start | bytes 589832 | tf_op jit(solution)/shard_map/ppermute | solution.py:130
  219.1 3.9 %collective-permute-done.29.refs_5_ = bf16[384,256]{1,0:T(8,128)(2,1)S(1)} collective-permute-done((bf16[384,256]{1,0:T(8,128)(2,1)S(1)}, bf16[384,256]{1,0:T(8,128)(2,1)S(1)}, u32[]{:S(2)}, u32[]{:S(2)}) %collective-permute-start.29) | collective-permute-done | bytes 196640 | tf_op jit(solution)/shard_map/ppermute | solution.py:130
  223.0 2.9 %collective-permute-done.26.refs_3_ = bf16[384,256]{1,0:T(8,128)(2,1)S(1)} collective-permute-done((bf16[384,256]{1,0:T(8,128)(2,1)S(1)}, bf16[384,256]{1,0:T(8,128)(2,1)S(1)}, u32[]{:S(2)}, u32[]{:S(2)}) %collective-permute-start.26) | collective-permute-done | bytes 196640 | tf_op jit(solution)/shard_map/ppermute | solution.py:130
  226.1 6.9 %collective-permute-done.30.refs_4_ = bf16[384,256]{1,0:T(8,128)(2,1)S(1)} collective-permute-done((bf16[384,256]{1,0:T(8,128)(2,1)S(1)}, bf16[384,256]{1,0:T(8,128)(2,1)S(1)}, u32[]{:S(2)}, u32[]{:S(2)}) %collective-permute-start.30) | collective-permute-done | bytes 196640 | tf_op jit(solution)/shard_map/ppermute | solution.py:133
  233.0 6.4 %shard_map.124 = bf16[384,1024]{1,0:T(8,128)(2,1)} custom-call(bf16[384,256]{1,0:T(8,128)(2,1)S(1)} %slice.39.refs_0_, bf16[384,256]{1,0:T(8,128)(2,1)S(1)} %collective-permute-done.24.refs_1_, bf16[384,256]{1,0:T(8,128)(2,1)S(1)} %collective-permute-done.25.refs_2_, bf16[384,256]{1,0:T(8,128)(2,1)S(1)} %collective-permute-done.26.refs_3_, ...), custom_call_target="tpu_custom_call" | custom-call | tf_op jit(solution)/shard_map/pallas_call | solution.py:108
  239.3 11.0 %all-to-all-start.3 = ((bf16[16,24,1024]{2,1,0:T(8,128)(2,1)}), bf16[16,24,1024]{2,1,0:T(8,128)(2,1)S(1)}, u32[]{:S(2)}, u32[]{:S(2)}) async-start(bf16[16,24,1024]{2,1,0:T(8,128)(2,1)} %bitcast.31), calls=%async_computation.3 | async-start | bytes 1572864 | tf_op jit(solution)/shard_map/all_to_all | solution.py:288
  250.4 10.1 %all-to-all-done.3 = bf16[16,24,1024]{2,1,0:T(8,128)(2,1)S(1)} async-done(((bf16[16,24,1024]{2,1,0:T(8,128)(2,1)}), bf16[16,24,1024]{2,1,0:T(8,128)(2,1)S(1)}, u32[]{:S(2)}, u32[]{:S(2)}) %all-to-all-start.3) | async-done | bytes 786464 | tf_op jit(solution)/shard_map/all_to_all | solution.py:288
  261.7 3.3 %all-to-all-start.4 = ((bf16[8,4,896]{2,1,0:T(4,128)(2,1)}), bf16[8,4,896]{2,1,0:T(4,128)(2,1)S(1)}, u32[]{:S(2)}, u32[]{:S(2)}) async-start(bf16[8,4,896]{2,1,0:T(4,128)(2,1)} %reshape.387), calls=%async_computation.4 | async-start | bytes 114688 | tf_op jit(solution)/shard_map/all_to_all | solution.py:300
  265.1 0.9 convert_bitcast_fusion
  266.2 7.1 %all-to-all-done.4 = bf16[8,4,896]{2,1,0:T(4,128)(2,1)S(1)} async-done(((bf16[8,4,896]{2,1,0:T(4,128)(2,1)}), bf16[8,4,896]{2,1,0:T(4,128)(2,1)S(1)}, u32[]{:S(2)}, u32[]{:S(2)}) %all-to-all-start.4) | async-done | bytes 57376 | tf_op jit(solution)/shard_map/all_to_all | solution.py:300
  (97 shorter events, 9.8 us)
Async XLA Ops:
  0.0 12.7 %copy-start = (bf16[8,512,128]{2,1,0:T(8,128)(2,1)S(1)}, bf16[8,512,128]{2,1,0:T(8,128)(2,1)}, u32[]{:S(2)}) copy-start(bf16[8,512,128]{2,1,0:T(8,128)(2,1)} %param.15) | copy-start | bytes 3145732
  13.2 8.5 %copy-start.4 = (bf16[1,7168,128]{2,1,0:T(8,128)(2,1)S(1)}, bf16[1,7168,128]{2,1,0:T(8,128)(2,1)}, u32[]{:S(2)}) copy-start(bf16[1,7168,128]{2,1,0:T(8,128)(2,1)} %param.23) | copy-start | bytes 5505028
  14.4 59.9 %all-to-all-start = ((bf16[16,272,128]{2,1,0:T(8,128)(2,1)}), bf16[16,272,128]{2,1,0:T(8,128)(2,1)}, u32[]{:S(2)}, u32[]{:S(2)}) async-start(bf16[16,272,128]{2,1,0:T(8,128)(2,1)} %fusion.11), calls=%async_computation | async-start | bytes 2228224 | tf_op jit(solution)/shard_map/all_to_all | solution.py:222
  21.8 31.4 %copy-start.5 = (bf16[1024,448]{0,1:T(8,128)(2,1)S(1)}, bf16[1024,448]{0,1:T(8,128)(2,1)}, u32[]{:S(2)}) copy-start(bf16[1024,448]{0,1:T(8,128)(2,1)} %param.16) | copy-start | bytes 2752516
  21.9 45.4 %copy-start.1 = (bf16[1,7168,128]{2,1,0:T(8,128)(2,1)S(1)}, bf16[1,7168,128]{2,1,0:T(8,128)(2,1)}, u32[]{:S(2)}) copy-start(bf16[1,7168,128]{2,1,0:T(8,128)(2,1)} %param.21) | copy-start | bytes 5505028
  21.9 16.5 %collective-permute-start.6 = (bf16[896,128]{1,0:T(8,128)(2,1)S(1)}, bf16[896,128]{1,0:T(8,128)(2,1)S(1)}, u32[]{:S(2)}, u32[]{:S(2)}) collective-permute-start(bf16[896,128]{1,0:T(8,128)(2,1)S(1)} %get-tuple-element.71), channel_id=1, source_target_pairs={{0,7},{1,0},{2,1},{3,2},{4,3},{5,4},{6,5},{7,6},{8,15},{9,8},{10,9... | collective-permute-start | bytes 688136 | tf_op jit(solution)/shard_map/ppermute | solution.py:184
  27.9 25.3 %collective-permute-start.5 = (bf16[896,128]{1,0:T(8,128)(2,1)S(1)}, bf16[896,128]{1,0:T(8,128)(2,1)}, u32[]{:S(2)}, u32[]{:S(2)}) collective-permute-start(bf16[896,128]{1,0:T(8,128)(2,1)S(1)} %get-tuple-element.72), channel_id=1, source_target_pairs={{0,6},{1,7},{2,0},{3,1},{4,2},{5,3},{6,4},{7,5},{8,14},{9,15},{10,... | collective-permute-start | bytes 688136 | tf_op jit(solution)/shard_map/ppermute | solution.py:184
  29.3 37.3 %collective-permute-start.4 = (bf16[896,128]{1,0:T(8,128)(2,1)S(1)}, bf16[896,128]{1,0:T(8,128)(2,1)S(1)}, u32[]{:S(2)}, u32[]{:S(2)}) collective-permute-start(bf16[896,128]{1,0:T(8,128)(2,1)S(1)} %get-tuple-element.73), channel_id=1, source_target_pairs={{0,5},{1,6},{2,7},{3,0},{4,1},{5,2},{6,3},{7,4},{8,13},{9,14},{10,... | collective-permute-start | bytes 688136 | tf_op jit(solution)/shard_map/ppermute | solution.py:184
  29.8 37.5 %collective-permute-start.3 = (bf16[896,128]{1,0:T(8,128)(2,1)S(1)}, bf16[896,128]{1,0:T(8,128)(2,1)}, u32[]{:S(2)}, u32[]{:S(2)}) collective-permute-start(bf16[896,128]{1,0:T(8,128)(2,1)S(1)} %get-tuple-element.74), channel_id=1, source_target_pairs={{0,4},{1,5},{2,6},{3,7},{4,0},{5,1},{6,2},{7,3},{8,12},{9,13},{10,... | collective-permute-start | bytes 688136 | tf_op jit(solution)/shard_map/ppermute | solution.py:184
  34.8 33.0 %collective-permute-start.2 = (bf16[896,128]{1,0:T(8,128)(2,1)S(1)}, bf16[896,128]{1,0:T(8,128)(2,1)}, u32[]{:S(2)}, u32[]{:S(2)}) collective-permute-start(bf16[896,128]{1,0:T(8,128)(2,1)S(1)} %get-tuple-element.75), channel_id=1, source_target_pairs={{0,3},{1,4},{2,5},{3,6},{4,7},{5,0},{6,1},{7,2},{8,11},{9,12},{10,... | collective-permute-start | bytes 688136 | tf_op jit(solution)/shard_map/ppermute | solution.py:184
  38.4 33.6 %collective-permute-start.1 = (bf16[896,128]{1,0:T(8,128)(2,1)S(1)}, bf16[896,128]{1,0:T(8,128)(2,1)}, u32[]{:S(2)}, u32[]{:S(2)}) collective-permute-start(bf16[896,128]{1,0:T(8,128)(2,1)S(1)} %get-tuple-element.76), channel_id=1, source_target_pairs={{0,2},{1,3},{2,4},{3,5},{4,6},{5,7},{6,0},{7,1},{8,10},{9,11},{10,... | collective-permute-start | bytes 688136 | tf_op jit(solution)/shard_map/ppermute | solution.py:184
  53.1 21.2 %collective-permute-start = (bf16[896,128]{1,0:T(8,128)(2,1)S(1)}, bf16[896,128]{1,0:T(8,128)(2,1)}, u32[]{:S(2)}, u32[]{:S(2)}) collective-permute-start(bf16[896,128]{1,0:T(8,128)(2,1)S(1)} %get-tuple-element.77), channel_id=1, source_target_pairs={{0,1},{1,2},{2,3},{3,4},{4,5},{5,6},{6,7},{7,0},{8,9},{9,10},{10,1... | collective-permute-start | bytes 688136 | tf_op jit(solution)/shard_map/ppermute | solution.py:184
  66.6 0.7 copy-start.2
  67.3 48.1 %collective-permute-start.7 = (bf16[7168,128]{1,0:T(8,128)(2,1)S(1)}, bf16[7168,128]{1,0:T(8,128)(2,1)}, u32[]{:S(2)}, u32[]{:S(2)}) collective-permute-start(bf16[7168,128]{1,0:T(8,128)(2,1)S(1)} %bitcast.81), channel_id=1, source_target_pairs={{0,128},{128,0},{1,129},{129,1},{2,130},{130,2},{3,131},{131,3},{4... | collective-permute-start | bytes 5505032 | tf_op jit(solution)/shard_map/ppermute | solution.py:174
  67.3 48.1 %collective-permute-start.8 = (bf16[7168,128]{1,0:T(8,128)(2,1)}, bf16[7168,128]{1,0:T(8,128)(2,1)}, u32[]{:S(2)}, u32[]{:S(2)}) collective-permute-start(bf16[7168,128]{1,0:T(8,128)(2,1)} %bitcast.26.refs_3_.refs_4_), channel_id=1, source_target_pairs={{0,128},{128,0},{1,129},{129,1},{2,130},{130,2},{3,131},{131,3},{4... | collective-permute-start | bytes 5505032 | tf_op jit(solution)/shard_map/ppermute | solution.py:174
  74.3 1.8 copy-start.6
  76.9 5.1 %copy-start.7 = (f32[7168]{0:T(1024)S(1)}, f32[7168]{0:T(1024)}, u32[]{:S(2)}) copy-start(f32[7168]{0:T(1024)} %param.18) | copy-start | bytes 86020
  77.8 21.6 %all-to-all-start.1 = ((bf16[8,64,448]{2,1,0:T(8,128)(2,1)}), bf16[8,64,448]{2,1,0:T(8,128)(2,1)}, u32[]{:S(2)}, u32[]{:S(2)}) async-start(bf16[8,64,448]{2,1,0:T(8,128)(2,1)} %copy.51), calls=%async_computation.1 | async-start | bytes 1048576 | tf_op jit(solution)/shard_map/all_to_all | solution.py:234
  85.2 26.0 %collective-permute-start.9 = (bf16[896,128]{1,0:T(8,128)(2,1)S(1)}, bf16[896,128]{1,0:T(8,128)(2,1)}, u32[]{:S(2)}, u32[]{:S(2)}) collective-permute-start(bf16[896,128]{1,0:T(8,128)(2,1)S(1)} %get-tuple-element.39.refs_8_), channel_id=1, source_target_pairs={{0,128},{128,0},{1,129},{129,1},{2,130},{130,2},{3,131},{131,3},{4... | collective-permute-start | bytes 688136 | tf_op jit(solution)/shard_map/ppermute | solution.py:174
  85.3 26.0 %collective-permute-start.10 = (bf16[896,128]{1,0:T(8,128)(2,1)}, bf16[896,128]{1,0:T(8,128)(2,1)}, u32[]{:S(2)}, u32[]{:S(2)}) collective-permute-start(bf16[896,128]{1,0:T(8,128)(2,1)} %collective-permute-done.refs_9_), channel_id=1, source_target_pairs={{0,128},{128,0},{1,129},{129,1},{2,130},{130,2},{3,131},{131,3},{4... | collective-permute-start | bytes 688136 | tf_op jit(solution)/shard_map/ppermute | solution.py:174
  86.1 26.9 %collective-permute-start.11 = (bf16[896,128]{1,0:T(8,128)(2,1)}, bf16[896,128]{1,0:T(8,128)(2,1)}, u32[]{:S(2)}, u32[]{:S(2)}) collective-permute-start(bf16[896,128]{1,0:T(8,128)(2,1)} %collective-permute-done.1.refs_10_), channel_id=1, source_target_pairs={{0,128},{128,0},{1,129},{129,1},{2,130},{130,2},{3,131},{131,3},{4... | collective-permute-start | bytes 688136 | tf_op jit(solution)/shard_map/ppermute | solution.py:174
  102.1 12.0 %copy-start.8 = (pred[48]{0:T(512)(128)(4,1)S(1)}, pred[48]{0:T(512)(128)(4,1)}, u32[]{:S(2)}) copy-start(pred[48]{0:T(512)(128)(4,1)} %get-tuple-element.81) | copy-start | bytes 148
  102.1 12.0 %copy-start.9 = (pred[48]{0:T(512)(128)(4,1)S(1)}, pred[48]{0:T(512)(128)(4,1)}, u32[]{:S(2)}) copy-start(pred[48]{0:T(512)(128)(4,1)} %get-tuple-element.82) | copy-start | bytes 148
  103.2 24.0 %all-to-all-start.2 = ((bf16[16,64,448]{2,1,0:T(8,128)(2,1)}), bf16[16,64,448]{2,1,0:T(8,128)(2,1)}, u32[]{:S(2)}, u32[]{:S(2)}) async-start(bf16[16,64,448]{2,1,0:T(8,128)(2,1)} %broadcast_in_dim.55), calls=%async_computation.2 | async-start | bytes 2097152 | tf_op jit(solution)/shard_map/all_to_all | solution.py:240
  111.2 2.0 collective-permute-start.12
  111.3 2.3 collective-permute-start.13
  113.0 1.9 collective-permute-start.14
  113.2 2.0 collective-permute-start.15
  113.6 1.8 collective-permute-start.16
  129.1 14.8 %collective-permute-start.18 = (bf16[48,7296]{1,0:T(8,128)(2,1)S(1)}, bf16[48,7296]{1,0:T(8,128)(2,1)S(1)}, u32[]{:S(2)}, u32[]{:S(2)}) collective-permute-start(bf16[48,7296]{1,0:T(8,128)(2,1)S(1)} %shard_map.118.refs_0_), channel_id=1, source_target_pairs={{0,7},{1,0},{2,1},{3,2},{4,3},{5,4},{6,5},{7,6},{8,15},{9,8},{10,9... | collective-permute-start | bytes 2101256 | tf_op jit(solution)/shard_map/ppermute | solution.py:130
  129.2 16.0 %collective-permute-start.17 = (bf16[48,7296]{1,0:T(8,128)(2,1)S(1)}, bf16[48,7296]{1,0:T(8,128)(2,1)S(1)}, u32[]{:S(2)}, u32[]{:S(2)}) collective-permute-start(bf16[48,7296]{1,0:T(8,128)(2,1)S(1)} %shard_map.118.refs_0_), channel_id=1, source_target_pairs={{0,1},{1,2},{2,3},{3,4},{4,5},{5,6},{6,7},{7,0},{8,9},{9,10},{10,1... | collective-permute-start | bytes 2101256 | tf_op jit(solution)/shard_map/ppermute | solution.py:130
  145.2 15.7 %collective-permute-start.19 = (bf16[48,7296]{1,0:T(8,128)(2,1)S(1)}, bf16[48,7296]{1,0:T(8,128)(2,1)}, u32[]{:S(2)}, u32[]{:S(2)}) collective-permute-start(bf16[48,7296]{1,0:T(8,128)(2,1)S(1)} %collective-permute-done.17.refs_0_), channel_id=1, source_target_pairs={{0,1},{1,2},{2,3},{3,4},{4,5},{5,6},{6,7},{7,0},{8,9},{9,10},{10,1... | collective-permute-start | bytes 2101256 | tf_op jit(solution)/shard_map/ppermute | solution.py:130
  147.0 13.9 %collective-permute-start.20 = (bf16[48,7296]{1,0:T(8,128)(2,1)S(1)}, bf16[48,7296]{1,0:T(8,128)(2,1)}, u32[]{:S(2)}, u32[]{:S(2)}) collective-permute-start(bf16[48,7296]{1,0:T(8,128)(2,1)S(1)} %collective-permute-done.18.refs_1_), channel_id=1, source_target_pairs={{0,7},{1,0},{2,1},{3,2},{4,3},{5,4},{6,5},{7,6},{8,15},{9,8},{10,9... | collective-permute-start | bytes 2101256 | tf_op jit(solution)/shard_map/ppermute | solution.py:130
  160.9 16.7 %collective-permute-start.21 = (bf16[48,7296]{1,0:T(8,128)(2,1)}, bf16[48,7296]{1,0:T(8,128)(2,1)}, u32[]{:S(2)}, u32[]{:S(2)}) collective-permute-start(bf16[48,7296]{1,0:T(8,128)(2,1)} %collective-permute-done.19.refs_0_), channel_id=1, source_target_pairs={{0,1},{1,2},{2,3},{3,4},{4,5},{5,6},{6,7},{7,0},{8,9},{9,10},{10,1... | collective-permute-start | bytes 2101256 | tf_op jit(solution)/shard_map/ppermute | solution.py:130
  162.6 22.9 %collective-permute-start.22 = (bf16[48,7296]{1,0:T(8,128)(2,1)}, bf16[48,7296]{1,0:T(8,128)(2,1)}, u32[]{:S(2)}, u32[]{:S(2)}) collective-permute-start(bf16[48,7296]{1,0:T(8,128)(2,1)} %collective-permute-done.20.refs_1_), channel_id=1, source_target_pairs={{0,7},{1,0},{2,1},{3,2},{4,3},{5,4},{6,5},{7,6},{8,15},{9,8},{10,9... | collective-permute-start | bytes 2101256 | tf_op jit(solution)/shard_map/ppermute | solution.py:130
  186.7 12.4 %collective-permute-start.23 = (bf16[48,7296]{1,0:T(8,128)(2,1)S(1)}, bf16[48,7296]{1,0:T(8,128)(2,1)S(1)}, u32[]{:S(2)}, u32[]{:S(2)}) collective-permute-start(bf16[48,7296]{1,0:T(8,128)(2,1)S(1)} %broadcast_select_fusion), channel_id=1, source_target_pairs={{0,1},{1,2},{2,3},{3,4},{4,5},{5,6},{6,7},{7,0},{128,135},{129,128... | collective-permute-start | bytes 2101256 | tf_op jit(solution)/shard_map/ppermute | solution.py:133
  203.1 29.9 %copy-start.3 = (bf16[896,128]{1,0:T(8,128)(2,1)S(1)}, bf16[896,128]{1,0:T(8,128)(2,1)}, u32[]{:S(2)}) copy-start(bf16[896,128]{1,0:T(8,128)(2,1)} %copy-done.2) | copy-start | bytes 688132
  203.5 5.7 %collective-permute-start.27 = (bf16[384,256]{1,0:T(8,128)(2,1)S(1)}, bf16[384,256]{1,0:T(8,128)(2,1)S(1)}, u32[]{:S(2)}, u32[]{:S(2)}) collective-permute-start(bf16[384,256]{1,0:T(8,128)(2,1)S(1)} %slice.39.refs_0_), channel_id=1, source_target_pairs={{0,7},{1,0},{2,1},{3,2},{4,3},{5,4},{6,5},{7,6},{8,15},{9,8},{10,9... | collective-permute-start | bytes 589832 | tf_op jit(solution)/shard_map/ppermute | solution.py:130
  204.8 7.4 %collective-permute-start.24 = (bf16[384,256]{1,0:T(8,128)(2,1)S(1)}, bf16[384,256]{1,0:T(8,128)(2,1)S(1)}, u32[]{:S(2)}, u32[]{:S(2)}) collective-permute-start(bf16[384,256]{1,0:T(8,128)(2,1)S(1)} %slice.39.refs_0_), channel_id=1, source_target_pairs={{0,1},{1,2},{2,3},{3,4},{4,5},{5,6},{6,7},{7,0},{8,9},{9,10},{10,1... | collective-permute-start | bytes 589832 | tf_op jit(solution)/shard_map/ppermute | solution.py:130
  209.2 6.2 %collective-permute-start.28 = (bf16[384,256]{1,0:T(8,128)(2,1)S(1)}, bf16[384,256]{1,0:T(8,128)(2,1)S(1)}, u32[]{:S(2)}, u32[]{:S(2)}) collective-permute-start(bf16[384,256]{1,0:T(8,128)(2,1)S(1)} %collective-permute-done.27.refs_7_), channel_id=1, source_target_pairs={{0,7},{1,0},{2,1},{3,2},{4,3},{5,4},{6,5},{7,6},{8,15},{9,8},{10,9... | collective-permute-start | bytes 589832 | tf_op jit(solution)/shard_map/ppermute | solution.py:130
  212.2 6.9 %collective-permute-start.25 = (bf16[384,256]{1,0:T(8,128)(2,1)S(1)}, bf16[384,256]{1,0:T(8,128)(2,1)S(1)}, u32[]{:S(2)}, u32[]{:S(2)}) collective-permute-start(bf16[384,256]{1,0:T(8,128)(2,1)S(1)} %collective-permute-done.24.refs_1_), channel_id=1, source_target_pairs={{0,1},{1,2},{2,3},{3,4},{4,5},{5,6},{6,7},{7,0},{8,9},{9,10},{10,1... | collective-permute-start | bytes 589832 | tf_op jit(solution)/shard_map/ppermute | solution.py:130
  215.4 7.6 %collective-permute-start.29 = (bf16[384,256]{1,0:T(8,128)(2,1)S(1)}, bf16[384,256]{1,0:T(8,128)(2,1)S(1)}, u32[]{:S(2)}, u32[]{:S(2)}) collective-permute-start(bf16[384,256]{1,0:T(8,128)(2,1)S(1)} %collective-permute-done.28.refs_6_), channel_id=1, source_target_pairs={{0,7},{1,0},{2,1},{3,2},{4,3},{5,4},{6,5},{7,6},{8,15},{9,8},{10,9... | collective-permute-start | bytes 589832 | tf_op jit(solution)/shard_map/ppermute | solution.py:130
  219.1 6.9 %collective-permute-start.26 = (bf16[384,256]{1,0:T(8,128)(2,1)S(1)}, bf16[384,256]{1,0:T(8,128)(2,1)S(1)}, u32[]{:S(2)}, u32[]{:S(2)}) collective-permute-start(bf16[384,256]{1,0:T(8,128)(2,1)S(1)} %collective-permute-done.25.refs_2_), channel_id=1, source_target_pairs={{0,1},{1,2},{2,3},{3,4},{4,5},{5,6},{6,7},{7,0},{8,9},{9,10},{10,1... | collective-permute-start | bytes 589832 | tf_op jit(solution)/shard_map/ppermute | solution.py:130
  226.0 7.0 %collective-permute-start.30 = (bf16[384,256]{1,0:T(8,128)(2,1)S(1)}, bf16[384,256]{1,0:T(8,128)(2,1)S(1)}, u32[]{:S(2)}, u32[]{:S(2)}) collective-permute-start(bf16[384,256]{1,0:T(8,128)(2,1)S(1)} %broadcast_select_fusion.1), channel_id=1, source_target_pairs={{0,1},{1,2},{2,3},{3,4},{4,5},{5,6},{6,7},{7,0},{128,135},{129,128... | collective-permute-start | bytes 589832 | tf_op jit(solution)/shard_map/ppermute | solution.py:133
  239.3 21.2 %all-to-all-start.3 = ((bf16[16,24,1024]{2,1,0:T(8,128)(2,1)}), bf16[16,24,1024]{2,1,0:T(8,128)(2,1)S(1)}, u32[]{:S(2)}, u32[]{:S(2)}) async-start(bf16[16,24,1024]{2,1,0:T(8,128)(2,1)} %bitcast.31), calls=%async_computation.3 | async-start | bytes 1572864 | tf_op jit(solution)/shard_map/all_to_all | solution.py:288
  261.7 11.6 %all-to-all-start.4 = ((bf16[8,4,896]{2,1,0:T(4,128)(2,1)}), bf16[8,4,896]{2,1,0:T(4,128)(2,1)S(1)}, u32[]{:S(2)}, u32[]{:S(2)}) async-start(bf16[8,4,896]{2,1,0:T(4,128)(2,1)} %reshape.387), calls=%async_computation.4 | async-start | bytes 114688 | tf_op jit(solution)/shard_map/all_to_all | solution.py:300

commit v2 on v1

--- a/solution.py
+++ b/solution.py
@@ -83,24 +83,22 @@
     actives, downs, downs2 = refs[:count], refs[count : 2 * count], refs[2 * count : 3 * count]
     facts_ref, out_ref = refs[3 * count :]
     cols = downs[0].shape[0]
-    step = 128
-    weights = [
-        jnp.concatenate([one[...], two[...]], axis=1) for one, two in zip(downs, downs2)
-    ]
-    for r in range(0, out_ref.shape[0], step):
-        total = 0.0
-        for k in range(count):
-            total += lax.dot_general(
-                actives[k][r : r + step],
-                weights[k],
-                (((1,), (1,)), ((), ())),
-                preferred_element_type=f32,
-            )
-        facts = facts_ref[r : r + step].astype(f32)
-        total *= facts[:, :1] + facts[:, 1:2]
-        out_ref[r : r + step, :cols] = total.astype(bf16)
-        rest = out_ref.shape[1] - cols
-        out_ref[r : r + step, cols:] = jnp.broadcast_to(facts[:, 2:3], (step, rest)).astype(bf16)
+    step = 256
+    active = jnp.concatenate([a[...] for a in actives], axis=1)
+    facts = facts_ref[...].astype(f32)
+    weight = facts[:, :1] + facts[:, 1:2]
+    for c in range(0, cols, step):
+        end = min(c + step, cols)
+        weights = [w[c:end] for pair in zip(downs, downs2) for w in pair]
+        total = lax.dot_general(
+            active,
+            jnp.concatenate(weights, axis=1),
+            (((1,), (1,)), ((), ())),
+            preferred_element_type=f32,
+        )
+        out_ref[:, c:end] = (total * weight).astype(bf16)
+    rest = out_ref.shape[1] - cols
+    out_ref[:, cols:] = jnp.broadcast_to(facts[:, 2:3], (facts.shape[0], rest)).astype(bf16)
 
 
 def down_sums(actives, downs, downs2, facts):
@@ -177,12 +175,13 @@
     ups = (w_up[0], swap(w_up[0]))
 
     slabs = w_down[0].reshape(n_head, piece, w_down.shape[2])
-    downs = []
-    for k in range(n_head):
-        slab = lax.dynamic_index_in_dim(slabs, lax.rem(z + k, n_head), 0, False)
-        if k > 0:
-            slab = lax.ppermute(slab, "head", [(i, (i + k) % n_head) for i in range(n_head)])
-        downs.append(slab)
+    slabs = [
+        lax.dynamic_index_in_dim(slabs, lax.rem(z + k, n_head), 0, False) for k in range(n_head)
+    ]
+    downs = slabs[:1] + [None] * (n_head - 1)
+
+    def shift(k):
+        downs[k] = lax.ppermute(slabs[k], "head", [(i, (i + k) % n_head) for i in range(n_head)])
 
     expert_ids = jnp.arange(EXPERTS, dtype=jnp.int32)
     chosen = routes[0][:, :, None] == expert_ids[None, None, :]
@@ -220,6 +219,12 @@
         axis=1,
     )
     got = lax.all_to_all(send, "dp", split_axis=0, concat_axis=0, tiled=True)
+    for k in (1, 7, 2, 6):
+        shift(k)
+    wave = lax.optimization_barrier((downs[1], downs[7], slabs[3], slabs[5], slabs[4]))
+    downs[1], downs[7], slabs[3], slabs[5], slabs[4] = wave
+    for k in (3, 5, 4):
+        shift(k)
     got, downs = lax.optimization_barrier((got, downs))
     res_piece = got[:, heads * reqs : heads * reqs + res_rows].reshape(n_dp * rows, cols)
     fact = got[:, heads * reqs + res_rows :, :rows]
@@ -234,6 +239,7 @@
     partial = lax.all_to_all(
         partial.reshape(n_head, n_dp * rows, cols), "head", split_axis=0, concat_axis=0, tiled=True
     )
+    partial, gates, ups = lax.optimization_barrier((partial, gates, ups))
     attended = jnp.sum(partial.astype(f32), axis=0).astype(bf16)
     hidden_piece = (res_piece.astype(f32) + attended.astype(f32)).astype(bf16)
 
@@ -245,7 +251,7 @@
         tiled=True,
     )
     downs2 = [swap(d) for d in downs]
-    hidden, gates, ups, downs2 = lax.optimization_barrier((hidden, gates, ups, downs2))
+    hidden, downs2 = lax.optimization_barrier((hidden, downs2))
     home = lax.dynamic_slice(hidden, (0, dp * rows, 0), (n_dp, rows, cols))
 
     def index(shape, axis):

time: 279 us -> 258 us (0.925); the launches traced: 274 us -> 257 us
  waiting for transfers between devices: 134 us -> 126 us
  starting transfers between devices: 76.5 us -> 68.9 us
    ppermute x6, waiting for transfers between devices: 12.7 us -> 21.4 us  [ring(): lax.ppermute(held[0], 'head', right)]
    all_to_all x1, starting transfers between devices: 11 us -> 4.84 us  [local(): back = lax.all_to_all(out, 'dp', split_axis=0, concat_axis=0, tiled=True)]
    ppermute x7, waiting for transfers between devices: 37.1 us -> 32 us  [shift(): lax.ppermute(slabs[k], 'head', [(i, (i + k) % n_head) for i in range(n_he...]
    all_to_all x1, waiting for transfers between devices: 11.8 us -> 6.74 us  [local(): lax.all_to_all(jnp.broadcast_to(hidden_piece[None], (n_dp,) + hidden_piec...]
    ppermute x6, starting transfers between devices: 6.27 us -> 2.3 us  [ring(): lax.ppermute(held[0], 'head', right)]
    ppermute x6, waiting for transfers between devices: 27.4 us -> 23.5 us  [ring(): lax.ppermute(held[-1], 'head', left)]
    ppermute x7, starting transfers between devices: 12.9 us -> 16.6 us  [shift(): lax.ppermute(slabs[k], 'head', [(i, (i + k) % n_head) for i in range(n_he...]
    ppermute x6, starting transfers between devices: 20.2 us -> 16.8 us  [ring(): lax.ppermute(held[-1], 'head', left)]
  transfers between devices with their start and end apart: 36 -> 36, of which waited for: 22 -> 29; matrix products, arithmetic and copies ran while one was open for 6% -> 7% of each run, Pallas kernels for 6% -> 6%
where the time goes in v2:
time: 258 us; the launch traced here: 257 us
  waiting for transfers between devices  126 us (49%)
  starting transfers between devices  68.9 us (27%)
  Pallas kernels  27.3 us (11%)
  matrix products  11.8 us (5%)
  local copies, waits for them, and re-layouts  11.7 us (5%)
  other arithmetic  11.5 us (4%)
    ppermute x7, waiting for transfers between devices, shift(): lax.ppermute(slabs[k], 'head', [(i, (i + k) % n_head) for i in range(n_he...  32 us
    ppermute x6, waiting for transfers between devices, ring(): lax.ppermute(held[-1], 'head', left)  23.5 us
    ppermute x6, waiting for transfers between devices, ring(): lax.ppermute(held[0], 'head', right)  21.4 us
    pallas_call x5, Pallas kernels, gate_up(): pl.pallas_call(functools.partial(gate_up_kernel, len(blocks)), out_shape=...  20.7 us
    ppermute x6, starting transfers between devices, ring(): lax.ppermute(held[-1], 'head', left)  16.8 us
    ppermute x7, starting transfers between devices, shift(): lax.ppermute(slabs[k], 'head', [(i, (i + k) % n_head) for i in range(n_he...  16.6 us
    ppermute x2, waiting for transfers between devices, ring(): got = (lax.ppermute(one, ('group', 'head'), both),)  13.1 us
    all_to_all x1, waiting for transfers between devices, local(): lax.all_to_all(partial.reshape(n_head, n_dp * rows, cols), 'head', split_...  10.4 us
  transfers between devices with their start and end apart: 36, of which 29 were waited for; matrix products, arithmetic and copies ran while one was open for 7% of the time, Pallas kernels for 6%

profile of v2, /device:TPU:8, one launch (start us, length us, event | category | flops | bytes accessed | tf_op | source)
XLA Modules:
  0.0 257.3 jit_solution(14700127155210919251)
XLA Ops:
  0.0 0.9 select_reduce_fusion
  1.7 0.9 reshape_squeeze.7
  2.9 6.1 %fusion.75 = (f32[32,8]{1,0:T(8,128)S(1)}, f32[32,8,192]{2,1,0:T(8,128)S(1)}) fusion(bf16[1,32,8,576]{3,2,1,0:T(8,128)(2,1)} %param.12, pred[32,192]{1,0:T(8,128)(4,1)S(1)} %iota_compare_fusion.4, bf16[1,32,192,576]{3,2,1,0:T(8,128)(2,1)} %param.13), kind=kOutput, calls=%fused_computation.154 | convolution fusion | flops 56819904 | bytes 7576576 | tf_op jit(solution)/shard_map/sub | solution.py:199
  8.9 3.7 %fusion.6 = bf16[32,8,512]{2,1,0:T(8,128)(2,1)S(1)} fusion(bf16[32,192,576]{2,1,0:T(8,128)(2,1)} %bitcast.87, f32[32,8,192]{2,1,0:T(8,128)S(1)} %get-tuple-element.92, f32[32,8]{1,0:T(8,128)S(1)} %get-tuple-element.91), kind=kOutput, calls=%fused_computation.9 | convolution fusion | flops 50561024 | bytes 6751232 | tf_op jit(solution)/shard_map/rhl,rlc->rhc/dot_general | solution.py:201
  13.2 1.1 fusion.11
  14.4 7.4 %all-to-all-start = ((bf16[16,272,128]{2,1,0:T(8,128)(2,1)}), bf16[16,272,128]{2,1,0:T(8,128)(2,1)}, u32[]{:S(2)}, u32[]{:S(2)}) async-start(bf16[16,272,128]{2,1,0:T(8,128)(2,1)} %fusion.11), calls=%async_computation | async-start | bytes 2228224 | tf_op jit(solution)/shard_map/all_to_all | solution.py:221
  21.8 1.8 dynamic-slice_bitcast_fusion
  23.6 5.9 %collective-permute-start.1 = (bf16[896,128]{1,0:T(8,128)(2,1)S(1)}, bf16[896,128]{1,0:T(8,128)(2,1)S(1)}, u32[]{:S(2)}, u32[]{:S(2)}) collective-permute-start(bf16[896,128]{1,0:T(8,128)(2,1)S(1)} %get-tuple-element.88), channel_id=1, source_target_pairs={{0,7},{1,0},{2,1},{3,2},{4,3},{5,4},{6,5},{7,6},{8,15},{9,8},{10,9... | collective-permute-start | bytes 688136 | tf_op jit(solution)/shard_map/ppermute | solution.py:184
  30.1 2.5 collective-permute-start.6
  32.5 3.7 %collective-permute-done.1.refs_15_ = bf16[896,128]{1,0:T(8,128)(2,1)S(1)} collective-permute-done((bf16[896,128]{1,0:T(8,128)(2,1)S(1)}, bf16[896,128]{1,0:T(8,128)(2,1)S(1)}, u32[]{:S(2)}, u32[]{:S(2)}) %collective-permute-start.1) | collective-permute-done | bytes 229408 | tf_op jit(solution)/shard_map/ppermute | solution.py:184
  36.3 5.7 %collective-permute-done.refs_9_ = bf16[896,128]{1,0:T(8,128)(2,1)} collective-permute-done((bf16[896,128]{1,0:T(8,128)(2,1)S(1)}, bf16[896,128]{1,0:T(8,128)(2,1)}, u32[]{:S(2)}, u32[]{:S(2)}) %collective-permute-start) | collective-permute-done | bytes 229408 | tf_op jit(solution)/shard_map/ppermute | solution.py:184
  42.0 1.8 collective-permute-done.6.refs_14_
  43.7 4.3 %collective-permute-start.4 = (bf16[896,128]{1,0:T(8,128)(2,1)S(1)}, bf16[896,128]{1,0:T(8,128)(2,1)}, u32[]{:S(2)}, u32[]{:S(2)}) collective-permute-start(bf16[896,128]{1,0:T(8,128)(2,1)S(1)} %get-tuple-element.46), channel_id=1, source_target_pairs={{0,4},{1,5},{2,6},{3,7},{4,0},{5,1},{6,2},{7,3},{8,12},{9,13},{10,... | collective-permute-start | bytes 688136 | tf_op jit(solution)/shard_map/ppermute | solution.py:184
  48.0 5.6 %collective-permute-done.2.refs_10_ = bf16[896,128]{1,0:T(8,128)(2,1)} collective-permute-done((bf16[896,128]{1,0:T(8,128)(2,1)S(1)}, bf16[896,128]{1,0:T(8,128)(2,1)}, u32[]{:S(2)}, u32[]{:S(2)}) %collective-permute-start.2) | collective-permute-done | bytes 229408 | tf_op jit(solution)/shard_map/ppermute | solution.py:184
  53.6 3.9 %collective-permute-start.5 = (bf16[896,128]{1,0:T(8,128)(2,1)S(1)}, bf16[896,128]{1,0:T(8,128)(2,1)}, u32[]{:S(2)}, u32[]{:S(2)}) collective-permute-start(bf16[896,128]{1,0:T(8,128)(2,1)S(1)} %get-tuple-element.47), channel_id=1, source_target_pairs={{0,5},{1,6},{2,7},{3,0},{4,1},{5,2},{6,3},{7,4},{8,13},{9,14},{10,... | collective-permute-start | bytes 688136 | tf_op jit(solution)/shard_map/ppermute | solution.py:184
  57.5 1.3 copy.62
  58.8 11.9 %collective-permute-done.3.refs_11_ = bf16[896,128]{1,0:T(8,128)(2,1)} collective-permute-done((bf16[896,128]{1,0:T(8,128)(2,1)S(1)}, bf16[896,128]{1,0:T(8,128)(2,1)}, u32[]{:S(2)}, u32[]{:S(2)}) %collective-permute-start.3) | collective-permute-done | bytes 229408 | tf_op jit(solution)/shard_map/ppermute | solution.py:184
  70.6 3.4 %collective-permute-done.5.refs_13_ = bf16[896,128]{1,0:T(8,128)(2,1)} collective-permute-done((bf16[896,128]{1,0:T(8,128)(2,1)S(1)}, bf16[896,128]{1,0:T(8,128)(2,1)}, u32[]{:S(2)}, u32[]{:S(2)}) %collective-permute-start.5) | collective-permute-done | bytes 229408 | tf_op jit(solution)/shard_map/ppermute | solution.py:184
  74.0 1.6 copy.48
  76.6 1.0 copy.51
  77.6 4.1 %all-to-all-start.1 = ((bf16[8,64,448]{2,1,0:T(8,128)(2,1)}), bf16[8,64,448]{2,1,0:T(8,128)(2,1)}, u32[]{:S(2)}, u32[]{:S(2)}) async-start(bf16[8,64,448]{2,1,0:T(8,128)(2,1)} %copy.51), calls=%async_computation.1 | async-start | bytes 1048576 | tf_op jit(solution)/shard_map/all_to_all | solution.py:239
  82.5 1.5 slice_convert_fusion
  84.0 1.0 reshape.388
  85.9 10.4 %all-to-all-done.1 = bf16[8,64,448]{2,1,0:T(8,128)(2,1)} async-done(((bf16[8,64,448]{2,1,0:T(8,128)(2,1)}), bf16[8,64,448]{2,1,0:T(8,128)(2,1)}, u32[]{:S(2)}, u32[]{:S(2)}) %all-to-all-start.1) | async-done | bytes 458784 | tf_op jit(solution)/shard_map/all_to_all | solution.py:239
  96.3 1.8 reduce_sum.22
  98.1 0.9 add_convert_fusion
  98.9 1.2 broadcast_in_dim.55
  100.1 7.2 %all-to-all-start.2 = ((bf16[16,64,448]{2,1,0:T(8,128)(2,1)}), bf16[16,64,448]{2,1,0:T(8,128)(2,1)}, u32[]{:S(2)}, u32[]{:S(2)}) async-start(bf16[16,64,448]{2,1,0:T(8,128)(2,1)} %broadcast_in_dim.55), calls=%async_computation.2 | async-start | bytes 2097152 | tf_op jit(solution)/shard_map/all_to_all | solution.py:246
  107.3 0.8 slice_bitcast_fusion
  108.1 0.8 compare_reduce_fusion
  112.2 6.7 %all-to-all-done.2.hidden_ref = bf16[16,64,448]{2,1,0:T(8,128)(2,1)} async-done(((bf16[16,64,448]{2,1,0:T(8,128)(2,1)}), bf16[16,64,448]{2,1,0:T(8,128)(2,1)}, u32[]{:S(2)}, u32[]{:S(2)}) %all-to-all-start.2) | async-done | bytes 917536 | tf_op jit(solution)/shard_map/all_to_all | solution.py:246
  118.9 2.0 shard_map.118.refs_0_
  120.9 0.8 collective-permute-start.18
  121.7 1.3 collective-permute-start.17
  123.0 4.0 %shard_map.119 = bf16[48,384]{1,0:T(8,128)(2,1)S(1)} custom-call(bf16[48,7296]{1,0:T(8,128)(2,1)S(1)} %shard_map.118.refs_0_, bf16[7168,128]{1,0:T(8,128)(2,1)S(1)} %bitcast.82, bf16[7168,128]{1,0:T(8,128)(2,1)} %collective-permute-done.7.refs_2_.refs_3_, bf16[7168,128]{1,0:T(8,128)(2,1)} %bitcast.26.refs_3_.refs_4_, ...), custom_call_target="tpu_custom_call" | custom-call | flops 352321536 | bytes 7340032 | tf_op jit(solution)/shard_map/pallas_call | solution.py:70
  127.0 8.6 %collective-permute-done.18.refs_1_ = bf16[48,7296]{1,0:T(8,128)(2,1)S(1)} collective-permute-done((bf16[48,7296]{1,0:T(8,128)(2,1)S(1)}, bf16[48,7296]{1,0:T(8,128)(2,1)S(1)}, u32[]{:S(2)}, u32[]{:S(2)}) %collective-permute-start.18) | collective-permute-done | bytes 700448 | tf_op jit(solution)/shard_map/ppermute | solution.py:128
  135.6 2.3 collective-permute-done.17.refs_0_
  137.9 1.0 collective-permute-start.19
  138.9 2.3 collective-permute-start.20
  141.1 3.9 %shard_map.120 = bf16[96,384]{1,0:T(8,128)(2,1)S(1)} custom-call(bf16[48,7296]{1,0:T(8,128)(2,1)S(1)} %collective-permute-done.17.refs_0_, bf16[48,7296]{1,0:T(8,128)(2,1)S(1)} %collective-permute-done.18.refs_1_, bf16[7168,128]{1,0:T(8,128)(2,1)S(1)} %bitcast.83, bf16[7168,128]{1,0:T(8,128)(2,1)} %collective-permute-done.7.refs_2_.refs_3_, ...), custom_call_target="tpu_custom_call" | custom-call | flops 704643072 | bytes 7340032 | tf_op jit(solution)/shard_map/pallas_call | solution.py:70
  145.1 9.9 %collective-permute-done.19.refs_0_ = bf16[48,7296]{1,0:T(8,128)(2,1)} collective-permute-done((bf16[48,7296]{1,0:T(8,128)(2,1)S(1)}, bf16[48,7296]{1,0:T(8,128)(2,1)}, u32[]{:S(2)}, u32[]{:S(2)}) %collective-permute-start.19) | collective-permute-done | bytes 700448 | tf_op jit(solution)/shard_map/ppermute | solution.py:128
  155.7 3.2 %collective-permute-start.22 = (bf16[48,7296]{1,0:T(8,128)(2,1)}, bf16[48,7296]{1,0:T(8,128)(2,1)}, u32[]{:S(2)}, u32[]{:S(2)}) collective-permute-start(bf16[48,7296]{1,0:T(8,128)(2,1)} %collective-permute-done.20.refs_1_), channel_id=1, source_target_pairs={{0,7},{1,0},{2,1},{3,2},{4,3},{5,4},{6,5},{7,6},{8,15},{9,8},{10,9... | collective-permute-start | bytes 2101256 | tf_op jit(solution)/shard_map/ppermute | solution.py:128
  158.9 4.4 %shard_map.121 = bf16[96,384]{1,0:T(8,128)(2,1)S(1)} custom-call(bf16[48,7296]{1,0:T(8,128)(2,1)} %collective-permute-done.19.refs_0_, bf16[48,7296]{1,0:T(8,128)(2,1)} %collective-permute-done.20.refs_1_, bf16[7168,128]{1,0:T(8,128)(2,1)S(1)} %bitcast.84, bf16[7168,128]{1,0:T(8,128)(2,1)} %collective-permute-done.7.refs_2_.refs_3_, ...), custom_call_target="tpu_custom_call" | custom-call | flops 704643072 | bytes 7340032 | tf_op jit(solution)/shard_map/pallas_call | solution.py:70
  163.3 5.0 %collective-permute-done.21.refs_0_ = bf16[48,7296]{1,0:T(8,128)(2,1)} collective-permute-done((bf16[48,7296]{1,0:T(8,128)(2,1)}, bf16[48,7296]{1,0:T(8,128)(2,1)}, u32[]{:S(2)}, u32[]{:S(2)}) %collective-permute-start.21) | collective-permute-done | bytes 700448 | tf_op jit(solution)/shard_map/ppermute | solution.py:128
  168.3 5.0 %collective-permute-done.22.refs_1_ = bf16[48,7296]{1,0:T(8,128)(2,1)} collective-permute-done((bf16[48,7296]{1,0:T(8,128)(2,1)}, bf16[48,7296]{1,0:T(8,128)(2,1)}, u32[]{:S(2)}, u32[]{:S(2)}) %collective-permute-start.22) | collective-permute-done | bytes 700448 | tf_op jit(solution)/shard_map/ppermute | solution.py:128
  173.3 1.2 broadcast_select_fusion
  174.5 3.2 %collective-permute-start.23 = (bf16[48,7296]{1,0:T(8,128)(2,1)S(1)}, bf16[48,7296]{1,0:T(8,128)(2,1)S(1)}, u32[]{:S(2)}, u32[]{:S(2)}) collective-permute-start(bf16[48,7296]{1,0:T(8,128)(2,1)S(1)} %broadcast_select_fusion), channel_id=1, source_target_pairs={{0,1},{1,2},{2,3},{3,4},{4,5},{5,6},{6,7},{7,0},{128,135},{129,128... | collective-permute-start | bytes 2101256 | tf_op jit(solution)/shard_map/ppermute | solution.py:131
  177.7 4.4 %shard_map.122 = bf16[96,384]{1,0:T(8,128)(2,1)S(1)} custom-call(bf16[48,7296]{1,0:T(8,128)(2,1)} %collective-permute-done.21.refs_0_, bf16[48,7296]{1,0:T(8,128)(2,1)} %collective-permute-done.22.refs_1_, bf16[7168,128]{1,0:T(8,128)(2,1)S(1)} %bitcast.85, bf16[7168,128]{1,0:T(8,128)(2,1)} %collective-permute-done.7.refs_2_.refs_3_, ...), custom_call_target="tpu_custom_call" | custom-call | flops 704643072 | bytes 7340032 | tf_op jit(solution)/shard_map/pallas_call | solution.py:70
  182.1 6.2 %collective-permute-done.23.refs_0_ = bf16[48,7296]{1,0:T(8,128)(2,1)S(1)} collective-permute-done((bf16[48,7296]{1,0:T(8,128)(2,1)S(1)}, bf16[48,7296]{1,0:T(8,128)(2,1)S(1)}, u32[]{:S(2)}, u32[]{:S(2)}) %collective-permute-start.23) | collective-permute-done | bytes 700448 | tf_op jit(solution)/shard_map/ppermute | solution.py:131
  188.3 4.0 %shard_map.123 = bf16[48,384]{1,0:T(8,128)(2,1)S(1)} custom-call(bf16[48,7296]{1,0:T(8,128)(2,1)S(1)} %collective-permute-done.23.refs_0_, bf16[7168,128]{1,0:T(8,128)(2,1)S(1)} %bitcast.86, bf16[7168,128]{1,0:T(8,128)(2,1)} %collective-permute-done.7.refs_2_.refs_3_, bf16[7168,128]{1,0:T(8,128)(2,1)} %bitcast.26.refs_3_.refs_4_, ...), custom_call_target="tpu_custom_call" | custom-call | flops 352321536 | bytes 7340032 | tf_op jit(solution)/shard_map/pallas_call | solution.py:70
  192.8 3.1 %collective-permute-start.27 = (bf16[384,256]{1,0:T(8,128)(2,1)S(1)}, bf16[384,256]{1,0:T(8,128)(2,1)S(1)}, u32[]{:S(2)}, u32[]{:S(2)}) collective-permute-start(bf16[384,256]{1,0:T(8,128)(2,1)S(1)} %slice.39.refs_0_), channel_id=1, source_target_pairs={{0,7},{1,0},{2,1},{3,2},{4,3},{5,4},{6,5},{7,6},{8,15},{9,8},{10,9... | collective-permute-start | bytes 589832 | tf_op jit(solution)/shard_map/ppermute | solution.py:128
  195.9 3.2 %collective-permute-done.27.refs_7_ = bf16[384,256]{1,0:T(8,128)(2,1)S(1)} collective-permute-done((bf16[384,256]{1,0:T(8,128)(2,1)S(1)}, bf16[384,256]{1,0:T(8,128)(2,1)S(1)}, u32[]{:S(2)}, u32[]{:S(2)}) %collective-permute-start.27) | collective-permute-done | bytes 196640 | tf_op jit(solution)/shard_map/ppermute | solution.py:128
  199.1 3.7 %collective-permute-start.28 = (bf16[384,256]{1,0:T(8,128)(2,1)S(1)}, bf16[384,256]{1,0:T(8,128)(2,1)S(1)}, u32[]{:S(2)}, u32[]{:S(2)}) collective-permute-start(bf16[384,256]{1,0:T(8,128)(2,1)S(1)} %collective-permute-done.27.refs_7_), channel_id=1, source_target_pairs={{0,7},{1,0},{2,1},{3,2},{4,3},{5,4},{6,5},{7,6},{8,15},{9,8},{10,9... | collective-permute-start | bytes 589832 | tf_op jit(solution)/shard_map/ppermute | solution.py:128
  203.0 3.0 %collective-permute-done.28.refs_6_ = bf16[384,256]{1,0:T(8,128)(2,1)S(1)} collective-permute-done((bf16[384,256]{1,0:T(8,128)(2,1)S(1)}, bf16[384,256]{1,0:T(8,128)(2,1)S(1)}, u32[]{:S(2)}, u32[]{:S(2)}) %collective-permute-start.28) | collective-permute-done | bytes 196640 | tf_op jit(solution)/shard_map/ppermute | solution.py:128
  206.0 3.7 %collective-permute-start.29 = (bf16[384,256]{1,0:T(8,128)(2,1)S(1)}, bf16[384,256]{1,0:T(8,128)(2,1)S(1)}, u32[]{:S(2)}, u32[]{:S(2)}) collective-permute-start(bf16[384,256]{1,0:T(8,128)(2,1)S(1)} %collective-permute-done.28.refs_6_), channel_id=1, source_target_pairs={{0,7},{1,0},{2,1},{3,2},{4,3},{5,4},{6,5},{7,6},{8,15},{9,8},{10,9... | collective-permute-start | bytes 589832 | tf_op jit(solution)/shard_map/ppermute | solution.py:128
  209.9 3.0 %collective-permute-done.29.refs_5_ = bf16[384,256]{1,0:T(8,128)(2,1)S(1)} collective-permute-done((bf16[384,256]{1,0:T(8,128)(2,1)S(1)}, bf16[384,256]{1,0:T(8,128)(2,1)S(1)}, u32[]{:S(2)}, u32[]{:S(2)}) %collective-permute-start.29) | collective-permute-done | bytes 196640 | tf_op jit(solution)/shard_map/ppermute | solution.py:128
  212.9 3.9 %collective-permute-done.26.refs_3_ = bf16[384,256]{1,0:T(8,128)(2,1)S(1)} collective-permute-done((bf16[384,256]{1,0:T(8,128)(2,1)S(1)}, bf16[384,256]{1,0:T(8,128)(2,1)S(1)}, u32[]{:S(2)}, u32[]{:S(2)}) %collective-permute-start.26) | collective-permute-done | bytes 196640 | tf_op jit(solution)/shard_map/ppermute | solution.py:128
  216.9 6.9 %collective-permute-done.30.refs_4_ = bf16[384,256]{1,0:T(8,128)(2,1)S(1)} collective-permute-done((bf16[384,256]{1,0:T(8,128)(2,1)S(1)}, bf16[384,256]{1,0:T(8,128)(2,1)S(1)}, u32[]{:S(2)}, u32[]{:S(2)}) %collective-permute-start.30) | collective-permute-done | bytes 196640 | tf_op jit(solution)/shard_map/ppermute | solution.py:131
  223.7 4.7 %shard_map.124 = bf16[384,1024]{1,0:T(8,128)(2,1)} custom-call(bf16[384,256]{1,0:T(8,128)(2,1)S(1)} %slice.39.refs_0_, bf16[384,256]{1,0:T(8,128)(2,1)S(1)} %collective-permute-done.24.refs_1_, bf16[384,256]{1,0:T(8,128)(2,1)S(1)} %collective-permute-done.25.refs_2_, bf16[384,256]{1,0:T(8,128)(2,1)S(1)} %collective-permute-done.26.refs_3_, ...), custom_call_target="tpu_custom_call" | custom-call | tf_op jit(solution)/shard_map/pallas_call | solution.py:106
  228.4 4.8 %all-to-all-start.3 = ((bf16[16,24,1024]{2,1,0:T(8,128)(2,1)}), bf16[16,24,1024]{2,1,0:T(8,128)(2,1)S(1)}, u32[]{:S(2)}, u32[]{:S(2)}) async-start(bf16[16,24,1024]{2,1,0:T(8,128)(2,1)} %bitcast.31), calls=%async_computation.3 | async-start | bytes 1572864 | tf_op jit(solution)/shard_map/all_to_all | solution.py:294
  233.3 10.2 %all-to-all-done.3 = bf16[16,24,1024]{2,1,0:T(8,128)(2,1)S(1)} async-done(((bf16[16,24,1024]{2,1,0:T(8,128)(2,1)}), bf16[16,24,1024]{2,1,0:T(8,128)(2,1)S(1)}, u32[]{:S(2)}, u32[]{:S(2)}) %all-to-all-start.3) | async-done | bytes 786464 | tf_op jit(solution)/shard_map/all_to_all | solution.py:294
  244.7 3.7 %all-to-all-start.4 = ((bf16[8,4,896]{2,1,0:T(4,128)(2,1)}), bf16[8,4,896]{2,1,0:T(4,128)(2,1)S(1)}, u32[]{:S(2)}, u32[]{:S(2)}) async-start(bf16[8,4,896]{2,1,0:T(4,128)(2,1)} %reshape.387), calls=%async_computation.4 | async-start | bytes 114688 | tf_op jit(solution)/shard_map/all_to_all | solution.py:306
  248.3 0.9 convert_bitcast_fusion
  249.5 7.2 %all-to-all-done.4 = bf16[8,4,896]{2,1,0:T(4,128)(2,1)S(1)} async-done(((bf16[8,4,896]{2,1,0:T(4,128)(2,1)}), bf16[8,4,896]{2,1,0:T(4,128)(2,1)S(1)}, u32[]{:S(2)}, u32[]{:S(2)}) %all-to-all-start.4) | async-done | bytes 57376 | tf_op jit(solution)/shard_map/all_to_all | solution.py:306
  (91 shorter events, 11.6 us)
Async XLA Ops:
  0.0 12.7 %copy-start = (bf16[8,512,128]{2,1,0:T(8,128)(2,1)S(1)}, bf16[8,512,128]{2,1,0:T(8,128)(2,1)}, u32[]{:S(2)}) copy-start(bf16[8,512,128]{2,1,0:T(8,128)(2,1)} %param.15) | copy-start | bytes 3145732
  14.4 59.6 %all-to-all-start = ((bf16[16,272,128]{2,1,0:T(8,128)(2,1)}), bf16[16,272,128]{2,1,0:T(8,128)(2,1)}, u32[]{:S(2)}, u32[]{:S(2)}) async-start(bf16[16,272,128]{2,1,0:T(8,128)(2,1)} %fusion.11), calls=%async_computation | async-start | bytes 2228224 | tf_op jit(solution)/shard_map/all_to_all | solution.py:221
  21.7 7.8 %copy-start.1 = (bf16[1,7168,128]{2,1,0:T(8,128)(2,1)S(1)}, bf16[1,7168,128]{2,1,0:T(8,128)(2,1)}, u32[]{:S(2)}) copy-start(bf16[1,7168,128]{2,1,0:T(8,128)(2,1)} %param.21) | copy-start | bytes 5505028
  21.8 35.7 %copy-start.2 = (bf16[1024,448]{0,1:T(8,128)(2,1)S(1)}, bf16[1024,448]{0,1:T(8,128)(2,1)}, u32[]{:S(2)}) copy-start(bf16[1024,448]{0,1:T(8,128)(2,1)} %param.16) | copy-start | bytes 2752516
  23.6 12.7 %collective-permute-start.1 = (bf16[896,128]{1,0:T(8,128)(2,1)S(1)}, bf16[896,128]{1,0:T(8,128)(2,1)S(1)}, u32[]{:S(2)}, u32[]{:S(2)}) collective-permute-start(bf16[896,128]{1,0:T(8,128)(2,1)S(1)} %get-tuple-element.88), channel_id=1, source_target_pairs={{0,7},{1,0},{2,1},{3,2},{4,3},{5,4},{6,5},{7,6},{8,15},{9,8},{10,9... | collective-permute-start | bytes 688136 | tf_op jit(solution)/shard_map/ppermute | solution.py:184
  29.5 56.4 %collective-permute-start.7 = (bf16[7168,128]{1,0:T(8,128)(2,1)S(1)}, bf16[7168,128]{1,0:T(8,128)(2,1)}, u32[]{:S(2)}, u32[]{:S(2)}) collective-permute-start(bf16[7168,128]{1,0:T(8,128)(2,1)S(1)} %bitcast.81), channel_id=1, source_target_pairs={{0,128},{128,0},{1,129},{129,1},{2,130},{130,2},{3,131},{131,3},{4... | collective-permute-start | bytes 5505032 | tf_op jit(solution)/shard_map/ppermute | solution.py:172
  29.5 56.4 %collective-permute-start.8 = (bf16[7168,128]{1,0:T(8,128)(2,1)}, bf16[7168,128]{1,0:T(8,128)(2,1)}, u32[]{:S(2)}, u32[]{:S(2)}) collective-permute-start(bf16[7168,128]{1,0:T(8,128)(2,1)} %bitcast.26.refs_3_.refs_4_), channel_id=1, source_target_pairs={{0,128},{128,0},{1,129},{129,1},{2,130},{130,2},{3,131},{131,3},{4... | collective-permute-start | bytes 5505032 | tf_op jit(solution)/shard_map/ppermute | solution.py:172
  30.1 11.9 %collective-permute-start = (bf16[896,128]{1,0:T(8,128)(2,1)S(1)}, bf16[896,128]{1,0:T(8,128)(2,1)}, u32[]{:S(2)}, u32[]{:S(2)}) collective-permute-start(bf16[896,128]{1,0:T(8,128)(2,1)S(1)} %get-tuple-element.89), channel_id=1, source_target_pairs={{0,1},{1,2},{2,3},{3,4},{4,5},{5,6},{6,7},{7,0},{8,9},{9,10},{10,1... | collective-permute-start | bytes 688136 | tf_op jit(solution)/shard_map/ppermute | solution.py:184
  30.1 13.6 %collective-permute-start.6 = (bf16[896,128]{1,0:T(8,128)(2,1)S(1)}, bf16[896,128]{1,0:T(8,128)(2,1)}, u32[]{:S(2)}, u32[]{:S(2)}) collective-permute-start(bf16[896,128]{1,0:T(8,128)(2,1)S(1)} %get-tuple-element.83), channel_id=1, source_target_pairs={{0,6},{1,7},{2,0},{3,1},{4,2},{5,3},{6,4},{7,5},{8,14},{9,15},{10,... | collective-permute-start | bytes 688136 | tf_op jit(solution)/shard_map/ppermute | solution.py:184
  36.3 17.3 %collective-permute-start.2 = (bf16[896,128]{1,0:T(8,128)(2,1)S(1)}, bf16[896,128]{1,0:T(8,128)(2,1)}, u32[]{:S(2)}, u32[]{:S(2)}) collective-permute-start(bf16[896,128]{1,0:T(8,128)(2,1)S(1)} %get-tuple-element.84), channel_id=1, source_target_pairs={{0,2},{1,3},{2,4},{3,5},{4,6},{5,7},{6,0},{7,1},{8,10},{9,11},{10,... | collective-permute-start | bytes 688136 | tf_op jit(solution)/shard_map/ppermute | solution.py:184
  41.9 28.7 %collective-permute-start.3 = (bf16[896,128]{1,0:T(8,128)(2,1)S(1)}, bf16[896,128]{1,0:T(8,128)(2,1)}, u32[]{:S(2)}, u32[]{:S(2)}) collective-permute-start(bf16[896,128]{1,0:T(8,128)(2,1)S(1)} %get-tuple-element.45), channel_id=1, source_target_pairs={{0,3},{1,4},{2,5},{3,6},{4,7},{5,0},{6,1},{7,2},{8,11},{9,12},{10,... | collective-permute-start | bytes 688136 | tf_op jit(solution)/shard_map/ppermute | solution.py:184
  43.7 26.9 %collective-permute-start.4 = (bf16[896,128]{1,0:T(8,128)(2,1)S(1)}, bf16[896,128]{1,0:T(8,128)(2,1)}, u32[]{:S(2)}, u32[]{:S(2)}) collective-permute-start(bf16[896,128]{1,0:T(8,128)(2,1)S(1)} %get-tuple-element.46), channel_id=1, source_target_pairs={{0,4},{1,5},{2,6},{3,7},{4,0},{5,1},{6,2},{7,3},{8,12},{9,13},{10,... | collective-permute-start | bytes 688136 | tf_op jit(solution)/shard_map/ppermute | solution.py:184
  53.6 20.4 %collective-permute-start.5 = (bf16[896,128]{1,0:T(8,128)(2,1)S(1)}, bf16[896,128]{1,0:T(8,128)(2,1)}, u32[]{:S(2)}, u32[]{:S(2)}) collective-permute-start(bf16[896,128]{1,0:T(8,128)(2,1)S(1)} %get-tuple-element.47), channel_id=1, source_target_pairs={{0,5},{1,6},{2,7},{3,0},{4,1},{5,2},{6,3},{7,4},{8,13},{9,14},{10,... | collective-permute-start | bytes 688136 | tf_op jit(solution)/shard_map/ppermute | solution.py:184
  74.0 1.8 copy-start.3
  76.6 5.2 %copy-start.4 = (f32[7168]{0:T(1024)S(1)}, f32[7168]{0:T(1024)}, u32[]{:S(2)}) copy-start(f32[7168]{0:T(1024)} %param.18) | copy-start | bytes 86020
  77.6 18.7 %all-to-all-start.1 = ((bf16[8,64,448]{2,1,0:T(8,128)(2,1)}), bf16[8,64,448]{2,1,0:T(8,128)(2,1)}, u32[]{:S(2)}, u32[]{:S(2)}) async-start(bf16[8,64,448]{2,1,0:T(8,128)(2,1)} %copy.51), calls=%async_computation.1 | async-start | bytes 1048576 | tf_op jit(solution)/shard_map/all_to_all | solution.py:239
  85.0 24.8 %collective-permute-start.9 = (bf16[896,128]{1,0:T(8,128)(2,1)S(1)}, bf16[896,128]{1,0:T(8,128)(2,1)}, u32[]{:S(2)}, u32[]{:S(2)}) collective-permute-start(bf16[896,128]{1,0:T(8,128)(2,1)S(1)} %get-tuple-element.51.refs_8_), channel_id=1, source_target_pairs={{0,128},{128,0},{1,129},{129,1},{2,130},{130,2},{3,131},{131,3},{4... | collective-permute-start | bytes 688136 | tf_op jit(solution)/shard_map/ppermute | solution.py:172
  85.1 24.9 %collective-permute-start.10 = (bf16[896,128]{1,0:T(8,128)(2,1)}, bf16[896,128]{1,0:T(8,128)(2,1)}, u32[]{:S(2)}, u32[]{:S(2)}) collective-permute-start(bf16[896,128]{1,0:T(8,128)(2,1)} %collective-permute-done.refs_9_), channel_id=1, source_target_pairs={{0,128},{128,0},{1,129},{129,1},{2,130},{130,2},{3,131},{131,3},{4... | collective-permute-start | bytes 688136 | tf_op jit(solution)/shard_map/ppermute | solution.py:172
  85.6 24.8 %collective-permute-start.11 = (bf16[896,128]{1,0:T(8,128)(2,1)}, bf16[896,128]{1,0:T(8,128)(2,1)}, u32[]{:S(2)}, u32[]{:S(2)}) collective-permute-start(bf16[896,128]{1,0:T(8,128)(2,1)} %collective-permute-done.2.refs_10_), channel_id=1, source_target_pairs={{0,128},{128,0},{1,129},{129,1},{2,130},{130,2},{3,131},{131,3},{4... | collective-permute-start | bytes 688136 | tf_op jit(solution)/shard_map/ppermute | solution.py:172
  98.9 11.9 %copy-start.5 = (pred[48]{0:T(512)(128)(4,1)S(1)}, pred[48]{0:T(512)(128)(4,1)}, u32[]{:S(2)}) copy-start(pred[48]{0:T(512)(128)(4,1)} %get-tuple-element.93) | copy-start | bytes 148
  98.9 11.9 %copy-start.6 = (pred[48]{0:T(512)(128)(4,1)S(1)}, pred[48]{0:T(512)(128)(4,1)}, u32[]{:S(2)}) copy-start(pred[48]{0:T(512)(128)(4,1)} %get-tuple-element.94) | copy-start | bytes 148
  100.1 18.8 %all-to-all-start.2 = ((bf16[16,64,448]{2,1,0:T(8,128)(2,1)}), bf16[16,64,448]{2,1,0:T(8,128)(2,1)}, u32[]{:S(2)}, u32[]{:S(2)}) async-start(bf16[16,64,448]{2,1,0:T(8,128)(2,1)} %broadcast_in_dim.55), calls=%async_computation.2 | async-start | bytes 2097152 | tf_op jit(solution)/shard_map/all_to_all | solution.py:246
  109.2 1.9 collective-permute-start.12
  109.2 2.1 collective-permute-start.13
  109.8 1.9 collective-permute-start.14
  110.0 2.1 collective-permute-start.15
  110.4 1.8 collective-permute-start.16
  120.9 14.8 %collective-permute-start.18 = (bf16[48,7296]{1,0:T(8,128)(2,1)S(1)}, bf16[48,7296]{1,0:T(8,128)(2,1)S(1)}, u32[]{:S(2)}, u32[]{:S(2)}) collective-permute-start(bf16[48,7296]{1,0:T(8,128)(2,1)S(1)} %shard_map.118.refs_0_), channel_id=1, source_target_pairs={{0,7},{1,0},{2,1},{3,2},{4,3},{5,4},{6,5},{7,6},{8,15},{9,8},{10,9... | collective-permute-start | bytes 2101256 | tf_op jit(solution)/shard_map/ppermute | solution.py:128
  121.7 16.2 %collective-permute-start.17 = (bf16[48,7296]{1,0:T(8,128)(2,1)S(1)}, bf16[48,7296]{1,0:T(8,128)(2,1)S(1)}, u32[]{:S(2)}, u32[]{:S(2)}) collective-permute-start(bf16[48,7296]{1,0:T(8,128)(2,1)S(1)} %shard_map.118.refs_0_), channel_id=1, source_target_pairs={{0,1},{1,2},{2,3},{3,4},{4,5},{5,6},{6,7},{7,0},{8,9},{9,10},{10,1... | collective-permute-start | bytes 2101256 | tf_op jit(solution)/shard_map/ppermute | solution.py:128
  137.9 17.1 %collective-permute-start.19 = (bf16[48,7296]{1,0:T(8,128)(2,1)S(1)}, bf16[48,7296]{1,0:T(8,128)(2,1)}, u32[]{:S(2)}, u32[]{:S(2)}) collective-permute-start(bf16[48,7296]{1,0:T(8,128)(2,1)S(1)} %collective-permute-done.17.refs_0_), channel_id=1, source_target_pairs={{0,1},{1,2},{2,3},{3,4},{4,5},{5,6},{6,7},{7,0},{8,9},{9,10},{10,1... | collective-permute-start | bytes 2101256 | tf_op jit(solution)/shard_map/ppermute | solution.py:128
  138.9 16.8 %collective-permute-start.20 = (bf16[48,7296]{1,0:T(8,128)(2,1)S(1)}, bf16[48,7296]{1,0:T(8,128)(2,1)}, u32[]{:S(2)}, u32[]{:S(2)}) collective-permute-start(bf16[48,7296]{1,0:T(8,128)(2,1)S(1)} %collective-permute-done.18.refs_1_), channel_id=1, source_target_pairs={{0,7},{1,0},{2,1},{3,2},{4,3},{5,4},{6,5},{7,6},{8,15},{9,8},{10,9... | collective-permute-start | bytes 2101256 | tf_op jit(solution)/shard_map/ppermute | solution.py:128
  155.7 12.6 %collective-permute-start.21 = (bf16[48,7296]{1,0:T(8,128)(2,1)}, bf16[48,7296]{1,0:T(8,128)(2,1)}, u32[]{:S(2)}, u32[]{:S(2)}) collective-permute-start(bf16[48,7296]{1,0:T(8,128)(2,1)} %collective-permute-done.19.refs_0_), channel_id=1, source_target_pairs={{0,1},{1,2},{2,3},{3,4},{4,5},{5,6},{6,7},{7,0},{8,9},{9,10},{10,1... | collective-permute-start | bytes 2101256 | tf_op jit(solution)/shard_map/ppermute | solution.py:128
  155.7 17.6 %collective-permute-start.22 = (bf16[48,7296]{1,0:T(8,128)(2,1)}, bf16[48,7296]{1,0:T(8,128)(2,1)}, u32[]{:S(2)}, u32[]{:S(2)}) collective-permute-start(bf16[48,7296]{1,0:T(8,128)(2,1)} %collective-permute-done.20.refs_1_), channel_id=1, source_target_pairs={{0,7},{1,0},{2,1},{3,2},{4,3},{5,4},{6,5},{7,6},{8,15},{9,8},{10,9... | collective-permute-start | bytes 2101256 | tf_op jit(solution)/shard_map/ppermute | solution.py:128
  174.5 13.9 %collective-permute-start.23 = (bf16[48,7296]{1,0:T(8,128)(2,1)S(1)}, bf16[48,7296]{1,0:T(8,128)(2,1)S(1)}, u32[]{:S(2)}, u32[]{:S(2)}) collective-permute-start(bf16[48,7296]{1,0:T(8,128)(2,1)S(1)} %broadcast_select_fusion), channel_id=1, source_target_pairs={{0,1},{1,2},{2,3},{3,4},{4,5},{5,6},{6,7},{7,0},{128,135},{129,128... | collective-permute-start | bytes 2101256 | tf_op jit(solution)/shard_map/ppermute | solution.py:131
  192.8 6.3 %collective-permute-start.27 = (bf16[384,256]{1,0:T(8,128)(2,1)S(1)}, bf16[384,256]{1,0:T(8,128)(2,1)S(1)}, u32[]{:S(2)}, u32[]{:S(2)}) collective-permute-start(bf16[384,256]{1,0:T(8,128)(2,1)S(1)} %slice.39.refs_0_), channel_id=1, source_target_pairs={{0,7},{1,0},{2,1},{3,2},{4,3},{5,4},{6,5},{7,6},{8,15},{9,8},{10,9... | collective-permute-start | bytes 589832 | tf_op jit(solution)/shard_map/ppermute | solution.py:128
  195.9 7.1 %collective-permute-start.24 = (bf16[384,256]{1,0:T(8,128)(2,1)S(1)}, bf16[384,256]{1,0:T(8,128)(2,1)S(1)}, u32[]{:S(2)}, u32[]{:S(2)}) collective-permute-start(bf16[384,256]{1,0:T(8,128)(2,1)S(1)} %slice.39.refs_0_), channel_id=1, source_target_pairs={{0,1},{1,2},{2,3},{3,4},{4,5},{5,6},{6,7},{7,0},{8,9},{9,10},{10,1... | collective-permute-start | bytes 589832 | tf_op jit(solution)/shard_map/ppermute | solution.py:128
  199.1 6.9 %collective-permute-start.28 = (bf16[384,256]{1,0:T(8,128)(2,1)S(1)}, bf16[384,256]{1,0:T(8,128)(2,1)S(1)}, u32[]{:S(2)}, u32[]{:S(2)}) collective-permute-start(bf16[384,256]{1,0:T(8,128)(2,1)S(1)} %collective-permute-done.27.refs_7_), channel_id=1, source_target_pairs={{0,7},{1,0},{2,1},{3,2},{4,3},{5,4},{6,5},{7,6},{8,15},{9,8},{10,9... | collective-permute-start | bytes 589832 | tf_op jit(solution)/shard_map/ppermute | solution.py:128
  203.0 6.9 %collective-permute-start.25 = (bf16[384,256]{1,0:T(8,128)(2,1)S(1)}, bf16[384,256]{1,0:T(8,128)(2,1)S(1)}, u32[]{:S(2)}, u32[]{:S(2)}) collective-permute-start(bf16[384,256]{1,0:T(8,128)(2,1)S(1)} %collective-permute-done.24.refs_1_), channel_id=1, source_target_pairs={{0,1},{1,2},{2,3},{3,4},{4,5},{5,6},{6,7},{7,0},{8,9},{9,10},{10,1... | collective-permute-start | bytes 589832 | tf_op jit(solution)/shard_map/ppermute | solution.py:128
  206.0 6.9 %collective-permute-start.29 = (bf16[384,256]{1,0:T(8,128)(2,1)S(1)}, bf16[384,256]{1,0:T(8,128)(2,1)S(1)}, u32[]{:S(2)}, u32[]{:S(2)}) collective-permute-start(bf16[384,256]{1,0:T(8,128)(2,1)S(1)} %collective-permute-done.28.refs_6_), channel_id=1, source_target_pairs={{0,7},{1,0},{2,1},{3,2},{4,3},{5,4},{6,5},{7,6},{8,15},{9,8},{10,9... | collective-permute-start | bytes 589832 | tf_op jit(solution)/shard_map/ppermute | solution.py:128
  209.9 6.9 %collective-permute-start.26 = (bf16[384,256]{1,0:T(8,128)(2,1)S(1)}, bf16[384,256]{1,0:T(8,128)(2,1)S(1)}, u32[]{:S(2)}, u32[]{:S(2)}) collective-permute-start(bf16[384,256]{1,0:T(8,128)(2,1)S(1)} %collective-permute-done.25.refs_2_), channel_id=1, source_target_pairs={{0,1},{1,2},{2,3},{3,4},{4,5},{5,6},{6,7},{7,0},{8,9},{9,10},{10,1... | collective-permute-start | bytes 589832 | tf_op jit(solution)/shard_map/ppermute | solution.py:128
  216.8 7.0 %collective-permute-start.30 = (bf16[384,256]{1,0:T(8,128)(2,1)S(1)}, bf16[384,256]{1,0:T(8,128)(2,1)S(1)}, u32[]{:S(2)}, u32[]{:S(2)}) collective-permute-start(bf16[384,256]{1,0:T(8,128)(2,1)S(1)} %broadcast_select_fusion.1), channel_id=1, source_target_pairs={{0,1},{1,2},{2,3},{3,4},{4,5},{5,6},{6,7},{7,0},{128,135},{129,128... | collective-permute-start | bytes 589832 | tf_op jit(solution)/shard_map/ppermute | solution.py:131
  228.4 15.1 %all-to-all-start.3 = ((bf16[16,24,1024]{2,1,0:T(8,128)(2,1)}), bf16[16,24,1024]{2,1,0:T(8,128)(2,1)S(1)}, u32[]{:S(2)}, u32[]{:S(2)}) async-start(bf16[16,24,1024]{2,1,0:T(8,128)(2,1)} %bitcast.31), calls=%async_computation.3 | async-start | bytes 1572864 | tf_op jit(solution)/shard_map/all_to_all | solution.py:294
  244.7 12.0 %all-to-all-start.4 = ((bf16[8,4,896]{2,1,0:T(4,128)(2,1)}), bf16[8,4,896]{2,1,0:T(4,128)(2,1)S(1)}, u32[]{:S(2)}, u32[]{:S(2)}) async-start(bf16[8,4,896]{2,1,0:T(4,128)(2,1)} %reshape.387), calls=%async_computation.4 | async-start | bytes 114688 | tf_op jit(solution)/shard_map/all_to_all | solution.py:306

commit v3 on v2

--- a/solution.py
+++ b/solution.py
@@ -47,6 +47,26 @@
         out_specs=VMEM,
         compiler_params=pltpu.CompilerParams(vmem_limit_bytes=32 << 20),
     )(hidden, gain, pack, extra)
+
+
+def merge_kernel(partial_ref, residual_ref, out_ref):
+    total = partial_ref[0].astype(f32)
+    for k in range(1, partial_ref.shape[0]):
+        total += partial_ref[k].astype(f32)
+    attended = total.astype(bf16).astype(f32)
+    hidden = (residual_ref[...].astype(f32) + attended).astype(bf16)
+    for p in range(out_ref.shape[0]):
+        out_ref[p] = hidden
+
+
+def merge(partial, residual, copies):
+    return pl.pallas_call(
+        merge_kernel,
+        out_shape=jax.ShapeDtypeStruct((copies,) + residual.shape, bf16),
+        in_specs=[VMEM] * 2,
+        out_specs=VMEM,
+        compiler_params=pltpu.CompilerParams(vmem_limit_bytes=32 << 20),
+    )(partial, residual)
 
 
 def gate_up_kernel(count, *refs):
@@ -219,13 +239,9 @@
         axis=1,
     )
     got = lax.all_to_all(send, "dp", split_axis=0, concat_axis=0, tiled=True)
-    for k in (1, 7, 2, 6):
+    got, slabs = lax.optimization_barrier((got, slabs))
+    for k in (1, 7, 2, 6, 3, 5, 4):
         shift(k)
-    wave = lax.optimization_barrier((downs[1], downs[7], slabs[3], slabs[5], slabs[4]))
-    downs[1], downs[7], slabs[3], slabs[5], slabs[4] = wave
-    for k in (3, 5, 4):
-        shift(k)
-    got, downs = lax.optimization_barrier((got, downs))
     res_piece = got[:, heads * reqs : heads * reqs + res_rows].reshape(n_dp * rows, cols)
     fact = got[:, heads * reqs + res_rows :, :rows]
     mine = fact[:, 0].reshape(1, n_dp * rows) > 0
@@ -240,18 +256,15 @@
         partial.reshape(n_head, n_dp * rows, cols), "head", split_axis=0, concat_axis=0, tiled=True
     )
     partial, gates, ups = lax.optimization_barrier((partial, gates, ups))
-    attended = jnp.sum(partial.astype(f32), axis=0).astype(bf16)
-    hidden_piece = (res_piece.astype(f32) + attended.astype(f32)).astype(bf16)
 
     hidden = lax.all_to_all(
-        jnp.broadcast_to(hidden_piece[None], (n_dp,) + hidden_piece.shape),
-        "dp",
-        split_axis=0,
-        concat_axis=0,
-        tiled=True,
-    )
-    downs2 = [swap(d) for d in downs]
-    hidden, downs2 = lax.optimization_barrier((hidden, downs2))
+        merge(partial, res_piece, n_dp), "dp", split_axis=0, concat_axis=0, tiled=True
+    )
+    hidden, downs[1], downs[7], downs[2], downs[6], downs[3], downs[5], downs[4] = lax.optimization_barrier((hidden, downs[1], downs[7], downs[2], downs[6], downs[3], downs[5], downs[4]))
+    downs2 = [None] * n_head
+    for k in (0,):
+        downs2[k] = swap(downs[k])
+    hidden, downs2[0] = lax.optimization_barrier((hidden, downs2[0]))
     home = lax.dynamic_slice(hidden, (0, dp * rows, 0), (n_dp, rows, cols))
 
     def index(shape, axis):
@@ -287,6 +300,9 @@
     order = (index((n_head * fill, n_head * fill), 0) == to).astype(bf16)
     active = jnp.dot(order, active, preferred_element_type=f32).astype(bf16)
 
+    for k in (1, 7, 2, 6, 3, 5, 4):
+        downs2[k] = swap(downs[k])
+    active, downs2[1], downs2[7], downs2[2], downs2[6], downs2[3], downs2[5], downs2[4] = lax.optimization_barrier((active, downs2[1], downs2[7], downs2[2], downs2[6], downs2[3], downs2[5], downs2[4]))
     steps, _ = ring(active[:, : 2 * LANES], None)
     actives = [s[0] for s in steps] + [s[1] for s in steps[-2:0:-1]]
     out = down_sums(actives, downs, downs2, active[:, 2 * LANES :])

time: 258 us -> 246 us (0.953)
  waiting for transfers between devices: 126 us -> 109 us
  local copies, waits for them, and re-layouts: 11.7 us -> 18.2 us
  starting transfers between devices: 68.9 us -> 73.3 us
  other arithmetic: 11.5 us -> 8.02 us
  Pallas kernels: 27.3 us -> 24.1 us
    ppermute x6, waiting for transfers between devices: 23.5 us -> 3.54 us  [ring(): lax.ppermute(held[-1], 'head', left)]
    ppermute x7, waiting for transfers between devices: 32 us -> 17.4 us  [shift(): lax.ppermute(slabs[k], 'head', [(i, (i + k) % n_head) for i in range(n_he...]
    ppermute x6, waiting for transfers between devices: 21.4 us -> 35.6 us  [ring(): lax.ppermute(held[0], 'head', right)]
    all_to_all x1, waiting for transfers between devices: 0.01 us -> 11.3 us  [local(): got = lax.all_to_all(send, 'dp', split_axis=0, concat_axis=0, tiled=True)]
    ppermute x6, starting transfers between devices: 2.3 us -> 9.27 us  [ring(): lax.ppermute(held[0], 'head', right)]
    all_to_all x1, waiting for transfers between devices: 6.74 us -> 0.01 us  [local(): lax.all_to_all(merge(partial, res_piece, n_dp), 'dp', split_axis=0, conca...]
    unnamed x20 -> x22, local copies, waits for them, and re-layouts: 1.45 us -> 6.49 us
    all_to_all x1, starting transfers between devices: 4.15 us -> 8.47 us  [local(): lax.all_to_all(partial.reshape(n_head, n_dp * rows, cols), 'head', split_...]
  transfers between devices with their start and end apart: 36 -> 36, of which waited for: 29 -> 19; matrix products, arithmetic and copies ran while one was open for 7% -> 7% of each run, Pallas kernels for 6% -> 7%
where the time goes in v3:
time: 246 us; the launch traced here: 245 us
  waiting for transfers between devices  109 us (44%)
  starting transfers between devices  73.3 us (30%)
  Pallas kernels  24.1 us (10%)
  local copies, waits for them, and re-layouts  18.2 us (7%)
  matrix products  11.7 us (5%)
  other arithmetic  8.02 us (3%)
    ppermute x6, waiting for transfers between devices, ring(): lax.ppermute(held[0], 'head', right)  35.6 us
    pallas_call x5, Pallas kernels, gate_up(): pl.pallas_call(functools.partial(gate_up_kernel, len(blocks)), out_shape=...  17.9 us
    ppermute x7, waiting for transfers between devices, shift(): lax.ppermute(slabs[k], 'head', [(i, (i + k) % n_head) for i in range(n_he...  17.4 us
    ppermute x6, starting transfers between devices, ring(): lax.ppermute(held[-1], 'head', left)  15.5 us
    ppermute x2, waiting for transfers between devices, ring(): got = (lax.ppermute(one, ('group', 'head'), both),)  14 us
    ppermute x7, starting transfers between devices, shift(): lax.ppermute(slabs[k], 'head', [(i, (i + k) % n_head) for i in range(n_he...  13.7 us
    all_to_all x1, waiting for transfers between devices, local(): got = lax.all_to_all(send, 'dp', split_axis=0, concat_axis=0, tiled=True)  11.3 us
    all_to_all x1, waiting for transfers between devices, local(): back = lax.all_to_all(out, 'dp', split_axis=0, concat_axis=0, tiled=True)  10.1 us
  transfers between devices with their start and end apart: 36, of which 19 were waited for; matrix products, arithmetic and copies ran while one was open for 7% of the time, Pallas kernels for 7%

profile of v3, /device:TPU:8, one launch (start us, length us, event | category | flops | bytes accessed | tf_op | source)
XLA Modules:
  0.0 244.8 jit_solution(5847527048560012114)
XLA Ops:
  0.0 0.9 select_reduce_fusion
  1.0 0.9 reshape_squeeze.7
  2.1 0.7 iota_compare_fusion.4
  2.9 6.1 %fusion.75 = (f32[32,8]{1,0:T(8,128)S(1)}, f32[32,8,192]{2,1,0:T(8,128)S(1)}) fusion(bf16[1,32,8,576]{3,2,1,0:T(8,128)(2,1)} %param.12, pred[32,192]{1,0:T(8,128)(4,1)S(1)} %iota_compare_fusion.4, bf16[1,32,192,576]{3,2,1,0:T(8,128)(2,1)} %param.13), kind=kOutput, calls=%fused_computation.152 | convolution fusion | flops 56819904 | bytes 7576576 | tf_op jit(solution)/shard_map/sub | solution.py:219
  8.9 3.7 %fusion.6 = bf16[32,8,512]{2,1,0:T(8,128)(2,1)S(1)} fusion(bf16[32,192,576]{2,1,0:T(8,128)(2,1)} %bitcast.93, f32[32,8,192]{2,1,0:T(8,128)S(1)} %get-tuple-element.98, f32[32,8]{1,0:T(8,128)S(1)} %get-tuple-element.97), kind=kOutput, calls=%fused_computation.9 | convolution fusion | flops 50561024 | bytes 6751232 | tf_op jit(solution)/shard_map/rhl,rlc->rhc/dot_general | solution.py:221
  13.2 1.1 fusion.11
  14.4 7.4 %all-to-all-start = ((bf16[16,272,128]{2,1,0:T(8,128)(2,1)}), bf16[16,272,128]{2,1,0:T(8,128)(2,1)}, u32[]{:S(2)}, u32[]{:S(2)}) async-start(bf16[16,272,128]{2,1,0:T(8,128)(2,1)} %fusion.11), calls=%async_computation | async-start | bytes 2228224 | tf_op jit(solution)/shard_map/all_to_all | solution.py:241
  22.4 2.4 copy.67
  24.7 3.0 %dynamic-slice_bitcast_fusion = (bf16[896,128]{1,0:T(8,128)(2,1)}, bf16[896,128]{1,0:T(8,128)(2,1)}, bf16[896,128]{1,0:T(8,128)(2,1)}, bf16[896,128]{1,0:T(8,128...) fusion(bf16[8,896,128]{2,1,0:T(8,128)(2,1)} %bitcast.96, ...), kind=kLoop, calls=%fused_computation.33 | loop fusion | bytes 3670048 | tf_op jit(solution)/shard_map/jit(dynamic_index_in_dim)/squeeze | solution.py:199
  27.7 11.3 %all-to-all-done = bf16[16,272,128]{2,1,0:T(8,128)(2,1)} async-done(((bf16[16,272,128]{2,1,0:T(8,128)(2,1)}), bf16[16,272,128]{2,1,0:T(8,128)(2,1)}, u32[]{:S(2)}, u32[]{:S(2)}) %all-to-all-start) | async-done | bytes 1114144 | tf_op jit(solution)/shard_map/all_to_all | solution.py:241
  39.0 1.6 copy.52
  40.8 0.8 fusion.4
  41.6 1.0 copy.63
  42.6 8.5 %all-to-all-start.1 = ((bf16[8,64,448]{2,1,0:T(8,128)(2,1)}), bf16[8,64,448]{2,1,0:T(8,128)(2,1)S(1)}, u32[]{:S(2)}, u32[]{:S(2)}) async-start(bf16[8,64,448]{2,1,0:T(8,128)(2,1)} %copy.63), calls=%async_computation.1 | async-start | bytes 1048576 | tf_op jit(solution)/shard_map/all_to_all | solution.py:255
  51.8 1.5 slice.30
  53.3 1.0 reshape.373.residual_ref
  54.3 2.1 collective-permute-start.2
  56.3 1.3 collective-permute-start.3
  57.6 1.6 collective-permute-start.4
  59.3 8.6 %all-to-all-done.1.partial_ref = bf16[8,64,448]{2,1,0:T(8,128)(2,1)S(1)} async-done(((bf16[8,64,448]{2,1,0:T(8,128)(2,1)}), bf16[8,64,448]{2,1,0:T(8,128)(2,1)S(1)}, u32[]{:S(2)}, u32[]{:S(2)}) %all-to-all-start.1) | async-done | bytes 458784 | tf_op jit(solution)/shard_map/all_to_all | solution.py:255
  68.1 1.0 copy-done.4
  69.0 5.5 %all-to-all-start.2 = ((bf16[16,64,448]{2,1,0:T(8,128)(2,1)}), bf16[16,64,448]{2,1,0:T(8,128)(2,1)}, u32[]{:S(2)}, u32[]{:S(2)}) async-start(bf16[16,64,448]{2,1,0:T(8,128)(2,1)} %copy-done.4), calls=%async_computation.2 | async-start | bytes 2097152 | tf_op jit(solution)/shard_map/all_to_all | solution.py:260
  74.5 0.8 slice_bitcast_fusion
  75.3 0.8 compare_reduce_fusion
  76.6 2.4 collective-permute-start.6
  79.0 2.7 %collective-permute-start.7 = (bf16[896,128]{1,0:T(8,128)(2,1)}, bf16[896,128]{1,0:T(8,128)(2,1)}, u32[]{:S(2)}, u32[]{:S(2)}) collective-permute-start(bf16[896,128]{1,0:T(8,128)(2,1)} %get-tuple-element.54), channel_id=1, source_target_pairs={{0,5},{1,6},{2,7},{3,0},{4,1},{5,2},{6,3},{7,4},{8,13},{9,14},{10,... | collective-permute-start | bytes 688136 | tf_op jit(solution)/shard_map/ppermute | solution.py:204
  81.7 3.5 %collective-permute-start.8 = (bf16[896,128]{1,0:T(8,128)(2,1)}, bf16[896,128]{1,0:T(8,128)(2,1)}, u32[]{:S(2)}, u32[]{:S(2)}) collective-permute-start(bf16[896,128]{1,0:T(8,128)(2,1)} %get-tuple-element.55), channel_id=1, source_target_pairs={{0,4},{1,5},{2,6},{3,7},{4,0},{5,1},{6,2},{7,3},{8,12},{9,13},{10,... | collective-permute-start | bytes 688136 | tf_op jit(solution)/shard_map/ppermute | solution.py:204
  85.5 0.8 fusion.38.pack_ref
  86.3 12.2 %collective-permute-done.5.refs_14_ = bf16[896,128]{1,0:T(8,128)(2,1)S(1)} collective-permute-done((bf16[896,128]{1,0:T(8,128)(2,1)}, bf16[896,128]{1,0:T(8,128)(2,1)S(1)}, u32[]{:S(2)}, u32[]{:S(2)}) %collective-permute-start.5) | collective-permute-done | bytes 229408 | tf_op jit(solution)/shard_map/ppermute | solution.py:204
  98.5 5.1 %collective-permute-done.8.refs_12_ = bf16[896,128]{1,0:T(8,128)(2,1)} collective-permute-done((bf16[896,128]{1,0:T(8,128)(2,1)}, bf16[896,128]{1,0:T(8,128)(2,1)}, u32[]{:S(2)}, u32[]{:S(2)}) %collective-permute-start.8) | collective-permute-done | bytes 229408 | tf_op jit(solution)/shard_map/ppermute | solution.py:204
  103.7 2.0 shard_map.119.refs_0_
  105.6 8.6 %collective-permute-start.10 = (bf16[48,7296]{1,0:T(8,128)(2,1)S(1)}, bf16[48,7296]{1,0:T(8,128)(2,1)S(1)}, u32[]{:S(2)}, u32[]{:S(2)}) collective-permute-start(bf16[48,7296]{1,0:T(8,128)(2,1)S(1)} %shard_map.119.refs_0_), channel_id=1, source_target_pairs={{0,1},{1,2},{2,3},{3,4},{4,5},{5,6},{6,7},{7,0},{8,9},{9,10},{10,1... | collective-permute-start | bytes 2101256 | tf_op jit(solution)/shard_map/ppermute | solution.py:148
  114.2 1.5 copy-done.2
  115.7 3.5 %shard_map.120 = bf16[48,384]{1,0:T(8,128)(2,1)S(1)} custom-call(bf16[48,7296]{1,0:T(8,128)(2,1)S(1)} %shard_map.119.refs_0_, bf16[7168,128]{1,0:T(8,128)(2,1)S(1)} %bitcast.82, bf16[7168,128]{1,0:T(8,128)(2,1)} %collective-permute-done.refs_2_.refs_3_, bf16[7168,128]{1,0:T(8,128)(2,1)S(1)} %bitcast.88, bf16[7168,128]{1,0:T(8,128)(2,1)} %collective-permute-done.1.refs_4_.refs_5_), custom_call_target="tpu_custom_call" | custom-call | flops 352321536 | bytes 7340032 | tf_op jit(solution)/shard_map/pallas_call | solution.py:90
  119.2 8.3 %collective-permute-done.10.refs_0_ = bf16[48,7296]{1,0:T(8,128)(2,1)S(1)} collective-permute-done((bf16[48,7296]{1,0:T(8,128)(2,1)S(1)}, bf16[48,7296]{1,0:T(8,128)(2,1)S(1)}, u32[]{:S(2)}, u32[]{:S(2)}) %collective-permute-start.10) | collective-permute-done | bytes 700448 | tf_op jit(solution)/shard_map/ppermute | solution.py:148
  127.5 2.2 collective-permute-done.11.refs_1_
  130.0 3.0 %collective-permute-start.13 = (bf16[48,7296]{1,0:T(8,128)(2,1)S(1)}, bf16[48,7296]{1,0:T(8,128)(2,1)}, u32[]{:S(2)}, u32[]{:S(2)}) collective-permute-start(bf16[48,7296]{1,0:T(8,128)(2,1)S(1)} %collective-permute-done.11.refs_1_), channel_id=1, source_target_pairs={{0,7},{1,0},{2,1},{3,2},{4,3},{5,4},{6,5},{7,6},{8,15},{9,8},{10,9... | collective-permute-start | bytes 2101256 | tf_op jit(solution)/shard_map/ppermute | solution.py:148
  132.9 3.4 %shard_map.121 = bf16[96,384]{1,0:T(8,128)(2,1)S(1)} custom-call(bf16[48,7296]{1,0:T(8,128)(2,1)S(1)} %collective-permute-done.10.refs_0_, bf16[48,7296]{1,0:T(8,128)(2,1)S(1)} %collective-permute-done.11.refs_1_, bf16[7168,128]{1,0:T(8,128)(2,1)S(1)} %bitcast.83, bf16[7168,128]{1,0:T(8,128)(2,1)} %collective-permute-done.refs_2_.refs_3_, ...), custom_call_target="tpu_custom_call" | custom-call | flops 704643072 | bytes 7340032 | tf_op jit(solution)/shard_map/pallas_call | solution.py:90
  136.3 8.5 %collective-permute-done.12.refs_0_ = bf16[48,7296]{1,0:T(8,128)(2,1)} collective-permute-done((bf16[48,7296]{1,0:T(8,128)(2,1)S(1)}, bf16[48,7296]{1,0:T(8,128)(2,1)}, u32[]{:S(2)}, u32[]{:S(2)}) %collective-permute-start.12) | collective-permute-done | bytes 700448 | tf_op jit(solution)/shard_map/ppermute | solution.py:148
  145.6 2.9 %collective-permute-start.15 = (bf16[48,7296]{1,0:T(8,128)(2,1)}, bf16[48,7296]{1,0:T(8,128)(2,1)}, u32[]{:S(2)}, u32[]{:S(2)}) collective-permute-start(bf16[48,7296]{1,0:T(8,128)(2,1)} %collective-permute-done.13.refs_1_), channel_id=1, source_target_pairs={{0,7},{1,0},{2,1},{3,2},{4,3},{5,4},{6,5},{7,6},{8,15},{9,8},{10,9... | collective-permute-start | bytes 2101256 | tf_op jit(solution)/shard_map/ppermute | solution.py:148
  148.5 1.5 copy-done.3
  150.0 3.8 %shard_map.122 = bf16[96,384]{1,0:T(8,128)(2,1)S(1)} custom-call(bf16[48,7296]{1,0:T(8,128)(2,1)} %collective-permute-done.12.refs_0_, bf16[48,7296]{1,0:T(8,128)(2,1)} %collective-permute-done.13.refs_1_, bf16[7168,128]{1,0:T(8,128)(2,1)S(1)} %bitcast.84, bf16[7168,128]{1,0:T(8,128)(2,1)} %collective-permute-done.refs_2_.refs_3_, ...), custom_call_target="tpu_custom_call" | custom-call | flops 704643072 | bytes 7340032 | tf_op jit(solution)/shard_map/pallas_call | solution.py:90
  153.8 5.7 %collective-permute-done.14.refs_0_ = bf16[48,7296]{1,0:T(8,128)(2,1)} collective-permute-done((bf16[48,7296]{1,0:T(8,128)(2,1)}, bf16[48,7296]{1,0:T(8,128)(2,1)}, u32[]{:S(2)}, u32[]{:S(2)}) %collective-permute-start.14) | collective-permute-done | bytes 700448 | tf_op jit(solution)/shard_map/ppermute | solution.py:148
  159.5 0.9 collective-permute-done.15.refs_1_
  160.4 1.2 broadcast_select_fusion
  163.0 3.8 %shard_map.123 = bf16[96,384]{1,0:T(8,128)(2,1)S(1)} custom-call(bf16[48,7296]{1,0:T(8,128)(2,1)} %collective-permute-done.14.refs_0_, bf16[48,7296]{1,0:T(8,128)(2,1)} %collective-permute-done.15.refs_1_, bf16[7168,128]{1,0:T(8,128)(2,1)S(1)} %bitcast.85, bf16[7168,128]{1,0:T(8,128)(2,1)} %collective-permute-done.refs_2_.refs_3_, ...), custom_call_target="tpu_custom_call" | custom-call | flops 704643072 | bytes 7340032 | tf_op jit(solution)/shard_map/pallas_call | solution.py:90
  166.8 7.2 %collective-permute-done.16.refs_0_ = bf16[48,7296]{1,0:T(8,128)(2,1)S(1)} collective-permute-done((bf16[48,7296]{1,0:T(8,128)(2,1)S(1)}, bf16[48,7296]{1,0:T(8,128)(2,1)S(1)}, u32[]{:S(2)}, u32[]{:S(2)}) %collective-permute-start.16) | collective-permute-done | bytes 700448 | tf_op jit(solution)/shard_map/ppermute | solution.py:151
  174.0 3.5 %shard_map.124 = bf16[48,384]{1,0:T(8,128)(2,1)S(1)} custom-call(bf16[48,7296]{1,0:T(8,128)(2,1)S(1)} %collective-permute-done.16.refs_0_, bf16[7168,128]{1,0:T(8,128)(2,1)S(1)} %bitcast.86, bf16[7168,128]{1,0:T(8,128)(2,1)} %collective-permute-done.refs_2_.refs_3_, bf16[7168,128]{1,0:T(8,128)(2,1)S(1)} %bitcast.92, ...), custom_call_target="tpu_custom_call" | custom-call | flops 352321536 | bytes 7340032 | tf_op jit(solution)/shard_map/pallas_call | solution.py:90
  178.5 0.9 collective-permute-done.22.refs_21_
  179.9 3.2 %collective-permute-start.27 = (bf16[384,256]{1,0:T(8,128)(2,1)S(1)}, bf16[384,256]{1,0:T(8,128)(2,1)S(1)}, u32[]{:S(2)}, u32[]{:S(2)}) collective-permute-start(bf16[384,256]{1,0:T(8,128)(2,1)S(1)} %slice.33.refs_0_), channel_id=1, source_target_pairs={{0,7},{1,0},{2,1},{3,2},{4,3},{5,4},{6,5},{7,6},{8,15},{9,8},{10,9... | collective-permute-start | bytes 589832 | tf_op jit(solution)/shard_map/ppermute | solution.py:148
  183.1 5.1 %collective-permute-done.24.refs_1_ = bf16[384,256]{1,0:T(8,128)(2,1)S(1)} collective-permute-done((bf16[384,256]{1,0:T(8,128)(2,1)S(1)}, bf16[384,256]{1,0:T(8,128)(2,1)S(1)}, u32[]{:S(2)}, u32[]{:S(2)}) %collective-permute-start.24) | collective-permute-done | bytes 196640 | tf_op jit(solution)/shard_map/ppermute | solution.py:148
  188.2 3.2 %collective-permute-start.28 = (bf16[384,256]{1,0:T(8,128)(2,1)S(1)}, bf16[384,256]{1,0:T(8,128)(2,1)S(1)}, u32[]{:S(2)}, u32[]{:S(2)}) collective-permute-start(bf16[384,256]{1,0:T(8,128)(2,1)S(1)} %collective-permute-done.27.refs_7_), channel_id=1, source_target_pairs={{0,7},{1,0},{2,1},{3,2},{4,3},{5,4},{6,5},{7,6},{8,15},{9,8},{10,9... | collective-permute-start | bytes 589832 | tf_op jit(solution)/shard_map/ppermute | solution.py:148
  191.5 4.3 %collective-permute-done.25.refs_2_ = bf16[384,256]{1,0:T(8,128)(2,1)S(1)} collective-permute-done((bf16[384,256]{1,0:T(8,128)(2,1)S(1)}, bf16[384,256]{1,0:T(8,128)(2,1)S(1)}, u32[]{:S(2)}, u32[]{:S(2)}) %collective-permute-start.25) | collective-permute-done | bytes 196640 | tf_op jit(solution)/shard_map/ppermute | solution.py:148
  195.8 3.2 %collective-permute-start.29 = (bf16[384,256]{1,0:T(8,128)(2,1)S(1)}, bf16[384,256]{1,0:T(8,128)(2,1)S(1)}, u32[]{:S(2)}, u32[]{:S(2)}) collective-permute-start(bf16[384,256]{1,0:T(8,128)(2,1)S(1)} %collective-permute-done.28.refs_6_), channel_id=1, source_target_pairs={{0,7},{1,0},{2,1},{3,2},{4,3},{5,4},{6,5},{7,6},{8,15},{9,8},{10,9... | collective-permute-start | bytes 589832 | tf_op jit(solution)/shard_map/ppermute | solution.py:148
  199.0 3.6 %collective-permute-done.26.refs_3_ = bf16[384,256]{1,0:T(8,128)(2,1)S(1)} collective-permute-done((bf16[384,256]{1,0:T(8,128)(2,1)S(1)}, bf16[384,256]{1,0:T(8,128)(2,1)S(1)}, u32[]{:S(2)}, u32[]{:S(2)}) %collective-permute-start.26) | collective-permute-done | bytes 196640 | tf_op jit(solution)/shard_map/ppermute | solution.py:148
  202.8 6.9 %collective-permute-done.30.refs_4_ = bf16[384,256]{1,0:T(8,128)(2,1)S(1)} collective-permute-done((bf16[384,256]{1,0:T(8,128)(2,1)S(1)}, bf16[384,256]{1,0:T(8,128)(2,1)S(1)}, u32[]{:S(2)}, u32[]{:S(2)}) %collective-permute-start.30) | collective-permute-done | bytes 196640 | tf_op jit(solution)/shard_map/ppermute | solution.py:151
  209.6 4.1 %shard_map.125 = bf16[384,1024]{1,0:T(8,128)(2,1)} custom-call(bf16[384,256]{1,0:T(8,128)(2,1)S(1)} %slice.33.refs_0_, bf16[384,256]{1,0:T(8,128)(2,1)S(1)} %collective-permute-done.24.refs_1_, bf16[384,256]{1,0:T(8,128)(2,1)S(1)} %collective-permute-done.25.refs_2_, bf16[384,256]{1,0:T(8,128)(2,1)S(1)} %collective-permute-done.26.refs_3_, ...), custom_call_target="tpu_custom_call" | custom-call | tf_op jit(solution)/shard_map/pallas_call | solution.py:126
  213.8 7.3 %all-to-all-start.3 = ((bf16[16,24,1024]{2,1,0:T(8,128)(2,1)}), bf16[16,24,1024]{2,1,0:T(8,128)(2,1)S(1)}, u32[]{:S(2)}, u32[]{:S(2)}) async-start(bf16[16,24,1024]{2,1,0:T(8,128)(2,1)} %bitcast.31), calls=%async_computation.3 | async-start | bytes 1572864 | tf_op jit(solution)/shard_map/all_to_all | solution.py:310
  221.0 10.1 %all-to-all-done.3 = bf16[16,24,1024]{2,1,0:T(8,128)(2,1)S(1)} async-done(((bf16[16,24,1024]{2,1,0:T(8,128)(2,1)}), bf16[16,24,1024]{2,1,0:T(8,128)(2,1)S(1)}, u32[]{:S(2)}, u32[]{:S(2)}) %all-to-all-start.3) | async-done | bytes 786464 | tf_op jit(solution)/shard_map/all_to_all | solution.py:310
  231.7 0.7 reshape.378
  232.4 3.5 %all-to-all-start.4 = ((bf16[8,4,896]{2,1,0:T(4,128)(2,1)}), bf16[8,4,896]{2,1,0:T(4,128)(2,1)S(1)}, u32[]{:S(2)}, u32[]{:S(2)}) async-start(bf16[8,4,896]{2,1,0:T(4,128)(2,1)} %reshape.378), calls=%async_computation.4 | async-start | bytes 114688 | tf_op jit(solution)/shard_map/all_to_all | solution.py:322
  235.9 0.9 convert_bitcast_fusion
  237.0 7.2 %all-to-all-done.4 = bf16[8,4,896]{2,1,0:T(4,128)(2,1)S(1)} async-done(((bf16[8,4,896]{2,1,0:T(4,128)(2,1)}), bf16[8,4,896]{2,1,0:T(4,128)(2,1)S(1)}, u32[]{:S(2)}, u32[]{:S(2)}) %all-to-all-start.4) | async-done | bytes 57376 | tf_op jit(solution)/shard_map/all_to_all | solution.py:322
  244.2 0.7 add_convert_fusion
  (91 shorter events, 8.1 us)
Async XLA Ops:
  0.0 12.7 %copy-start = (bf16[8,512,128]{2,1,0:T(8,128)(2,1)S(1)}, bf16[8,512,128]{2,1,0:T(8,128)(2,1)}, u32[]{:S(2)}) copy-start(bf16[8,512,128]{2,1,0:T(8,128)(2,1)} %param.15) | copy-start | bytes 3145732
  13.2 8.5 %copy-start.1 = (bf16[1,7168,128]{2,1,0:T(8,128)(2,1)S(1)}, bf16[1,7168,128]{2,1,0:T(8,128)(2,1)}, u32[]{:S(2)}) copy-start(bf16[1,7168,128]{2,1,0:T(8,128)(2,1)} %param.21) | copy-start | bytes 5505028
  14.4 24.6 %all-to-all-start = ((bf16[16,272,128]{2,1,0:T(8,128)(2,1)}), bf16[16,272,128]{2,1,0:T(8,128)(2,1)}, u32[]{:S(2)}, u32[]{:S(2)}) async-start(bf16[16,272,128]{2,1,0:T(8,128)(2,1)} %fusion.11), calls=%async_computation | async-start | bytes 2228224 | tf_op jit(solution)/shard_map/all_to_all | solution.py:241
  21.8 35.9 %collective-permute-start = (bf16[7168,128]{1,0:T(8,128)(2,1)S(1)}, bf16[7168,128]{1,0:T(8,128)(2,1)}, u32[]{:S(2)}, u32[]{:S(2)}) collective-permute-start(bf16[7168,128]{1,0:T(8,128)(2,1)S(1)} %bitcast.81), channel_id=1, source_target_pairs={{0,128},{128,0},{1,129},{129,1},{2,130},{130,2},{3,131},{131,3},{4... | collective-permute-start | bytes 5505032 | tf_op jit(solution)/shard_map/ppermute | solution.py:192
  21.9 37.4 %collective-permute-start.1 = (bf16[7168,128]{1,0:T(8,128)(2,1)}, bf16[7168,128]{1,0:T(8,128)(2,1)}, u32[]{:S(2)}, u32[]{:S(2)}) collective-permute-start(bf16[7168,128]{1,0:T(8,128)(2,1)} %bitcast.87), channel_id=1, source_target_pairs={{0,128},{128,0},{1,129},{129,1},{2,130},{130,2},{3,131},{131,3},{4... | collective-permute-start | bytes 5505032 | tf_op jit(solution)/shard_map/ppermute | solution.py:192
  39.0 1.8 copy-start.6
  41.6 9.5 %copy-start.7 = (f32[7168]{0:T(1024)S(1)}, f32[7168]{0:T(1024)}, u32[]{:S(2)}) copy-start(f32[7168]{0:T(1024)} %param.18) | copy-start | bytes 86020
  42.6 25.3 %all-to-all-start.1 = ((bf16[8,64,448]{2,1,0:T(8,128)(2,1)}), bf16[8,64,448]{2,1,0:T(8,128)(2,1)S(1)}, u32[]{:S(2)}, u32[]{:S(2)}) async-start(bf16[8,64,448]{2,1,0:T(8,128)(2,1)} %copy.63), calls=%async_computation.1 | async-start | bytes 1048576 | tf_op jit(solution)/shard_map/all_to_all | solution.py:255
  51.0 52.6 %collective-permute-start.9 = (bf16[896,128]{1,0:T(8,128)(2,1)}, bf16[896,128]{1,0:T(8,128)(2,1)}, u32[]{:S(2)}, u32[]{:S(2)}) collective-permute-start(bf16[896,128]{1,0:T(8,128)(2,1)} %get-tuple-element.96.refs_8_), channel_id=1, source_target_pairs={{0,128},{128,0},{1,129},{129,1},{2,130},{130,2},{3,131},{131,3},{4... | collective-permute-start | bytes 688136 | tf_op jit(solution)/shard_map/ppermute | solution.py:192
  54.3 22.3 %collective-permute-start.2 = (bf16[896,128]{1,0:T(8,128)(2,1)}, bf16[896,128]{1,0:T(8,128)(2,1)}, u32[]{:S(2)}, u32[]{:S(2)}) collective-permute-start(bf16[896,128]{1,0:T(8,128)(2,1)} %get-tuple-element.49), channel_id=1, source_target_pairs={{0,1},{1,2},{2,3},{3,4},{4,5},{5,6},{6,7},{7,0},{8,9},{9,10},{10,1... | collective-permute-start | bytes 688136 | tf_op jit(solution)/shard_map/ppermute | solution.py:204
  56.3 22.7 %collective-permute-start.3 = (bf16[896,128]{1,0:T(8,128)(2,1)}, bf16[896,128]{1,0:T(8,128)(2,1)}, u32[]{:S(2)}, u32[]{:S(2)}) collective-permute-start(bf16[896,128]{1,0:T(8,128)(2,1)} %get-tuple-element.50), channel_id=1, source_target_pairs={{0,7},{1,0},{2,1},{3,2},{4,3},{5,4},{6,5},{7,6},{8,15},{9,8},{10,9... | collective-permute-start | bytes 688136 | tf_op jit(solution)/shard_map/ppermute | solution.py:204
  57.6 24.1 %collective-permute-start.4 = (bf16[896,128]{1,0:T(8,128)(2,1)}, bf16[896,128]{1,0:T(8,128)(2,1)}, u32[]{:S(2)}, u32[]{:S(2)}) collective-permute-start(bf16[896,128]{1,0:T(8,128)(2,1)} %get-tuple-element.51), channel_id=1, source_target_pairs={{0,2},{1,3},{2,4},{3,5},{4,6},{5,7},{6,0},{7,1},{8,10},{9,11},{10,... | collective-permute-start | bytes 688136 | tf_op jit(solution)/shard_map/ppermute | solution.py:204
  68.0 1.0 copy-start.4
  69.0 34.7 %all-to-all-start.2 = ((bf16[16,64,448]{2,1,0:T(8,128)(2,1)}), bf16[16,64,448]{2,1,0:T(8,128)(2,1)}, u32[]{:S(2)}, u32[]{:S(2)}) async-start(bf16[16,64,448]{2,1,0:T(8,128)(2,1)} %copy-done.4), calls=%async_computation.2 | async-start | bytes 2097152 | tf_op jit(solution)/shard_map/all_to_all | solution.py:260
  76.1 22.4 %collective-permute-start.5 = (bf16[896,128]{1,0:T(8,128)(2,1)}, bf16[896,128]{1,0:T(8,128)(2,1)S(1)}, u32[]{:S(2)}, u32[]{:S(2)}) collective-permute-start(bf16[896,128]{1,0:T(8,128)(2,1)} %get-tuple-element.52), channel_id=1, source_target_pairs={{0,6},{1,7},{2,0},{3,1},{4,2},{5,3},{6,4},{7,5},{8,14},{9,15},{10,... | collective-permute-start | bytes 688136 | tf_op jit(solution)/shard_map/ppermute | solution.py:204
  76.6 21.9 %collective-permute-start.6 = (bf16[896,128]{1,0:T(8,128)(2,1)}, bf16[896,128]{1,0:T(8,128)(2,1)S(1)}, u32[]{:S(2)}, u32[]{:S(2)}) collective-permute-start(bf16[896,128]{1,0:T(8,128)(2,1)} %get-tuple-element.53), channel_id=1, source_target_pairs={{0,3},{1,4},{2,5},{3,6},{4,7},{5,0},{6,1},{7,2},{8,11},{9,12},{10,... | collective-permute-start | bytes 688136 | tf_op jit(solution)/shard_map/ppermute | solution.py:204
  79.0 19.5 %collective-permute-start.7 = (bf16[896,128]{1,0:T(8,128)(2,1)}, bf16[896,128]{1,0:T(8,128)(2,1)}, u32[]{:S(2)}, u32[]{:S(2)}) collective-permute-start(bf16[896,128]{1,0:T(8,128)(2,1)} %get-tuple-element.54), channel_id=1, source_target_pairs={{0,5},{1,6},{2,7},{3,0},{4,1},{5,2},{6,3},{7,4},{8,13},{9,14},{10,... | collective-permute-start | bytes 688136 | tf_op jit(solution)/shard_map/ppermute | solution.py:204
  81.7 22.0 %collective-permute-start.8 = (bf16[896,128]{1,0:T(8,128)(2,1)}, bf16[896,128]{1,0:T(8,128)(2,1)}, u32[]{:S(2)}, u32[]{:S(2)}) collective-permute-start(bf16[896,128]{1,0:T(8,128)(2,1)} %get-tuple-element.55), channel_id=1, source_target_pairs={{0,4},{1,5},{2,6},{3,7},{4,0},{5,1},{6,2},{7,3},{8,12},{9,13},{10,... | collective-permute-start | bytes 688136 | tf_op jit(solution)/shard_map/ppermute | solution.py:204
  105.6 21.8 %collective-permute-start.10 = (bf16[48,7296]{1,0:T(8,128)(2,1)S(1)}, bf16[48,7296]{1,0:T(8,128)(2,1)S(1)}, u32[]{:S(2)}, u32[]{:S(2)}) collective-permute-start(bf16[48,7296]{1,0:T(8,128)(2,1)S(1)} %shard_map.119.refs_0_), channel_id=1, source_target_pairs={{0,1},{1,2},{2,3},{3,4},{4,5},{5,6},{6,7},{7,0},{8,9},{9,10},{10,1... | collective-permute-start | bytes 2101256 | tf_op jit(solution)/shard_map/ppermute | solution.py:148
  114.2 15.5 %collective-permute-start.11 = (bf16[48,7296]{1,0:T(8,128)(2,1)S(1)}, bf16[48,7296]{1,0:T(8,128)(2,1)S(1)}, u32[]{:S(2)}, u32[]{:S(2)}) collective-permute-start(bf16[48,7296]{1,0:T(8,128)(2,1)S(1)} %shard_map.119.refs_0_), channel_id=1, source_target_pairs={{0,7},{1,0},{2,1},{3,2},{4,3},{5,4},{6,5},{7,6},{8,15},{9,8},{10,9... | collective-permute-start | bytes 2101256 | tf_op jit(solution)/shard_map/ppermute | solution.py:148
  114.2 1.5 copy-start.2
  129.7 15.2 %collective-permute-start.12 = (bf16[48,7296]{1,0:T(8,128)(2,1)S(1)}, bf16[48,7296]{1,0:T(8,128)(2,1)}, u32[]{:S(2)}, u32[]{:S(2)}) collective-permute-start(bf16[48,7296]{1,0:T(8,128)(2,1)S(1)} %collective-permute-done.10.refs_0_), channel_id=1, source_target_pairs={{0,1},{1,2},{2,3},{3,4},{4,5},{5,6},{6,7},{7,0},{8,9},{9,10},{10,1... | collective-permute-start | bytes 2101256 | tf_op jit(solution)/shard_map/ppermute | solution.py:148
  130.0 15.3 %collective-permute-start.13 = (bf16[48,7296]{1,0:T(8,128)(2,1)S(1)}, bf16[48,7296]{1,0:T(8,128)(2,1)}, u32[]{:S(2)}, u32[]{:S(2)}) collective-permute-start(bf16[48,7296]{1,0:T(8,128)(2,1)S(1)} %collective-permute-done.11.refs_1_), channel_id=1, source_target_pairs={{0,7},{1,0},{2,1},{3,2},{4,3},{5,4},{6,5},{7,6},{8,15},{9,8},{10,9... | collective-permute-start | bytes 2101256 | tf_op jit(solution)/shard_map/ppermute | solution.py:148
  145.3 14.2 %collective-permute-start.14 = (bf16[48,7296]{1,0:T(8,128)(2,1)}, bf16[48,7296]{1,0:T(8,128)(2,1)}, u32[]{:S(2)}, u32[]{:S(2)}) collective-permute-start(bf16[48,7296]{1,0:T(8,128)(2,1)} %collective-permute-done.12.refs_0_), channel_id=1, source_target_pairs={{0,1},{1,2},{2,3},{3,4},{4,5},{5,6},{6,7},{7,0},{8,9},{9,10},{10,1... | collective-permute-start | bytes 2101256 | tf_op jit(solution)/shard_map/ppermute | solution.py:148
  145.6 14.8 %collective-permute-start.15 = (bf16[48,7296]{1,0:T(8,128)(2,1)}, bf16[48,7296]{1,0:T(8,128)(2,1)}, u32[]{:S(2)}, u32[]{:S(2)}) collective-permute-start(bf16[48,7296]{1,0:T(8,128)(2,1)} %collective-permute-done.13.refs_1_), channel_id=1, source_target_pairs={{0,7},{1,0},{2,1},{3,2},{4,3},{5,4},{6,5},{7,6},{8,15},{9,8},{10,9... | collective-permute-start | bytes 2101256 | tf_op jit(solution)/shard_map/ppermute | solution.py:148
  148.5 1.5 copy-start.3
  161.6 12.4 %collective-permute-start.16 = (bf16[48,7296]{1,0:T(8,128)(2,1)S(1)}, bf16[48,7296]{1,0:T(8,128)(2,1)S(1)}, u32[]{:S(2)}, u32[]{:S(2)}) collective-permute-start(bf16[48,7296]{1,0:T(8,128)(2,1)S(1)} %broadcast_select_fusion), channel_id=1, source_target_pairs={{0,1},{1,2},{2,3},{3,4},{4,5},{5,6},{6,7},{7,0},{128,135},{129,128... | collective-permute-start | bytes 2101256 | tf_op jit(solution)/shard_map/ppermute | solution.py:151
  161.8 15.6 %collective-permute-start.17 = (bf16[896,128]{1,0:T(8,128)(2,1)}, bf16[896,128]{1,0:T(8,128)(2,1)S(1)}, u32[]{:S(2)}, u32[]{:S(2)}) collective-permute-start(bf16[896,128]{1,0:T(8,128)(2,1)} %collective-permute-done.2.refs_9_), channel_id=1, source_target_pairs={{0,128},{128,0},{1,129},{129,1},{2,130},{130,2},{3,131},{131,3},{4... | collective-permute-start | bytes 688136 | tf_op jit(solution)/shard_map/ppermute | solution.py:192
  161.9 16.2 %collective-permute-start.18 = (bf16[896,128]{1,0:T(8,128)(2,1)}, bf16[896,128]{1,0:T(8,128)(2,1)S(1)}, u32[]{:S(2)}, u32[]{:S(2)}) collective-permute-start(bf16[896,128]{1,0:T(8,128)(2,1)} %collective-permute-done.3.refs_15_), channel_id=1, source_target_pairs={{0,128},{128,0},{1,129},{129,1},{2,130},{130,2},{3,131},{131,3},{4... | collective-permute-start | bytes 688136 | tf_op jit(solution)/shard_map/ppermute | solution.py:192
  162.4 16.1 %collective-permute-start.19 = (bf16[896,128]{1,0:T(8,128)(2,1)}, bf16[896,128]{1,0:T(8,128)(2,1)S(1)}, u32[]{:S(2)}, u32[]{:S(2)}) collective-permute-start(bf16[896,128]{1,0:T(8,128)(2,1)} %collective-permute-done.4.refs_10_), channel_id=1, source_target_pairs={{0,128},{128,0},{1,129},{129,1},{2,130},{130,2},{3,131},{131,3},{4... | collective-permute-start | bytes 688136 | tf_op jit(solution)/shard_map/ppermute | solution.py:192
  162.5 16.0 %collective-permute-start.20 = (bf16[896,128]{1,0:T(8,128)(2,1)S(1)}, bf16[896,128]{1,0:T(8,128)(2,1)S(1)}, u32[]{:S(2)}, u32[]{:S(2)}) collective-permute-start(bf16[896,128]{1,0:T(8,128)(2,1)S(1)} %collective-permute-done.5.refs_14_), channel_id=1, source_target_pairs={{0,128},{128,0},{1,129},{129,1},{2,130},{130,2},{3,131},{131,3},{4... | collective-permute-start | bytes 688136 | tf_op jit(solution)/shard_map/ppermute | solution.py:192
  174.0 4.6 %collective-permute-start.21 = (bf16[896,128]{1,0:T(8,128)(2,1)S(1)}, bf16[896,128]{1,0:T(8,128)(2,1)S(1)}, u32[]{:S(2)}, u32[]{:S(2)}) collective-permute-start(bf16[896,128]{1,0:T(8,128)(2,1)S(1)} %collective-permute-done.6.refs_11_), channel_id=1, source_target_pairs={{0,128},{128,0},{1,129},{129,1},{2,130},{130,2},{3,131},{131,3},{4... | collective-permute-start | bytes 688136 | tf_op jit(solution)/shard_map/ppermute | solution.py:192
  177.4 32.2 %copy-start.5 = (bf16[896,128]{1,0:T(8,128)(2,1)S(1)}, bf16[896,128]{1,0:T(8,128)(2,1)}, u32[]{:S(2)}) copy-start(bf16[896,128]{1,0:T(8,128)(2,1)} %get-tuple-element.96.refs_8_) | copy-start | bytes 688132
  177.5 1.9 collective-permute-start.22
  178.1 1.7 collective-permute-start.23
  179.8 8.4 %collective-permute-start.24 = (bf16[384,256]{1,0:T(8,128)(2,1)S(1)}, bf16[384,256]{1,0:T(8,128)(2,1)S(1)}, u32[]{:S(2)}, u32[]{:S(2)}) collective-permute-start(bf16[384,256]{1,0:T(8,128)(2,1)S(1)} %slice.33.refs_0_), channel_id=1, source_target_pairs={{0,1},{1,2},{2,3},{3,4},{4,5},{5,6},{6,7},{7,0},{8,9},{9,10},{10,1... | collective-permute-start | bytes 589832 | tf_op jit(solution)/shard_map/ppermute | solution.py:148
  179.9 8.3 %collective-permute-start.27 = (bf16[384,256]{1,0:T(8,128)(2,1)S(1)}, bf16[384,256]{1,0:T(8,128)(2,1)S(1)}, u32[]{:S(2)}, u32[]{:S(2)}) collective-permute-start(bf16[384,256]{1,0:T(8,128)(2,1)S(1)} %slice.33.refs_0_), channel_id=1, source_target_pairs={{0,7},{1,0},{2,1},{3,2},{4,3},{5,4},{6,5},{7,6},{8,15},{9,8},{10,9... | collective-permute-start | bytes 589832 | tf_op jit(solution)/shard_map/ppermute | solution.py:148
  188.2 7.5 %collective-permute-start.25 = (bf16[384,256]{1,0:T(8,128)(2,1)S(1)}, bf16[384,256]{1,0:T(8,128)(2,1)S(1)}, u32[]{:S(2)}, u32[]{:S(2)}) collective-permute-start(bf16[384,256]{1,0:T(8,128)(2,1)S(1)} %collective-permute-done.24.refs_1_), channel_id=1, source_target_pairs={{0,1},{1,2},{2,3},{3,4},{4,5},{5,6},{6,7},{7,0},{8,9},{9,10},{10,1... | collective-permute-start | bytes 589832 | tf_op jit(solution)/shard_map/ppermute | solution.py:148
  188.2 7.5 %collective-permute-start.28 = (bf16[384,256]{1,0:T(8,128)(2,1)S(1)}, bf16[384,256]{1,0:T(8,128)(2,1)S(1)}, u32[]{:S(2)}, u32[]{:S(2)}) collective-permute-start(bf16[384,256]{1,0:T(8,128)(2,1)S(1)} %collective-permute-done.27.refs_7_), channel_id=1, source_target_pairs={{0,7},{1,0},{2,1},{3,2},{4,3},{5,4},{6,5},{7,6},{8,15},{9,8},{10,9... | collective-permute-start | bytes 589832 | tf_op jit(solution)/shard_map/ppermute | solution.py:148
  195.8 6.9 %collective-permute-start.26 = (bf16[384,256]{1,0:T(8,128)(2,1)S(1)}, bf16[384,256]{1,0:T(8,128)(2,1)S(1)}, u32[]{:S(2)}, u32[]{:S(2)}) collective-permute-start(bf16[384,256]{1,0:T(8,128)(2,1)S(1)} %collective-permute-done.25.refs_2_), channel_id=1, source_target_pairs={{0,1},{1,2},{2,3},{3,4},{4,5},{5,6},{6,7},{7,0},{8,9},{9,10},{10,1... | collective-permute-start | bytes 589832 | tf_op jit(solution)/shard_map/ppermute | solution.py:148
  195.8 6.9 %collective-permute-start.29 = (bf16[384,256]{1,0:T(8,128)(2,1)S(1)}, bf16[384,256]{1,0:T(8,128)(2,1)S(1)}, u32[]{:S(2)}, u32[]{:S(2)}) collective-permute-start(bf16[384,256]{1,0:T(8,128)(2,1)S(1)} %collective-permute-done.28.refs_6_), channel_id=1, source_target_pairs={{0,7},{1,0},{2,1},{3,2},{4,3},{5,4},{6,5},{7,6},{8,15},{9,8},{10,9... | collective-permute-start | bytes 589832 | tf_op jit(solution)/shard_map/ppermute | solution.py:148
  202.7 7.0 %collective-permute-start.30 = (bf16[384,256]{1,0:T(8,128)(2,1)S(1)}, bf16[384,256]{1,0:T(8,128)(2,1)S(1)}, u32[]{:S(2)}, u32[]{:S(2)}) collective-permute-start(bf16[384,256]{1,0:T(8,128)(2,1)S(1)} %broadcast_select_fusion.1), channel_id=1, source_target_pairs={{0,1},{1,2},{2,3},{3,4},{4,5},{5,6},{6,7},{7,0},{128,135},{129,128... | collective-permute-start | bytes 589832 | tf_op jit(solution)/shard_map/ppermute | solution.py:151
  213.8 17.4 %all-to-all-start.3 = ((bf16[16,24,1024]{2,1,0:T(8,128)(2,1)}), bf16[16,24,1024]{2,1,0:T(8,128)(2,1)S(1)}, u32[]{:S(2)}, u32[]{:S(2)}) async-start(bf16[16,24,1024]{2,1,0:T(8,128)(2,1)} %bitcast.31), calls=%async_computation.3 | async-start | bytes 1572864 | tf_op jit(solution)/shard_map/all_to_all | solution.py:310
  232.4 11.8 %all-to-all-start.4 = ((bf16[8,4,896]{2,1,0:T(4,128)(2,1)}), bf16[8,4,896]{2,1,0:T(4,128)(2,1)S(1)}, u32[]{:S(2)}, u32[]{:S(2)}) async-start(bf16[8,4,896]{2,1,0:T(4,128)(2,1)} %reshape.378), calls=%async_computation.4 | async-start | bytes 114688 | tf_op jit(solution)/shard_map/all_to_all | solution.py:322

commit v4 on v3

--- a/solution.py
+++ b/solution.py
@@ -24,6 +24,7 @@
 
 def norm_pack_kernel(hidden_ref, gain_ref, pack_ref, extra_ref, out_ref):
     parts, count, cols = hidden_ref.shape
+    kept = cols - LANES
     square = jnp.zeros((count, 1), f32)
     for p in range(parts):
         part = hidden_ref[p].astype(f32)
@@ -31,25 +32,30 @@
     scale = lax.rsqrt(square / (parts * cols) + norm_eps)
     pack = pack_ref[...]
     for p in range(parts):
-        normed = (hidden_ref[p].astype(f32) * scale * gain_ref[p : p + 1]).astype(bf16)
+        part = hidden_ref[p, :, :kept].astype(f32)
+        normed = (part * scale * gain_ref[p : p + 1, :kept]).astype(bf16)
         rows = jnp.dot(pack, normed, preferred_element_type=f32).astype(bf16)
-        out_ref[:, p * cols : (p + 1) * cols] = rows
-    extra = jnp.dot(pack, extra_ref[...], preferred_element_type=f32).astype(bf16)
-    out_ref[:, parts * cols :] = extra
+        out_ref[:, p * kept : (p + 1) * kept] = rows
+    high = scale.astype(bf16).astype(f32)
+    lane = lax.broadcasted_iota(jnp.int32, extra_ref.shape, 1)
+    extra = jnp.where(lane == 3, high, extra_ref[...].astype(f32))
+    extra = jnp.where(lane == 4, scale - high, extra).astype(bf16)
+    extra = jnp.dot(pack, extra, preferred_element_type=f32).astype(bf16)
+    out_ref[:, parts * kept :] = extra
 
 
 def norm_pack(hidden, gain, pack, extra):
     parts, _, cols = hidden.shape
     return pl.pallas_call(
         norm_pack_kernel,
-        out_shape=jax.ShapeDtypeStruct((pack.shape[0], parts * cols + LANES), bf16),
+        out_shape=jax.ShapeDtypeStruct((pack.shape[0], parts * (cols - LANES) + LANES), bf16),
         in_specs=[VMEM] * 4,
         out_specs=VMEM,
         compiler_params=pltpu.CompilerParams(vmem_limit_bytes=32 << 20),
     )(hidden, gain, pack, extra)
 
 
-def merge_kernel(partial_ref, residual_ref, out_ref):
+def merge_kernel(partial_ref, residual_ref, gain_ref, out_ref, side_ref):
     total = partial_ref[0].astype(f32)
     for k in range(1, partial_ref.shape[0]):
         total += partial_ref[k].astype(f32)
@@ -57,20 +63,24 @@
     hidden = (residual_ref[...].astype(f32) + attended).astype(bf16)
     for p in range(out_ref.shape[0]):
         out_ref[p] = hidden
-
-
-def merge(partial, residual, copies):
+    side_ref[...] = (hidden[:, -LANES:].astype(f32) * gain_ref[...]).astype(bf16)
+
+
+def merge(partial, residual, gain, copies):
     return pl.pallas_call(
         merge_kernel,
-        out_shape=jax.ShapeDtypeStruct((copies,) + residual.shape, bf16),
-        in_specs=[VMEM] * 2,
-        out_specs=VMEM,
+        out_shape=(
+            jax.ShapeDtypeStruct((copies,) + residual.shape, bf16),
+            jax.ShapeDtypeStruct((residual.shape[0], LANES), bf16),
+        ),
+        in_specs=[VMEM] * 3,
+        out_specs=(VMEM, VMEM),
         compiler_params=pltpu.CompilerParams(vmem_limit_bytes=32 << 20),
-    )(partial, residual)
+    )(partial, residual, gain)
 
 
 def gate_up_kernel(count, *refs):
-    blocks, (gate_ref, gate2_ref, up_ref, up2_ref, out_ref) = refs[:count], refs[count:]
+    blocks, (gate_ref, gate2_ref, up_ref, up2_ref, *outs) = refs[:count], refs[count:]
     width = gate_ref.shape[0]
     step = 1024
     gate = up = 0.0
@@ -80,8 +90,10 @@
         gate += jnp.dot(rows, weights, preferred_element_type=f32)
         weights = jnp.concatenate([up_ref[k : k + step], up2_ref[k : k + step]], axis=1)
         up += jnp.dot(rows, weights, preferred_element_type=f32)
-    out_ref[:, : 2 * LANES] = (gate / (1.0 + jnp.exp(-gate)) * up).astype(bf16)
-    out_ref[:, 2 * LANES :] = jnp.concatenate([b[:, width:] for b in blocks], axis=0)
+    out_ref, facts_ref = outs
+    out_ref[:, : 2 * LANES] = gate
+    out_ref[:, 2 * LANES :] = up
+    facts_ref[...] = jnp.concatenate([b[:, width:] for b in blocks], axis=0)
 
 
 def gate_up(blocks, gates, ups):
@@ -89,14 +101,66 @@
     width = gates[0].shape[0]
     return pl.pallas_call(
         functools.partial(gate_up_kernel, len(blocks)),
-        out_shape=jax.ShapeDtypeStruct((rows, 3 * LANES), bf16),
+        out_shape=(
+            jax.ShapeDtypeStruct((rows, 4 * LANES), f32),
+            jax.ShapeDtypeStruct((rows, LANES), bf16),
+        ),
         in_specs=[VMEM] * (len(blocks) + 4),
-        out_specs=VMEM,
+        out_specs=(VMEM, VMEM),
         compiler_params=pltpu.CompilerParams(vmem_limit_bytes=32 << 20),
         cost_estimate=pl.CostEstimate(
             flops=8 * rows * width * LANES, bytes_accessed=8 * width * LANES, transcendentals=0
         ),
     )(*blocks, *gates, *ups)
+
+
+def finish_kernel(places, *refs):
+    steps = len(places)
+    sums, facts, refs = refs[:steps], refs[steps : 2 * steps], refs[2 * steps :]
+    side_ref, gate_ref, gate2_ref, up_ref, up2_ref, out_ref, dense = refs
+    parts, tokens, _ = side_ref.shape
+    weights = jnp.concatenate([w[...] for w in (gate_ref, gate2_ref, up_ref, up2_ref)], axis=1)
+    step = 256
+    for t in range(0, tokens, step):
+        rows = jnp.concatenate([side_ref[p, t : t + step] for p in range(parts)], axis=1)
+        dense[t : t + step] = jnp.dot(rows, weights, preferred_element_type=f32)
+    count = tokens // sum(len(p) for p in places)
+    fill = out_ref.shape[0] // sum(len(p) for p in places)
+    at = 0
+    for some, sum_ref, fact_ref in zip(places, sums, facts):
+        for b, place in enumerate(some):
+            fact = fact_ref[b * fill : (b + 1) * fill]
+            fact_f = fact.astype(f32)
+            token = lax.broadcasted_iota(jnp.int32, (fill, count), 1).astype(f32)
+            hit = (token == fact_f[:, 5:6]).astype(f32).astype(bf16)
+            picked = dense[place * count : (place + 1) * count]
+            high = picked.astype(bf16)
+            low = (picked - high.astype(f32)).astype(bf16)
+            picked = jnp.dot(hit, high, preferred_element_type=f32) + jnp.dot(
+                hit, low, preferred_element_type=f32
+            )
+            total = sum_ref[b * fill : (b + 1) * fill] + picked * (fact_f[:, 3:4] + fact_f[:, 4:5])
+            gate, up = total[:, : 2 * LANES], total[:, 2 * LANES :]
+            active = (gate / (1.0 + jnp.exp(-gate)) * up).astype(bf16)
+            out_ref[at : at + fill, : 2 * LANES] = active
+            out_ref[at : at + fill, 2 * LANES :] = fact
+            at += fill
+
+
+def finish(places, done, side, weights):
+    rows = sum(d[0].shape[0] for d in done)
+    return pl.pallas_call(
+        functools.partial(finish_kernel, places),
+        out_shape=jax.ShapeDtypeStruct((rows, 3 * LANES), bf16),
+        in_specs=[VMEM] * (2 * len(done) + 5),
+        out_specs=VMEM,
+        scratch_shapes=[pltpu.VMEM((side.shape[1], 4 * LANES), f32)],
+        compiler_params=pltpu.CompilerParams(vmem_limit_bytes=32 << 20),
+    )(*[d[0] for d in done], *[d[1] for d in done], side, *weights)
+
+
+def by_distance(steps):
+    return [s[0] for s in steps] + [s[1] for s in steps[-2:0:-1]]
 
 
 def down_kernel(count, *refs):
@@ -150,12 +214,12 @@
             one = jnp.where(lax.axis_index("group") == 0, held[0], held[-1])
             got = (lax.ppermute(one, ("group", "head"), both),)
         if beside is not None:
-            result = beside(held)
+            result = beside(step, held)
             got, result = lax.optimization_barrier((got, result))
             results.append(result)
         steps.append(got)
     if beside is not None:
-        results.append(beside(steps[-1]))
+        results.append(beside(count // 2, steps[-1]))
     return steps, results
 
 
@@ -191,8 +255,11 @@
     def swap(block):
         return lax.ppermute(block, "group", [(0, 1), (1, 0)])
 
-    gates = (w_gate[0], swap(w_gate[0]))
-    ups = (w_up[0], swap(w_up[0]))
+    def both(weight):
+        weight = weight.reshape(n_dp, cols, weight.shape[1])
+        main = weight[:, :-LANES].reshape(-1, weight.shape[2])
+        side = weight[:, -LANES:].reshape(-1, weight.shape[2])
+        return (main, swap(main)), (side, swap(side))
 
     slabs = w_down[0].reshape(n_head, piece, w_down.shape[2])
     slabs = [
@@ -239,7 +306,9 @@
         axis=1,
     )
     got = lax.all_to_all(send, "dp", split_axis=0, concat_axis=0, tiled=True)
-    got, slabs = lax.optimization_barrier((got, slabs))
+    got, slabs, gate_w, up_w = lax.optimization_barrier((got, slabs, w_gate[0], w_up[0]))
+    gates, side_gates = both(gate_w)
+    ups, side_ups = both(up_w)
     for k in (1, 7, 2, 6, 3, 5, 4):
         shift(k)
     res_piece = got[:, heads * reqs : heads * reqs + res_rows].reshape(n_dp * rows, cols)
@@ -255,11 +324,14 @@
     partial = lax.all_to_all(
         partial.reshape(n_head, n_dp * rows, cols), "head", split_axis=0, concat_axis=0, tiled=True
     )
-    partial, gates, ups = lax.optimization_barrier((partial, gates, ups))
-
-    hidden = lax.all_to_all(
-        merge(partial, res_piece, n_dp), "dp", split_axis=0, concat_axis=0, tiled=True
-    )
+    beside = lax.optimization_barrier((partial, gates, ups, side_gates, side_ups))
+    partial, gates, ups, side_gates, side_ups = beside
+
+    side_gain = lax.dynamic_slice(norm_gain.reshape(n_dp, cols), (dp, cols - LANES), (1, LANES))
+    copies, side = merge(partial, res_piece, side_gain, n_dp)
+    hidden = lax.all_to_all(copies, "dp", split_axis=0, concat_axis=0, tiled=True)
+    side = jnp.concatenate(by_distance(ring(side, None)[0]), axis=0)
+    hidden, side = lax.optimization_barrier((hidden, side))
     hidden, downs[1], downs[7], downs[2], downs[6], downs[3], downs[5], downs[4] = lax.optimization_barrier((hidden, downs[1], downs[7], downs[2], downs[6], downs[3], downs[5], downs[4]))
     downs2 = [None] * n_head
     for k in (0,):
@@ -282,15 +354,29 @@
         [
             fact[:, :2].transpose(0, 2, 1).reshape(count, 2),
             (index((count, 1), 0) % rows).astype(bf16),
-            jnp.zeros((count, LANES - 3), bf16),
+            jnp.zeros((count, 2), bf16),
+            index((count, 1), 0).astype(bf16),
+            jnp.zeros((count, LANES - 6), bf16),
         ],
         axis=1,
     )
     packed = norm_pack(hidden, norm_gain.reshape(n_dp, cols), pack.astype(bf16), extra)
 
     fill = n_dp * CAP
-    _, done = ring(packed, lambda blocks: gate_up(blocks, gates, ups))
-    active = jnp.concatenate(done, axis=0)
+    side = lax.all_to_all(
+        jnp.broadcast_to(side[None], (n_dp,) + side.shape),
+        "dp",
+        split_axis=0,
+        concat_axis=0,
+        tiled=True,
+    )
+    half = n_head // 2
+    work = lambda step, blocks: (gate_up(blocks, gates, ups), side if step == half - 2 else None)
+    _, done = ring(packed, work)
+    side = done[half - 2][1]
+    done = [d[0] for d in done]
+    places = [(0,)] + [(k, n_head - k) for k in range(1, half)] + [(half,)]
+    active = finish(places, done, side, side_gates + side_ups)
 
     r = index((1, n_head * fill), 1)
     at = jnp.where(r < fill, 0, (r - fill) // (2 * fill) + 1)
@@ -304,7 +390,7 @@
         downs2[k] = swap(downs[k])
     active, downs2[1], downs2[7], downs2[2], downs2[6], downs2[3], downs2[5], downs2[4] = lax.optimization_barrier((active, downs2[1], downs2[7], downs2[2], downs2[6], downs2[3], downs2[5], downs2[4]))
     steps, _ = ring(active[:, : 2 * LANES], None)
-    actives = [s[0] for s in steps] + [s[1] for s in steps[-2:0:-1]]
+    actives = by_distance(steps)
     out = down_sums(actives, downs, downs2, active[:, 2 * LANES :])
     out = out.reshape(n_dp, n_head * CAP, -1)
     back = lax.all_to_all(out, "dp", split_axis=0, concat_axis=0, tiled=True)

time: 246 us -> 280 us (1.14); the launches traced: 245 us -> 274 us
  starting transfers between devices: 73.3 us -> 95.4 us
  local copies, waits for them, and re-layouts: 18.2 us -> 25.7 us
  waiting for transfers between devices: 109 us -> 106 us
    ppermute x6 -> x9, starting transfers between devices: 15.5 us -> 33 us  [ring(): lax.ppermute(held[-1], 'head', left)]
    ppermute x6 -> x9, waiting for transfers between devices: 35.6 us -> 25.6 us  [ring(): lax.ppermute(held[0], 'head', right)]
    all_to_all x1 -> x2, starting transfers between devices: 5.51 us -> 12.3 us  [the longest x1 7.41 us: local(): lax.all_to_all(jnp.broadcast_to(side[None], (n_dp,) + side.shape), 'dp',...]
    slice x0 -> x4, local copies, waits for them, and re-layouts: none -> 6.17 us  [the longest x2 3.18 us: both(): side = weight[:, -LANES:].reshape(-1, weight.shape[2])]
    ppermute x6 -> x9, waiting for transfers between devices: 3.54 us -> 7.6 us  [ring(): lax.ppermute(held[-1], 'head', left)]
    ppermute x6 -> x9, starting transfers between devices: 9.27 us -> 5.51 us  [ring(): lax.ppermute(held[0], 'head', right)]
    pallas_call x1 -> x2, Pallas kernels: 0.12 us -> 3.78 us  [the longest x1 3.59 us: finish(): pl.pallas_call(functools.partial(finish_kernel, places), out_shape=jax.Sh...]
    all_to_all x1, waiting for transfers between devices: 11.3 us -> 14.3 us  [local(): got = lax.all_to_all(send, 'dp', split_axis=0, concat_axis=0, tiled=True)]
  transfers between devices with their start and end apart: 36 -> 46, of which waited for: 19 -> 21; matrix products, arithmetic and copies ran while one was open for 7% -> 10% of each run, Pallas kernels for 7% -> 7%
where the time goes in v4:
time: 280 us; the launch traced here: 274 us
  waiting for transfers between devices  106 us (38%)
  starting transfers between devices  95.4 us (34%)
  local copies, waits for them, and re-layouts  25.7 us (9%)
  Pallas kernels  24.7 us (9%)
  matrix products  12.3 us (4%)
  other arithmetic  9.38 us (3%)
    ppermute x9, starting transfers between devices, ring(): lax.ppermute(held[-1], 'head', left)  33 us
    ppermute x9, waiting for transfers between devices, ring(): lax.ppermute(held[0], 'head', right)  25.6 us
    ppermute x7, waiting for transfers between devices, shift(): lax.ppermute(slabs[k], 'head', [(i, (i + k) % n_head) for i in range(n_he...  18.1 us
    pallas_call x5, Pallas kernels, gate_up(): pl.pallas_call(functools.partial(gate_up_kernel, len(blocks)), out_shape=...  15.9 us
    all_to_all x1, waiting for transfers between devices, local(): got = lax.all_to_all(send, 'dp', split_axis=0, concat_axis=0, tiled=True)  14.3 us
    ppermute x7, starting transfers between devices, shift(): lax.ppermute(slabs[k], 'head', [(i, (i + k) % n_head) for i in range(n_he...  13.9 us
    ppermute x3, waiting for transfers between devices, ring(): got = (lax.ppermute(one, ('group', 'head'), both),)  11.6 us
    all_to_all x1, waiting for transfers between devices, local(): back = lax.all_to_all(out, 'dp', split_axis=0, concat_axis=0, tiled=True)  10.1 us
  transfers between devices with their start and end apart: 46, of which 21 were waited for; matrix products, arithmetic and copies ran while one was open for 10% of the time, Pallas kernels for 7%

profile of v4, /device:TPU:8, one launch (start us, length us, event | category | flops | bytes accessed | tf_op | source)
XLA Modules:
  0.0 274.2 jit_solution(10959589633865750142)
XLA Ops:
  0.0 0.9 select_reduce_fusion
  1.0 0.9 reshape_squeeze.7
  2.9 6.1 %fusion.75 = (f32[32,8]{1,0:T(8,128)S(1)}, f32[32,8,192]{2,1,0:T(8,128)S(1)}) fusion(bf16[1,32,8,576]{3,2,1,0:T(8,128)(2,1)} %param.12, pred[32,192]{1,0:T(8,128)(4,1)S(1)} %iota_compare_fusion.4, bf16[1,32,192,576]{3,2,1,0:T(8,128)(2,1)} %param.13), kind=kOutput, calls=%fused_computation.157 | convolution fusion | flops 56819904 | bytes 7576576 | tf_op jit(solution)/shard_map/sub | solution.py:286
  8.9 3.7 %fusion.6 = bf16[32,8,512]{2,1,0:T(8,128)(2,1)S(1)} fusion(bf16[32,192,576]{2,1,0:T(8,128)(2,1)} %bitcast.95, f32[32,8,192]{2,1,0:T(8,128)S(1)} %get-tuple-element.150, f32[32,8]{1,0:T(8,128)S(1)} %get-tuple-element.149), kind=kOutput, calls=%fused_computation.9 | convolution fusion | flops 50561024 | bytes 6751232 | tf_op jit(solution)/shard_map/rhl,rlc->rhc/dot_general | solution.py:288
  13.2 1.1 fusion.11
  14.4 7.4 %all-to-all-start = ((bf16[16,272,128]{2,1,0:T(8,128)(2,1)}), bf16[16,272,128]{2,1,0:T(8,128)(2,1)S(1)}, u32[]{:S(2)}, u32[]{:S(2)}) async-start(bf16[16,272,128]{2,1,0:T(8,128)(2,1)} %fusion.11), calls=%async_computation | async-start | bytes 2228224 | tf_op jit(solution)/shard_map/all_to_all | solution.py:308
  21.8 2.9 %dynamic-slice_bitcast_fusion = (bf16[896,128]{1,0:T(8,128)(2,1)}, bf16[896,128]{1,0:T(8,128)(2,1)}, bf16[896,128]{1,0:T(8,128)(2,1)}, bf16[896,128]{1,0:T(8,128...) fusion(bf16[8,896,128]{2,1,0:T(8,128)(2,1)} %bitcast.102, ...), kind=kLoop, calls=%fused_computation.33 | loop fusion | bytes 3670048 | tf_op jit(solution)/shard_map/jit(dynamic_index_in_dim)/squeeze | solution.py:266
  24.6 14.3 %all-to-all-done = bf16[16,272,128]{2,1,0:T(8,128)(2,1)S(1)} async-done(((bf16[16,272,128]{2,1,0:T(8,128)(2,1)}), bf16[16,272,128]{2,1,0:T(8,128)(2,1)S(1)}, u32[]{:S(2)}, u32[]{:S(2)}) %all-to-all-start) | async-done | bytes 1114144 | tf_op jit(solution)/shard_map/all_to_all | solution.py:308
  38.9 1.9 slice.55
  41.2 1.1 slice.56
  44.0 1.0 copy.63
  45.0 8.5 %all-to-all-start.1 = ((bf16[8,64,448]{2,1,0:T(8,128)(2,1)}), bf16[8,64,448]{2,1,0:T(8,128)(2,1)S(1)}, u32[]{:S(2)}, u32[]{:S(2)}) async-start(bf16[8,64,448]{2,1,0:T(8,128)(2,1)} %copy.63), calls=%async_computation.1 | async-start | bytes 1048576 | tf_op jit(solution)/shard_map/all_to_all | solution.py:324
  53.6 1.1 slice.57
  54.7 2.1 slice.58
  59.7 1.5 slice.46
  61.2 1.0 reshape.407.residual_ref
  62.2 9.3 %all-to-all-done.1.partial_ref = bf16[8,64,448]{2,1,0:T(8,128)(2,1)S(1)} async-done(((bf16[8,64,448]{2,1,0:T(8,128)(2,1)}), bf16[8,64,448]{2,1,0:T(8,128)(2,1)S(1)}, u32[]{:S(2)}, u32[]{:S(2)}) %all-to-all-start.1) | async-done | bytes 458784 | tf_op jit(solution)/shard_map/all_to_all | solution.py:324
  71.7 1.0 copy-done.3
  73.2 2.7 collective-permute-start.7
  76.5 4.9 %all-to-all-start.2 = ((bf16[16,64,448]{2,1,0:T(8,128)(2,1)}), bf16[16,64,448]{2,1,0:T(8,128)(2,1)S(1)}, u32[]{:S(2)}, u32[]{:S(2)}) async-start(bf16[16,64,448]{2,1,0:T(8,128)(2,1)} %copy-done.3), calls=%async_computation.2 | async-start | bytes 2097152 | tf_op jit(solution)/shard_map/all_to_all | solution.py:332
  81.5 3.2 %collective-permute-start.8 = (bf16[64,128]{1,0:T(8,128)(2,1)S(1)}, bf16[64,128]{1,0:T(8,128)(2,1)S(1)}, u32[]{:S(2)}, u32[]{:S(2)}) collective-permute-start(bf16[64,128]{1,0:T(8,128)(2,1)S(1)} %collective-permute-done.7), channel_id=1, source_target_pairs={{0,7},{1,0},{2,1},{3,2},{4,3},{5,4},{6,5},{7,6},{8,15},{9,8},{10,9... | collective-permute-start | bytes 49160 | tf_op jit(solution)/shard_map/ppermute | solution.py:212
  85.4 1.1 collective-permute-done.5
  86.7 3.2 %collective-permute-start.9 = (bf16[64,128]{1,0:T(8,128)(2,1)S(1)}, bf16[64,128]{1,0:T(8,128)(2,1)S(1)}, u32[]{:S(2)}, u32[]{:S(2)}) collective-permute-start(bf16[64,128]{1,0:T(8,128)(2,1)S(1)} %collective-permute-done.8), channel_id=1, source_target_pairs={{0,7},{1,0},{2,1},{3,2},{4,3},{5,4},{6,5},{7,6},{8,15},{9,8},{10,9... | collective-permute-start | bytes 49160 | tf_op jit(solution)/shard_map/ppermute | solution.py:212
  90.5 1.1 collective-permute-done.6
  92.3 0.8 slice_bitcast_fusion
  93.1 3.3 %collective-permute-start.12 = (bf16[896,128]{1,0:T(8,128)(2,1)}, bf16[896,128]{1,0:T(8,128)(2,1)}, u32[]{:S(2)}, u32[]{:S(2)}) collective-permute-start(bf16[896,128]{1,0:T(8,128)(2,1)} %get-tuple-element.80), channel_id=1, source_target_pairs={{0,7},{1,0},{2,1},{3,2},{4,3},{5,4},{6,5},{7,6},{8,15},{9,8},{10,9... | collective-permute-start | bytes 688136 | tf_op jit(solution)/shard_map/ppermute | solution.py:271
  97.4 3.2 %collective-permute-start.14 = (bf16[896,128]{1,0:T(8,128)(2,1)}, bf16[896,128]{1,0:T(8,128)(2,1)}, u32[]{:S(2)}, u32[]{:S(2)}) collective-permute-start(bf16[896,128]{1,0:T(8,128)(2,1)} %get-tuple-element.82), channel_id=1, source_target_pairs={{0,6},{1,7},{2,0},{3,1},{4,2},{5,3},{6,4},{7,5},{8,14},{9,15},{10,... | collective-permute-start | bytes 688136 | tf_op jit(solution)/shard_map/ppermute | solution.py:271
  103.0 2.7 broadcast_in_dim.60
  105.6 7.4 %all-to-all-start.3 = ((bf16[16,512,128]{2,1,0:T(8,128)(2,1)}), bf16[16,512,128]{2,1,0:T(8,128)(2,1)}, u32[]{:S(2)}, u32[]{:S(2)}) async-start(bf16[16,512,128]{2,1,0:T(8,128)(2,1)} %broadcast_in_dim.60), calls=%async_computation.3 | async-start | bytes 4194304 | tf_op jit(solution)/shard_map/all_to_all | solution.py:366
  113.1 0.8 compare_reduce_fusion
  114.2 4.9 %collective-permute-start.16 = (bf16[896,128]{1,0:T(8,128)(2,1)}, bf16[896,128]{1,0:T(8,128)(2,1)}, u32[]{:S(2)}, u32[]{:S(2)}) collective-permute-start(bf16[896,128]{1,0:T(8,128)(2,1)} %get-tuple-element.84), channel_id=1, source_target_pairs={{0,5},{1,6},{2,7},{3,0},{4,1},{5,2},{6,3},{7,4},{8,13},{9,14},{10,... | collective-permute-start | bytes 688136 | tf_op jit(solution)/shard_map/ppermute | solution.py:271
  119.1 1.6 collective-permute-start.17
  121.9 0.8 fusion.38.pack_ref
  122.7 11.0 %collective-permute-done.15.refs_11_ = bf16[896,128]{1,0:T(8,128)(2,1)} collective-permute-done((bf16[896,128]{1,0:T(8,128)(2,1)}, bf16[896,128]{1,0:T(8,128)(2,1)}, u32[]{:S(2)}, u32[]{:S(2)}) %collective-permute-start.15) | collective-permute-done | bytes 229408 | tf_op jit(solution)/shard_map/ppermute | solution.py:271
  133.7 7.1 %collective-permute-done.17.refs_12_ = bf16[896,128]{1,0:T(8,128)(2,1)} collective-permute-done((bf16[896,128]{1,0:T(8,128)(2,1)}, bf16[896,128]{1,0:T(8,128)(2,1)}, u32[]{:S(2)}, u32[]{:S(2)}) %collective-permute-start.17) | collective-permute-done | bytes 229408 | tf_op jit(solution)/shard_map/ppermute | solution.py:271
  141.5 2.8 %collective-permute-start.19 = (bf16[48,5248]{1,0:T(8,128)(2,1)S(1)}, bf16[48,5248]{1,0:T(8,128)(2,1)S(1)}, u32[]{:S(2)}, u32[]{:S(2)}) collective-permute-start(bf16[48,5248]{1,0:T(8,128)(2,1)S(1)} %shard_map.119.refs_0_), channel_id=1, source_target_pairs={{0,1},{1,2},{2,3},{3,4},{4,5},{5,6},{6,7},{7,0},{8,9},{9,10},{10,1... | collective-permute-start | bytes 1511432 | tf_op jit(solution)/shard_map/ppermute | solution.py:212
  144.8 3.1 %shard_map.120 = (f32[48,512]{1,0:T(8,128)S(1)}, bf16[48,128]{1,0:T(8,128)(2,1)S(1)}) custom-call(bf16[48,5248]{1,0:T(8,128)(2,1)S(1)} %shard_map.119.refs_0_, bf16[5120,128]{1,0:T(8,128)(2,1)S(1)} %bitcast.88, bf16[5120,128]{1,0:T(8,128)(2,1)} %collective-permute-done.refs_2_.refs_3_, bf16[5120,128]{1,0:T(8,128)(2,1)} %bitcast.30.refs_3_.refs_4_, ...), custom_call_target="tpu_custom_call" | custom-call | flops 251658240 | bytes 5242880 | tf_op jit(solution)/shard_map/pallas_call | solution.py:102
  147.9 6.1 %collective-permute-done.19.refs_0_ = bf16[48,5248]{1,0:T(8,128)(2,1)S(1)} collective-permute-done((bf16[48,5248]{1,0:T(8,128)(2,1)S(1)}, bf16[48,5248]{1,0:T(8,128)(2,1)S(1)}, u32[]{:S(2)}, u32[]{:S(2)}) %collective-permute-start.19) | collective-permute-done | bytes 503840 | tf_op jit(solution)/shard_map/ppermute | solution.py:212
  154.1 2.2 collective-permute-done.20.refs_1_
  156.6 11.4 %collective-permute-start.22 = (bf16[48,5248]{1,0:T(8,128)(2,1)S(1)}, bf16[48,5248]{1,0:T(8,128)(2,1)S(1)}, u32[]{:S(2)}, u32[]{:S(2)}) collective-permute-start(bf16[48,5248]{1,0:T(8,128)(2,1)S(1)} %collective-permute-done.20.refs_1_), channel_id=1, source_target_pairs={{0,7},{1,0},{2,1},{3,2},{4,3},{5,4},{6,5},{7,6},{8,15},{9,8},{10,9... | collective-permute-start | bytes 1511432 | tf_op jit(solution)/shard_map/ppermute | solution.py:212
  168.0 3.1 %shard_map.121 = (f32[96,512]{1,0:T(8,128)S(1)}, bf16[96,128]{1,0:T(8,128)(2,1)S(1)}) custom-call(bf16[48,5248]{1,0:T(8,128)(2,1)S(1)} %collective-permute-done.19.refs_0_, bf16[48,5248]{1,0:T(8,128)(2,1)S(1)} %collective-permute-done.20.refs_1_, bf16[5120,128]{1,0:T(8,128)(2,1)S(1)} %bitcast.89, bf16[5120,128]{1,0:T(8,128)(2,1)} %collective-permute-done.refs_2_.refs_3_, ...), custom_call_target="tpu_custom_call" | custom-call | flops 503316480 | bytes 5242880 | tf_op jit(solution)/shard_map/pallas_call | solution.py:102
  171.2 5.3 %collective-permute-done.22.refs_1_ = bf16[48,5248]{1,0:T(8,128)(2,1)S(1)} collective-permute-done((bf16[48,5248]{1,0:T(8,128)(2,1)S(1)}, bf16[48,5248]{1,0:T(8,128)(2,1)S(1)}, u32[]{:S(2)}, u32[]{:S(2)}) %collective-permute-start.22) | collective-permute-done | bytes 503840 | tf_op jit(solution)/shard_map/ppermute | solution.py:212
  177.1 2.8 %collective-permute-start.24 = (bf16[48,5248]{1,0:T(8,128)(2,1)S(1)}, bf16[48,5248]{1,0:T(8,128)(2,1)}, u32[]{:S(2)}, u32[]{:S(2)}) collective-permute-start(bf16[48,5248]{1,0:T(8,128)(2,1)S(1)} %collective-permute-done.22.refs_1_), channel_id=1, source_target_pairs={{0,7},{1,0},{2,1},{3,2},{4,3},{5,4},{6,5},{7,6},{8,15},{9,8},{10,9... | collective-permute-start | bytes 1511432 | tf_op jit(solution)/shard_map/ppermute | solution.py:212
  180.0 3.1 %shard_map.122 = (f32[96,512]{1,0:T(8,128)S(1)}, bf16[96,128]{1,0:T(8,128)(2,1)S(1)}) custom-call(bf16[48,5248]{1,0:T(8,128)(2,1)S(1)} %collective-permute-done.21.refs_0_, bf16[48,5248]{1,0:T(8,128)(2,1)S(1)} %collective-permute-done.22.refs_1_, bf16[5120,128]{1,0:T(8,128)(2,1)S(1)} %bitcast.90, bf16[5120,128]{1,0:T(8,128)(2,1)} %collective-permute-done.refs_2_.refs_3_, ...), custom_call_target="tpu_custom_call" | custom-call | flops 503316480 | bytes 5242880 | tf_op jit(solution)/shard_map/pallas_call | solution.py:102
  183.8 4.4 %collective-permute-done.23.refs_0_ = bf16[48,5248]{1,0:T(8,128)(2,1)} collective-permute-done((bf16[48,5248]{1,0:T(8,128)(2,1)S(1)}, bf16[48,5248]{1,0:T(8,128)(2,1)}, u32[]{:S(2)}, u32[]{:S(2)}) %collective-permute-start.23) | collective-permute-done | bytes 503840 | tf_op jit(solution)/shard_map/ppermute | solution.py:212
  188.2 1.1 broadcast_select_fusion
  189.3 1.4 collective-permute-start.25
  191.8 3.4 %shard_map.123 = (f32[96,512]{1,0:T(8,128)S(1)}, bf16[96,128]{1,0:T(8,128)(2,1)S(1)}) custom-call(bf16[48,5248]{1,0:T(8,128)(2,1)} %collective-permute-done.23.refs_0_, bf16[48,5248]{1,0:T(8,128)(2,1)} %collective-permute-done.24.refs_1_, bf16[5120,128]{1,0:T(8,128)(2,1)S(1)} %bitcast.91, bf16[5120,128]{1,0:T(8,128)(2,1)} %collective-permute-done.refs_2_.refs_3_, ...), custom_call_target="tpu_custom_call" | custom-call | flops 503316480 | bytes 5242880 | tf_op jit(solution)/shard_map/pallas_call | solution.py:102
  195.1 4.4 %collective-permute-done.25.refs_0_ = bf16[48,5248]{1,0:T(8,128)(2,1)S(1)} collective-permute-done((bf16[48,5248]{1,0:T(8,128)(2,1)S(1)}, bf16[48,5248]{1,0:T(8,128)(2,1)S(1)}, u32[]{:S(2)}, u32[]{:S(2)}) %collective-permute-start.25) | collective-permute-done | bytes 503840 | tf_op jit(solution)/shard_map/ppermute | solution.py:215
  199.6 3.2 %shard_map.124 = (f32[48,512]{1,0:T(8,128)S(1)}, bf16[48,128]{1,0:T(8,128)(2,1)S(1)}) custom-call(bf16[48,5248]{1,0:T(8,128)(2,1)S(1)} %collective-permute-done.25.refs_0_, bf16[5120,128]{1,0:T(8,128)(2,1)S(1)} %bitcast.92, bf16[5120,128]{1,0:T(8,128)(2,1)} %collective-permute-done.refs_2_.refs_3_, bf16[5120,128]{1,0:T(8,128)(2,1)} %bitcast.30.refs_3_.refs_4_, ...), custom_call_target="tpu_custom_call" | custom-call | flops 251658240 | bytes 5242880 | tf_op jit(solution)/shard_map/pallas_call | solution.py:102
  202.8 3.6 %shard_map.125 = bf16[384,384]{1,0:T(8,128)(2,1)S(1)} custom-call(f32[48,512]{1,0:T(8,128)S(1)} %get-tuple-element.94.refs_0_, f32[96,512]{1,0:T(8,128)S(1)} %copy-done.5, f32[96,512]{1,0:T(8,128)S(1)} %copy-done.7, f32[96,512]{1,0:T(8,128)S(1)} %get-tuple-element.110.refs_3_, f32[48,512]{1,0:T(8,128)S(1)} %get-tuple-element.112.refs_4_, ...), custom_call_target="tpu_custom_call" | custom-call | tf_op jit(solution)/shard_map/pallas_call | solution.py:152
  207.5 0.9 collective-permute-done.31.refs_21_
  209.4 2.8 %collective-permute-start.36 = (bf16[384,256]{1,0:T(8,128)(2,1)S(1)}, bf16[384,256]{1,0:T(8,128)(2,1)S(1)}, u32[]{:S(2)}, u32[]{:S(2)}) collective-permute-start(bf16[384,256]{1,0:T(8,128)(2,1)S(1)} %slice.49.refs_0_), channel_id=1, source_target_pairs={{0,7},{1,0},{2,1},{3,2},{4,3},{5,4},{6,5},{7,6},{8,15},{9,8},{10,9... | collective-permute-start | bytes 589832 | tf_op jit(solution)/shard_map/ppermute | solution.py:212
  212.2 4.9 %collective-permute-done.33.refs_1_ = bf16[384,256]{1,0:T(8,128)(2,1)S(1)} collective-permute-done((bf16[384,256]{1,0:T(8,128)(2,1)S(1)}, bf16[384,256]{1,0:T(8,128)(2,1)S(1)}, u32[]{:S(2)}, u32[]{:S(2)}) %collective-permute-start.33) | collective-permute-done | bytes 196640 | tf_op jit(solution)/shard_map/ppermute | solution.py:212
  217.2 3.2 %collective-permute-start.37 = (bf16[384,256]{1,0:T(8,128)(2,1)S(1)}, bf16[384,256]{1,0:T(8,128)(2,1)S(1)}, u32[]{:S(2)}, u32[]{:S(2)}) collective-permute-start(bf16[384,256]{1,0:T(8,128)(2,1)S(1)} %collective-permute-done.36.refs_7_), channel_id=1, source_target_pairs={{0,7},{1,0},{2,1},{3,2},{4,3},{5,4},{6,5},{7,6},{8,15},{9,8},{10,9... | collective-permute-start | bytes 589832 | tf_op jit(solution)/shard_map/ppermute | solution.py:212
  220.4 4.3 %collective-permute-done.34.refs_2_ = bf16[384,256]{1,0:T(8,128)(2,1)S(1)} collective-permute-done((bf16[384,256]{1,0:T(8,128)(2,1)S(1)}, bf16[384,256]{1,0:T(8,128)(2,1)S(1)}, u32[]{:S(2)}, u32[]{:S(2)}) %collective-permute-start.34) | collective-permute-done | bytes 196640 | tf_op jit(solution)/shard_map/ppermute | solution.py:212
  224.7 3.2 %collective-permute-start.38 = (bf16[384,256]{1,0:T(8,128)(2,1)S(1)}, bf16[384,256]{1,0:T(8,128)(2,1)S(1)}, u32[]{:S(2)}, u32[]{:S(2)}) collective-permute-start(bf16[384,256]{1,0:T(8,128)(2,1)S(1)} %collective-permute-done.37.refs_6_), channel_id=1, source_target_pairs={{0,7},{1,0},{2,1},{3,2},{4,3},{5,4},{6,5},{7,6},{8,15},{9,8},{10,9... | collective-permute-start | bytes 589832 | tf_op jit(solution)/shard_map/ppermute | solution.py:212
  227.9 3.6 %collective-permute-done.35.refs_3_ = bf16[384,256]{1,0:T(8,128)(2,1)S(1)} collective-permute-done((bf16[384,256]{1,0:T(8,128)(2,1)S(1)}, bf16[384,256]{1,0:T(8,128)(2,1)S(1)}, u32[]{:S(2)}, u32[]{:S(2)}) %collective-permute-start.35) | collective-permute-done | bytes 196640 | tf_op jit(solution)/shard_map/ppermute | solution.py:212
  231.7 6.9 %collective-permute-done.39.refs_4_ = bf16[384,256]{1,0:T(8,128)(2,1)S(1)} collective-permute-done((bf16[384,256]{1,0:T(8,128)(2,1)S(1)}, bf16[384,256]{1,0:T(8,128)(2,1)S(1)}, u32[]{:S(2)}, u32[]{:S(2)}) %collective-permute-start.39) | collective-permute-done | bytes 196640 | tf_op jit(solution)/shard_map/ppermute | solution.py:215
  238.5 4.4 %shard_map.126 = bf16[384,1024]{1,0:T(8,128)(2,1)} custom-call(bf16[384,256]{1,0:T(8,128)(2,1)S(1)} %slice.49.refs_0_, bf16[384,256]{1,0:T(8,128)(2,1)S(1)} %collective-permute-done.33.refs_1_, bf16[384,256]{1,0:T(8,128)(2,1)S(1)} %collective-permute-done.34.refs_2_, bf16[384,256]{1,0:T(8,128)(2,1)S(1)} %collective-permute-done.35.refs_3_, ...), custom_call_target="tpu_custom_call" | custom-call | tf_op jit(solution)/shard_map/pallas_call | solution.py:190
  242.9 7.2 %all-to-all-start.4 = ((bf16[16,24,1024]{2,1,0:T(8,128)(2,1)}), bf16[16,24,1024]{2,1,0:T(8,128)(2,1)S(1)}, u32[]{:S(2)}, u32[]{:S(2)}) async-start(bf16[16,24,1024]{2,1,0:T(8,128)(2,1)} %bitcast.37), calls=%async_computation.4 | async-start | bytes 1572864 | tf_op jit(solution)/shard_map/all_to_all | solution.py:396
  250.1 10.1 %all-to-all-done.4 = bf16[16,24,1024]{2,1,0:T(8,128)(2,1)S(1)} async-done(((bf16[16,24,1024]{2,1,0:T(8,128)(2,1)}), bf16[16,24,1024]{2,1,0:T(8,128)(2,1)S(1)}, u32[]{:S(2)}, u32[]{:S(2)}) %all-to-all-start.4) | async-done | bytes 786464 | tf_op jit(solution)/shard_map/all_to_all | solution.py:396
  261.5 3.5 %all-to-all-start.5 = ((bf16[8,4,896]{2,1,0:T(4,128)(2,1)}), bf16[8,4,896]{2,1,0:T(4,128)(2,1)S(1)}, u32[]{:S(2)}, u32[]{:S(2)}) async-start(bf16[8,4,896]{2,1,0:T(4,128)(2,1)} %reshape.412), calls=%async_computation.5 | async-start | bytes 114688 | tf_op jit(solution)/shard_map/all_to_all | solution.py:408
  265.2 8.1 %all-to-all-done.5 = bf16[8,4,896]{2,1,0:T(4,128)(2,1)S(1)} async-done(((bf16[8,4,896]{2,1,0:T(4,128)(2,1)}), bf16[8,4,896]{2,1,0:T(4,128)(2,1)S(1)}, u32[]{:S(2)}, u32[]{:S(2)}) %all-to-all-start.5) | async-done | bytes 57376 | tf_op jit(solution)/shard_map/all_to_all | solution.py:408
  (139 shorter events, 23.6 us)
Async XLA Ops:
  0.0 12.7 %copy-start = (bf16[8,512,128]{2,1,0:T(8,128)(2,1)S(1)}, bf16[8,512,128]{2,1,0:T(8,128)(2,1)}, u32[]{:S(2)}) copy-start(bf16[8,512,128]{2,1,0:T(8,128)(2,1)} %param.15) | copy-start | bytes 3145732
  14.4 24.5 %all-to-all-start = ((bf16[16,272,128]{2,1,0:T(8,128)(2,1)}), bf16[16,272,128]{2,1,0:T(8,128)(2,1)S(1)}, u32[]{:S(2)}, u32[]{:S(2)}) async-start(bf16[16,272,128]{2,1,0:T(8,128)(2,1)} %fusion.11), calls=%async_computation | async-start | bytes 2228224 | tf_op jit(solution)/shard_map/all_to_all | solution.py:308
  38.9 3.9 %copy-start.10 = (bf16[16,272,128]{2,1,0:T(8,128)(2,1)}, bf16[16,272,128]{2,1,0:T(8,128)(2,1)S(1)}, u32[]{:S(2)}) copy-start(bf16[16,272,128]{2,1,0:T(8,128)(2,1)S(1)} %all-to-all-done) | copy-start | bytes 3342340
  38.9 2.3 copy-start.11
  40.8 1.8 copy-start.12
  40.8 30.7 %collective-permute-start = (bf16[5120,128]{1,0:T(8,128)(2,1)S(1)}, bf16[5120,128]{1,0:T(8,128)(2,1)}, u32[]{:S(2)}, u32[]{:S(2)}) collective-permute-start(bf16[5120,128]{1,0:T(8,128)(2,1)S(1)} %bitcast.87), channel_id=1, source_target_pairs={{0,128},{128,0},{1,129},{129,1},{2,130},{130,2},{3,131},{131,3},{4... | collective-permute-start | bytes 3932168 | tf_op jit(solution)/shard_map/ppermute | solution.py:256
  42.4 29.1 %collective-permute-start.1 = (bf16[5120,128]{1,0:T(8,128)(2,1)}, bf16[5120,128]{1,0:T(8,128)(2,1)}, u32[]{:S(2)}, u32[]{:S(2)}) collective-permute-start(bf16[5120,128]{1,0:T(8,128)(2,1)} %bitcast.30.refs_3_.refs_4_), channel_id=1, source_target_pairs={{0,128},{128,0},{1,129},{129,1},{2,130},{130,2},{3,131},{131,3},{4... | collective-permute-start | bytes 3932168 | tf_op jit(solution)/shard_map/ppermute | solution.py:256
  44.0 9.5 %copy-start.14 = (f32[7168]{0:T(1024)S(1)}, f32[7168]{0:T(1024)}, u32[]{:S(2)}) copy-start(f32[7168]{0:T(1024)} %param.18) | copy-start | bytes 86020
  45.0 26.5 %all-to-all-start.1 = ((bf16[8,64,448]{2,1,0:T(8,128)(2,1)}), bf16[8,64,448]{2,1,0:T(8,128)(2,1)S(1)}, u32[]{:S(2)}, u32[]{:S(2)}) async-start(bf16[8,64,448]{2,1,0:T(8,128)(2,1)} %copy.63), calls=%async_computation.1 | async-start | bytes 1048576 | tf_op jit(solution)/shard_map/all_to_all | solution.py:324
  53.5 87.3 %collective-permute-start.18 = (bf16[896,128]{1,0:T(8,128)(2,1)}, bf16[896,128]{1,0:T(8,128)(2,1)}, u32[]{:S(2)}, u32[]{:S(2)}) collective-permute-start(bf16[896,128]{1,0:T(8,128)(2,1)} %get-tuple-element.146.refs_8_), channel_id=1, source_target_pairs={{0,128},{128,0},{1,129},{129,1},{2,130},{130,2},{3,131},{131,3},{4... | collective-permute-start | bytes 688136 | tf_op jit(solution)/shard_map/ppermute | solution.py:256
  54.7 21.8 %copy-start.1 = (bf16[16,128,128]{2,1,0:T(8,128)(2,1)}, bf16[16,128,128]{2,1,0:T(8,128)(2,1)S(1)}, u32[]{:S(2)}) copy-start(bf16[16,128,128]{2,1,0:T(8,128)(2,1)S(1)} %slice.57) | copy-start | bytes 1572868
  56.8 5.4 %collective-permute-start.2 = (bf16[2048,128]{1,0:T(8,128)(2,1)S(1)}, bf16[2048,128]{1,0:T(8,128)(2,1)}, u32[]{:S(2)}, u32[]{:S(2)}) collective-permute-start(bf16[2048,128]{1,0:T(8,128)(2,1)S(1)} %bitcast.93), channel_id=1, source_target_pairs={{0,128},{128,0},{1,129},{129,1},{2,130},{130,2},{3,131},{131,3},{4... | collective-permute-start | bytes 1572872 | tf_op jit(solution)/shard_map/ppermute | solution.py:256
  57.3 4.9 %collective-permute-start.3 = (bf16[2048,128]{1,0:T(8,128)(2,1)}, bf16[2048,128]{1,0:T(8,128)(2,1)}, u32[]{:S(2)}, u32[]{:S(2)}) collective-permute-start(bf16[2048,128]{1,0:T(8,128)(2,1)} %bitcast.32.refs_13_), channel_id=1, source_target_pairs={{0,128},{128,0},{1,129},{129,1},{2,130},{130,2},{3,131},{131,3},{4... | collective-permute-start | bytes 1572872 | tf_op jit(solution)/shard_map/ppermute | solution.py:256
  71.7 1.0 copy-start.3
  72.7 8.7 %collective-permute-start.4 = (bf16[64,128]{1,0:T(8,128)(2,1)S(1)}, bf16[64,128]{1,0:T(8,128)(2,1)S(1)}, u32[]{:S(2)}, u32[]{:S(2)}) collective-permute-start(bf16[64,128]{1,0:T(8,128)(2,1)S(1)} %get-tuple-element.77), channel_id=1, source_target_pairs={{0,1},{1,2},{2,3},{3,4},{4,5},{5,6},{6,7},{7,0},{8,9},{9,10},{10,1... | collective-permute-start | bytes 49160 | tf_op jit(solution)/shard_map/ppermute | solution.py:212
  73.2 8.3 %collective-permute-start.7 = (bf16[64,128]{1,0:T(8,128)(2,1)S(1)}, bf16[64,128]{1,0:T(8,128)(2,1)S(1)}, u32[]{:S(2)}, u32[]{:S(2)}) collective-permute-start(bf16[64,128]{1,0:T(8,128)(2,1)S(1)} %get-tuple-element.77), channel_id=1, source_target_pairs={{0,7},{1,0},{2,1},{3,2},{4,3},{5,4},{6,5},{7,6},{8,15},{9,8},{10,9... | collective-permute-start | bytes 49160 | tf_op jit(solution)/shard_map/ppermute | solution.py:212
  76.5 26.5 %all-to-all-start.2 = ((bf16[16,64,448]{2,1,0:T(8,128)(2,1)}), bf16[16,64,448]{2,1,0:T(8,128)(2,1)S(1)}, u32[]{:S(2)}, u32[]{:S(2)}) async-start(bf16[16,64,448]{2,1,0:T(8,128)(2,1)} %copy-done.3), calls=%async_computation.2 | async-start | bytes 2097152 | tf_op jit(solution)/shard_map/all_to_all | solution.py:332
  81.4 5.0 %collective-permute-start.5 = (bf16[64,128]{1,0:T(8,128)(2,1)S(1)}, bf16[64,128]{1,0:T(8,128)(2,1)S(1)}, u32[]{:S(2)}, u32[]{:S(2)}) collective-permute-start(bf16[64,128]{1,0:T(8,128)(2,1)S(1)} %collective-permute-done.4), channel_id=1, source_target_pairs={{0,1},{1,2},{2,3},{3,4},{4,5},{5,6},{6,7},{7,0},{8,9},{9,10},{10,1... | collective-permute-start | bytes 49160 | tf_op jit(solution)/shard_map/ppermute | solution.py:212
  81.5 5.2 %collective-permute-start.8 = (bf16[64,128]{1,0:T(8,128)(2,1)S(1)}, bf16[64,128]{1,0:T(8,128)(2,1)S(1)}, u32[]{:S(2)}, u32[]{:S(2)}) collective-permute-start(bf16[64,128]{1,0:T(8,128)(2,1)S(1)} %collective-permute-done.7), channel_id=1, source_target_pairs={{0,7},{1,0},{2,1},{3,2},{4,3},{5,4},{6,5},{7,6},{8,15},{9,8},{10,9... | collective-permute-start | bytes 49160 | tf_op jit(solution)/shard_map/ppermute | solution.py:212
  86.5 5.2 %collective-permute-start.6 = (bf16[64,128]{1,0:T(8,128)(2,1)S(1)}, bf16[64,128]{1,0:T(8,128)(2,1)S(1)}, u32[]{:S(2)}, u32[]{:S(2)}) collective-permute-start(bf16[64,128]{1,0:T(8,128)(2,1)S(1)} %collective-permute-done.5), channel_id=1, source_target_pairs={{0,1},{1,2},{2,3},{3,4},{4,5},{5,6},{6,7},{7,0},{8,9},{9,10},{10,1... | collective-permute-start | bytes 49160 | tf_op jit(solution)/shard_map/ppermute | solution.py:212
  86.7 4.9 %collective-permute-start.9 = (bf16[64,128]{1,0:T(8,128)(2,1)S(1)}, bf16[64,128]{1,0:T(8,128)(2,1)S(1)}, u32[]{:S(2)}, u32[]{:S(2)}) collective-permute-start(bf16[64,128]{1,0:T(8,128)(2,1)S(1)} %collective-permute-done.8), channel_id=1, source_target_pairs={{0,7},{1,0},{2,1},{3,2},{4,3},{5,4},{6,5},{7,6},{8,15},{9,8},{10,9... | collective-permute-start | bytes 49160 | tf_op jit(solution)/shard_map/ppermute | solution.py:212
  92.3 5.1 %collective-permute-start.10 = (bf16[64,128]{1,0:T(8,128)(2,1)S(1)}, bf16[64,128]{1,0:T(8,128)(2,1)S(1)}, u32[]{:S(2)}, u32[]{:S(2)}) collective-permute-start(bf16[64,128]{1,0:T(8,128)(2,1)S(1)} %get-tuple-element.147), channel_id=1, source_target_pairs={{0,1},{1,2},{2,3},{3,4},{4,5},{5,6},{6,7},{7,0},{128,135},{129,128... | collective-permute-start | bytes 49160 | tf_op jit(solution)/shard_map/ppermute | solution.py:215
  93.0 20.9 %collective-permute-start.11 = (bf16[896,128]{1,0:T(8,128)(2,1)}, bf16[896,128]{1,0:T(8,128)(2,1)}, u32[]{:S(2)}, u32[]{:S(2)}) collective-permute-start(bf16[896,128]{1,0:T(8,128)(2,1)} %get-tuple-element.79), channel_id=1, source_target_pairs={{0,1},{1,2},{2,3},{3,4},{4,5},{5,6},{6,7},{7,0},{8,9},{9,10},{10,1... | collective-permute-start | bytes 688136 | tf_op jit(solution)/shard_map/ppermute | solution.py:271
  93.1 21.1 %collective-permute-start.12 = (bf16[896,128]{1,0:T(8,128)(2,1)}, bf16[896,128]{1,0:T(8,128)(2,1)}, u32[]{:S(2)}, u32[]{:S(2)}) collective-permute-start(bf16[896,128]{1,0:T(8,128)(2,1)} %get-tuple-element.80), channel_id=1, source_target_pairs={{0,7},{1,0},{2,1},{3,2},{4,3},{5,4},{6,5},{7,6},{8,15},{9,8},{10,9... | collective-permute-start | bytes 688136 | tf_op jit(solution)/shard_map/ppermute | solution.py:271
  96.4 22.7 %collective-permute-start.13 = (bf16[896,128]{1,0:T(8,128)(2,1)}, bf16[896,128]{1,0:T(8,128)(2,1)}, u32[]{:S(2)}, u32[]{:S(2)}) collective-permute-start(bf16[896,128]{1,0:T(8,128)(2,1)} %get-tuple-element.81), channel_id=1, source_target_pairs={{0,2},{1,3},{2,4},{3,5},{4,6},{5,7},{6,0},{7,1},{8,10},{9,11},{10,... | collective-permute-start | bytes 688136 | tf_op jit(solution)/shard_map/ppermute | solution.py:271
  97.4 25.3 %collective-permute-start.14 = (bf16[896,128]{1,0:T(8,128)(2,1)}, bf16[896,128]{1,0:T(8,128)(2,1)}, u32[]{:S(2)}, u32[]{:S(2)}) collective-permute-start(bf16[896,128]{1,0:T(8,128)(2,1)} %get-tuple-element.82), channel_id=1, source_target_pairs={{0,6},{1,7},{2,0},{3,1},{4,2},{5,3},{6,4},{7,5},{8,14},{9,15},{10,... | collective-permute-start | bytes 688136 | tf_op jit(solution)/shard_map/ppermute | solution.py:271
  105.6 15.1 %copy-start.15 = (s32[64]{0:T(128)S(1)}, s32[64]{0:T(128)}, u32[]{:S(2)}) copy-start(s32[64]{0:T(128)} %get-tuple-element.153) | copy-start | bytes 772
  105.6 15.1 %copy-start.16 = (s32[64]{0:T(128)S(1)}, s32[64]{0:T(128)}, u32[]{:S(2)}) copy-start(s32[64]{0:T(128)} %get-tuple-element.154) | copy-start | bytes 772
  105.6 16.1 %copy-start.13 = (bf16[64,1]{1,0:T(8,128)(2,1)S(1)}, bf16[64,1]{1,0:T(8,128)(2,1)}, u32[]{:S(2)}) copy-start(bf16[64,1]{1,0:T(8,128)(2,1)} %get-tuple-element.160) | copy-start | bytes 388
  105.6 82.5 %all-to-all-start.3 = ((bf16[16,512,128]{2,1,0:T(8,128)(2,1)}), bf16[16,512,128]{2,1,0:T(8,128)(2,1)}, u32[]{:S(2)}, u32[]{:S(2)}) async-start(bf16[16,512,128]{2,1,0:T(8,128)(2,1)} %broadcast_in_dim.60), calls=%async_computation.3 | async-start | bytes 4194304 | tf_op jit(solution)/shard_map/all_to_all | solution.py:366
  114.0 19.7 %collective-permute-start.15 = (bf16[896,128]{1,0:T(8,128)(2,1)}, bf16[896,128]{1,0:T(8,128)(2,1)}, u32[]{:S(2)}, u32[]{:S(2)}) collective-permute-start(bf16[896,128]{1,0:T(8,128)(2,1)} %get-tuple-element.83), channel_id=1, source_target_pairs={{0,3},{1,4},{2,5},{3,6},{4,7},{5,0},{6,1},{7,2},{8,11},{9,12},{10,... | collective-permute-start | bytes 688136 | tf_op jit(solution)/shard_map/ppermute | solution.py:271
  114.2 19.5 %collective-permute-start.16 = (bf16[896,128]{1,0:T(8,128)(2,1)}, bf16[896,128]{1,0:T(8,128)(2,1)}, u32[]{:S(2)}, u32[]{:S(2)}) collective-permute-start(bf16[896,128]{1,0:T(8,128)(2,1)} %get-tuple-element.84), channel_id=1, source_target_pairs={{0,5},{1,6},{2,7},{3,0},{4,1},{5,2},{6,3},{7,4},{8,13},{9,14},{10,... | collective-permute-start | bytes 688136 | tf_op jit(solution)/shard_map/ppermute | solution.py:271
  119.1 21.7 %collective-permute-start.17 = (bf16[896,128]{1,0:T(8,128)(2,1)}, bf16[896,128]{1,0:T(8,128)(2,1)}, u32[]{:S(2)}, u32[]{:S(2)}) collective-permute-start(bf16[896,128]{1,0:T(8,128)(2,1)} %get-tuple-element.85), channel_id=1, source_target_pairs={{0,4},{1,5},{2,6},{3,7},{4,0},{5,1},{6,2},{7,3},{8,12},{9,13},{10,... | collective-permute-start | bytes 688136 | tf_op jit(solution)/shard_map/ppermute | solution.py:271
  141.5 12.6 %collective-permute-start.19 = (bf16[48,5248]{1,0:T(8,128)(2,1)S(1)}, bf16[48,5248]{1,0:T(8,128)(2,1)S(1)}, u32[]{:S(2)}, u32[]{:S(2)}) collective-permute-start(bf16[48,5248]{1,0:T(8,128)(2,1)S(1)} %shard_map.119.refs_0_), channel_id=1, source_target_pairs={{0,1},{1,2},{2,3},{3,4},{4,5},{5,6},{6,7},{7,0},{8,9},{9,10},{10,1... | collective-permute-start | bytes 1511432 | tf_op jit(solution)/shard_map/ppermute | solution.py:212
  144.3 11.9 %collective-permute-start.20 = (bf16[48,5248]{1,0:T(8,128)(2,1)S(1)}, bf16[48,5248]{1,0:T(8,128)(2,1)S(1)}, u32[]{:S(2)}, u32[]{:S(2)}) collective-permute-start(bf16[48,5248]{1,0:T(8,128)(2,1)S(1)} %shard_map.119.refs_0_), channel_id=1, source_target_pairs={{0,7},{1,0},{2,1},{3,2},{4,3},{5,4},{6,5},{7,6},{8,15},{9,8},{10,9... | collective-permute-start | bytes 1511432 | tf_op jit(solution)/shard_map/ppermute | solution.py:212
  147.9 23.2 %copy-start.8 = (bf16[48,128]{1,0:T(8,128)(2,1)}, bf16[48,128]{1,0:T(8,128)(2,1)S(1)}, u32[]{:S(2)}) copy-start(bf16[48,128]{1,0:T(8,128)(2,1)S(1)} %get-tuple-element.113.refs_5_) | copy-start | bytes 36868
  156.3 14.9 %collective-permute-start.21 = (bf16[48,5248]{1,0:T(8,128)(2,1)S(1)}, bf16[48,5248]{1,0:T(8,128)(2,1)S(1)}, u32[]{:S(2)}, u32[]{:S(2)}) collective-permute-start(bf16[48,5248]{1,0:T(8,128)(2,1)S(1)} %collective-permute-done.19.refs_0_), channel_id=1, source_target_pairs={{0,1},{1,2},{2,3},{3,4},{4,5},{5,6},{6,7},{7,0},{8,9},{9,10},{10,1... | collective-permute-start | bytes 1511432 | tf_op jit(solution)/shard_map/ppermute | solution.py:212
  156.6 19.8 %collective-permute-start.22 = (bf16[48,5248]{1,0:T(8,128)(2,1)S(1)}, bf16[48,5248]{1,0:T(8,128)(2,1)S(1)}, u32[]{:S(2)}, u32[]{:S(2)}) collective-permute-start(bf16[48,5248]{1,0:T(8,128)(2,1)S(1)} %collective-permute-done.20.refs_1_), channel_id=1, source_target_pairs={{0,7},{1,0},{2,1},{3,2},{4,3},{5,4},{6,5},{7,6},{8,15},{9,8},{10,9... | collective-permute-start | bytes 1511432 | tf_op jit(solution)/shard_map/ppermute | solution.py:212
  171.2 11.9 %copy-start.4 = (f32[96,512]{1,0:T(8,128)}, f32[96,512]{1,0:T(8,128)S(1)}, u32[]{:S(2)}) copy-start(f32[96,512]{1,0:T(8,128)S(1)} %get-tuple-element.99.refs_1_) | copy-start | bytes 589828
  176.5 11.7 %collective-permute-start.23 = (bf16[48,5248]{1,0:T(8,128)(2,1)S(1)}, bf16[48,5248]{1,0:T(8,128)(2,1)}, u32[]{:S(2)}, u32[]{:S(2)}) collective-permute-start(bf16[48,5248]{1,0:T(8,128)(2,1)S(1)} %collective-permute-done.21.refs_0_), channel_id=1, source_target_pairs={{0,1},{1,2},{2,3},{3,4},{4,5},{5,6},{6,7},{7,0},{8,9},{9,10},{10,1... | collective-permute-start | bytes 1511432 | tf_op jit(solution)/shard_map/ppermute | solution.py:212
  177.1 11.0 %collective-permute-start.24 = (bf16[48,5248]{1,0:T(8,128)(2,1)S(1)}, bf16[48,5248]{1,0:T(8,128)(2,1)}, u32[]{:S(2)}, u32[]{:S(2)}) collective-permute-start(bf16[48,5248]{1,0:T(8,128)(2,1)S(1)} %collective-permute-done.22.refs_1_), channel_id=1, source_target_pairs={{0,7},{1,0},{2,1},{3,2},{4,3},{5,4},{6,5},{7,6},{8,15},{9,8},{10,9... | collective-permute-start | bytes 1511432 | tf_op jit(solution)/shard_map/ppermute | solution.py:212
  183.1 0.7 copy-start.6
  189.3 10.2 %collective-permute-start.25 = (bf16[48,5248]{1,0:T(8,128)(2,1)S(1)}, bf16[48,5248]{1,0:T(8,128)(2,1)S(1)}, u32[]{:S(2)}, u32[]{:S(2)}) collective-permute-start(bf16[48,5248]{1,0:T(8,128)(2,1)S(1)} %broadcast_select_fusion), channel_id=1, source_target_pairs={{0,1},{1,2},{2,3},{3,4},{4,5},{5,6},{6,7},{7,0},{128,135},{129,128... | collective-permute-start | bytes 1511432 | tf_op jit(solution)/shard_map/ppermute | solution.py:215
  190.6 15.8 %collective-permute-start.26 = (bf16[896,128]{1,0:T(8,128)(2,1)}, bf16[896,128]{1,0:T(8,128)(2,1)S(1)}, u32[]{:S(2)}, u32[]{:S(2)}) collective-permute-start(bf16[896,128]{1,0:T(8,128)(2,1)} %collective-permute-done.11.refs_9_), channel_id=1, source_target_pairs={{0,128},{128,0},{1,129},{129,1},{2,130},{130,2},{3,131},{131,3},{4... | collective-permute-start | bytes 688136 | tf_op jit(solution)/shard_map/ppermute | solution.py:256
  190.6 16.4 %collective-permute-start.27 = (bf16[896,128]{1,0:T(8,128)(2,1)}, bf16[896,128]{1,0:T(8,128)(2,1)S(1)}, u32[]{:S(2)}, u32[]{:S(2)}) collective-permute-start(bf16[896,128]{1,0:T(8,128)(2,1)} %collective-permute-done.12.refs_15_), channel_id=1, source_target_pairs={{0,128},{128,0},{1,129},{129,1},{2,130},{130,2},{3,131},{131,3},{4... | collective-permute-start | bytes 688136 | tf_op jit(solution)/shard_map/ppermute | solution.py:256
  191.2 16.3 %collective-permute-start.28 = (bf16[896,128]{1,0:T(8,128)(2,1)}, bf16[896,128]{1,0:T(8,128)(2,1)S(1)}, u32[]{:S(2)}, u32[]{:S(2)}) collective-permute-start(bf16[896,128]{1,0:T(8,128)(2,1)} %collective-permute-done.13.refs_10_), channel_id=1, source_target_pairs={{0,128},{128,0},{1,129},{129,1},{2,130},{130,2},{3,131},{131,3},{4... | collective-permute-start | bytes 688136 | tf_op jit(solution)/shard_map/ppermute | solution.py:256
  191.3 16.2 %collective-permute-start.29 = (bf16[896,128]{1,0:T(8,128)(2,1)}, bf16[896,128]{1,0:T(8,128)(2,1)S(1)}, u32[]{:S(2)}, u32[]{:S(2)}) collective-permute-start(bf16[896,128]{1,0:T(8,128)(2,1)} %collective-permute-done.14.refs_14_), channel_id=1, source_target_pairs={{0,128},{128,0},{1,129},{129,1},{2,130},{130,2},{3,131},{131,3},{4... | collective-permute-start | bytes 688136 | tf_op jit(solution)/shard_map/ppermute | solution.py:256
  199.5 7.9 %collective-permute-start.30 = (bf16[896,128]{1,0:T(8,128)(2,1)}, bf16[896,128]{1,0:T(8,128)(2,1)S(1)}, u32[]{:S(2)}, u32[]{:S(2)}) collective-permute-start(bf16[896,128]{1,0:T(8,128)(2,1)} %collective-permute-done.15.refs_11_), channel_id=1, source_target_pairs={{0,128},{128,0},{1,129},{129,1},{2,130},{130,2},{3,131},{131,3},{4... | collective-permute-start | bytes 688136 | tf_op jit(solution)/shard_map/ppermute | solution.py:256
  199.5 3.2 %copy-start.2 = (bf16[16,128,128]{2,1,0:T(8,128)(2,1)S(1)}, bf16[16,128,128]{2,1,0:T(8,128)(2,1)}, u32[]{:S(2)}) copy-start(bf16[16,128,128]{2,1,0:T(8,128)(2,1)} %copy-done.1) | copy-start | bytes 1572868
  199.5 3.2 %copy-start.5 = (f32[96,512]{1,0:T(8,128)S(1)}, f32[96,512]{1,0:T(8,128)}, u32[]{:S(2)}) copy-start(f32[96,512]{1,0:T(8,128)} %copy-done.4) | copy-start | bytes 589828
  199.5 3.2 %copy-start.7 = (f32[96,512]{1,0:T(8,128)S(1)}, f32[96,512]{1,0:T(8,128)}, u32[]{:S(2)}) copy-start(f32[96,512]{1,0:T(8,128)} %copy-done.6) | copy-start | bytes 589828
  199.5 3.3 %copy-start.9 = (bf16[48,128]{1,0:T(8,128)(2,1)S(1)}, bf16[48,128]{1,0:T(8,128)(2,1)}, u32[]{:S(2)}) copy-start(bf16[48,128]{1,0:T(8,128)(2,1)} %copy-done.8) | copy-start | bytes 36868
  206.4 1.9 collective-permute-start.31
  207.0 1.7 collective-permute-start.32
  208.7 8.4 %collective-permute-start.33 = (bf16[384,256]{1,0:T(8,128)(2,1)S(1)}, bf16[384,256]{1,0:T(8,128)(2,1)S(1)}, u32[]{:S(2)}, u32[]{:S(2)}) collective-permute-start(bf16[384,256]{1,0:T(8,128)(2,1)S(1)} %slice.49.refs_0_), channel_id=1, source_target_pairs={{0,1},{1,2},{2,3},{3,4},{4,5},{5,6},{6,7},{7,0},{8,9},{9,10},{10,1... | collective-permute-start | bytes 589832 | tf_op jit(solution)/shard_map/ppermute | solution.py:212
  209.4 7.8 %collective-permute-start.36 = (bf16[384,256]{1,0:T(8,128)(2,1)S(1)}, bf16[384,256]{1,0:T(8,128)(2,1)S(1)}, u32[]{:S(2)}, u32[]{:S(2)}) collective-permute-start(bf16[384,256]{1,0:T(8,128)(2,1)S(1)} %slice.49.refs_0_), channel_id=1, source_target_pairs={{0,7},{1,0},{2,1},{3,2},{4,3},{5,4},{6,5},{7,6},{8,15},{9,8},{10,9... | collective-permute-start | bytes 589832 | tf_op jit(solution)/shard_map/ppermute | solution.py:212
  217.1 7.5 %collective-permute-start.34 = (bf16[384,256]{1,0:T(8,128)(2,1)S(1)}, bf16[384,256]{1,0:T(8,128)(2,1)S(1)}, u32[]{:S(2)}, u32[]{:S(2)}) collective-permute-start(bf16[384,256]{1,0:T(8,128)(2,1)S(1)} %collective-permute-done.33.refs_1_), channel_id=1, source_target_pairs={{0,1},{1,2},{2,3},{3,4},{4,5},{5,6},{6,7},{7,0},{8,9},{9,10},{10,1... | collective-permute-start | bytes 589832 | tf_op jit(solution)/shard_map/ppermute | solution.py:212
  217.2 7.5 %collective-permute-start.37 = (bf16[384,256]{1,0:T(8,128)(2,1)S(1)}, bf16[384,256]{1,0:T(8,128)(2,1)S(1)}, u32[]{:S(2)}, u32[]{:S(2)}) collective-permute-start(bf16[384,256]{1,0:T(8,128)(2,1)S(1)} %collective-permute-done.36.refs_7_), channel_id=1, source_target_pairs={{0,7},{1,0},{2,1},{3,2},{4,3},{5,4},{6,5},{7,6},{8,15},{9,8},{10,9... | collective-permute-start | bytes 589832 | tf_op jit(solution)/shard_map/ppermute | solution.py:212
  224.7 6.9 %collective-permute-start.35 = (bf16[384,256]{1,0:T(8,128)(2,1)S(1)}, bf16[384,256]{1,0:T(8,128)(2,1)S(1)}, u32[]{:S(2)}, u32[]{:S(2)}) collective-permute-start(bf16[384,256]{1,0:T(8,128)(2,1)S(1)} %collective-permute-done.34.refs_2_), channel_id=1, source_target_pairs={{0,1},{1,2},{2,3},{3,4},{4,5},{5,6},{6,7},{7,0},{8,9},{9,10},{10,1... | collective-permute-start | bytes 589832 | tf_op jit(solution)/shard_map/ppermute | solution.py:212
  224.7 6.9 %collective-permute-start.38 = (bf16[384,256]{1,0:T(8,128)(2,1)S(1)}, bf16[384,256]{1,0:T(8,128)(2,1)S(1)}, u32[]{:S(2)}, u32[]{:S(2)}) collective-permute-start(bf16[384,256]{1,0:T(8,128)(2,1)S(1)} %collective-permute-done.37.refs_6_), channel_id=1, source_target_pairs={{0,7},{1,0},{2,1},{3,2},{4,3},{5,4},{6,5},{7,6},{8,15},{9,8},{10,9... | collective-permute-start | bytes 589832 | tf_op jit(solution)/shard_map/ppermute | solution.py:212
  231.6 7.0 %collective-permute-start.39 = (bf16[384,256]{1,0:T(8,128)(2,1)S(1)}, bf16[384,256]{1,0:T(8,128)(2,1)S(1)}, u32[]{:S(2)}, u32[]{:S(2)}) collective-permute-start(bf16[384,256]{1,0:T(8,128)(2,1)S(1)} %broadcast_select_fusion.1), channel_id=1, source_target_pairs={{0,1},{1,2},{2,3},{3,4},{4,5},{5,6},{6,7},{7,0},{128,135},{129,128... | collective-permute-start | bytes 589832 | tf_op jit(solution)/shard_map/ppermute | solution.py:215
  242.9 17.4 %all-to-all-start.4 = ((bf16[16,24,1024]{2,1,0:T(8,128)(2,1)}), bf16[16,24,1024]{2,1,0:T(8,128)(2,1)S(1)}, u32[]{:S(2)}, u32[]{:S(2)}) async-start(bf16[16,24,1024]{2,1,0:T(8,128)(2,1)} %bitcast.37), calls=%async_computation.4 | async-start | bytes 1572864 | tf_op jit(solution)/shard_map/all_to_all | solution.py:396
  261.5 11.8 %all-to-all-start.5 = ((bf16[8,4,896]{2,1,0:T(4,128)(2,1)}), bf16[8,4,896]{2,1,0:T(4,128)(2,1)S(1)}, u32[]{:S(2)}, u32[]{:S(2)}) async-start(bf16[8,4,896]{2,1,0:T(4,128)(2,1)} %reshape.412), calls=%async_computation.5 | async-start | bytes 114688 | tf_op jit(solution)/shard_map/all_to_all | solution.py:408
